TPU v7x, 128 devices: a whole 4x4x4 slice. The times are simulated.
128 devices in a mesh: row: 8 (over z, y_hi), col: 16 (over y_lo, x, core).
Axes of the slice: x: 4, y: 4 (y_hi: 2, y_lo: 2; y = y_hi * 2 + y_lo), z: 4, core: 2. Of those that a mesh axis runs over, the one named last changes fastest.
Arguments:
- raster: bfloat16 [1024, 1024, 128], P('row', 'col'), may hold values from -6 to 6
- conv_first: bfloat16 [3, 3, 128, 128], replicated, may hold values from -0.1875 to 0.1875
- conv_second: bfloat16 [3, 3, 128, 128], replicated, may hold values from -0.1875 to 0.1875
- crop_anchor: int32 [2, 4096], P(None, ('row', 'col')), may hold values from 0 to 1008, as said below
- agent_live: int32 [4096], P(('row', 'col')), may hold values from 0 to 1, as said below
- w_embed: bfloat16 [2048, 512], replicated, may hold values from -0.125 to 0.125
- gain_attn: float32 [512], replicated, may hold values from 0.25 to 1.75
- w_qkv: bfloat16 [512, 1536], replicated, may hold values from -0.25 to 0.25
- w_out: bfloat16 [512, 512], replicated, may hold values from -0.25 to 0.25
- gain_mlp: float32 [512], replicated, may hold values from 0.25 to 1.75
- w_up: bfloat16 [512, 2048], replicated, may hold values from -0.25 to 0.25
- w_down: bfloat16 [2048, 512], replicated, may hold values from -0.125 to 0.125
Outputs:
- features: bfloat16 [1024, 1024, 128], P('row', 'col')
- agent_out: bfloat16 [4096, 512], P(('row', 'col'))
Inputs may be any that keep to these rules, and one draw needn't show every extreme that they name: `crop_anchor`: the block of device (r, o) along row+col holds at column d * 2 + k the top-left cell of the crop for slot o * 2 + k of shard (r, d). That cell lies in grid rows r * 128 to r * 128 + 127 and grid columns o * 64 to o * 64 + 63, and the whole crop lies inside the grid. `agent_live`: every shard (an aligned block of 32 slots) has at least one live slot, and some shard has all 32 live.
All inputs are finite; a program needn't handle non-finite values.
Results may differ from a plain program's by a relative error of at most 0.0095.
Values may be sent and summed in bfloat16 or wider, within the bound.
No kernel may reach another device: no remote copies, remote signals or barrier semaphores. Data moves between devices by JAX's collectives and lax.ppermute only.
A program may use at most 128 MiB of HBM per device.

v0:
```python
import math

import jax
import jax.numpy as jnp
from jax import lax
from jax.sharding import PartitionSpec as P

HEADS = 8
CROP = 16
POOL = 4


EPS = 1e-06
SCORE_SCALE = 3.0


def extended(x, sides, width):
    for axis, dim in sides:
        devices, length = (lax.axis_size(axis), x.shape[dim])
        up = [(i, (i + 1) % devices) for i in range(devices - 1)]
        down = [(j, i) for i, j in up]
        last = lax.slice_in_dim(x, length - width, length, axis=dim)
        initial = lax.slice_in_dim(x, 0, width, axis=dim)
        before = lax.ppermute(last, axis, up)
        after = lax.ppermute(initial, axis, down)
        x = jnp.concatenate([before, x, after], axis=dim)
    return x


def from_behind(x, axis, by):
    devices = lax.axis_size(axis)
    pairs = [(i, i + by) for i in range(devices) if 0 <= i + by < devices]
    return lax.ppermute(x, axis, pairs)


def sent_together(arrays, axis, dim, along):
    columns = [a.reshape(*a.shape[:along], -1) for a in arrays]
    both = jnp.concatenate(columns, axis=along)
    out, at, done = (lax.all_gather(both, axis, axis=dim, tiled=True), 0, [])
    for a, column in zip(arrays, columns):
        section = out[..., at : at + column.shape[along]]
        done.append(section.reshape(*section.shape[:along], *a.shape[along:]))
        at += column.shape[along]
    return tuple(done)


def conv_valid(padded, kernel):
    return lax.conv_general_dilated(
        padded[None],
        kernel,
        (1, 1),
        "VALID",
        dimension_numbers=("NHWC", "HWIO", "NHWC"),
        preferred_element_type=jnp.float32,
    )[0]


def pool_crops(crop_block):
    leading = crop_block.shape[:-3]
    side_len = CROP // POOL
    channels = crop_block.shape[-1]
    shaped = crop_block.reshape(leading + (side_len, POOL, side_len, POOL, channels)).astype(
        jnp.float32
    )
    pool_means = jnp.mean(shaped, axis=(-4, -2))
    return pool_means.reshape(leading + (side_len * side_len * channels,)).astype(jnp.bfloat16)


def rms_scaled(values, gain_vec):
    return values * lax.rsqrt(jnp.mean(values * values, axis=-1, keepdims=True) + EPS) * gain_vec


def unit_heads(values):
    shaped = values.reshape(values.shape[0], HEADS, -1)
    return (shaped * lax.rsqrt(jnp.mean(shaped * shaped, axis=-1, keepdims=True) + EPS)).astype(
        jnp.bfloat16
    )


def keys_values(normed, w_qkv):
    model_width = normed.shape[1]
    projected = jnp.dot(normed, w_qkv[:, model_width:], preferred_element_type=jnp.float32)
    return (unit_heads(projected[:, :model_width]), projected[:, model_width:].astype(jnp.bfloat16))


def add_keys(unit_q, key_piece, value_piece, mask_piece):
    key_count = key_piece.shape[0]
    value_rows = value_piece.reshape(key_count, HEADS, -1)
    factor = SCORE_SCALE / math.sqrt(key_piece.shape[-1])
    scores = (
        jnp.einsum("qhd,khd->hqk", unit_q, key_piece, preferred_element_type=jnp.float32) * factor
    )
    weights = (jnp.exp(scores) * mask_piece.astype(jnp.float32)[None, None, :]).astype(jnp.bfloat16)
    numerator = jnp.einsum("hqk,khd->qhd", weights, value_rows, preferred_element_type=jnp.float32)
    denominator = jnp.sum(weights.astype(jnp.float32), axis=-1).T
    return (numerator, denominator)


def select_matrix(starts, extent, base):
    offsets = lax.broadcasted_iota(jnp.int32, (starts.shape[0], CROP, extent), 1)
    places = lax.broadcasted_iota(jnp.int32, (starts.shape[0], CROP, extent), 2) + base
    return (places == starts[:, None, None] + offsets).astype(jnp.bfloat16)


def per_device(
    raster,
    conv_first,
    conv_second,
    crop_anchor,
    agent_live,
    w_embed,
    gain_attn,
    w_qkv,
    w_out,
    gain_mlp,
    w_up,
    w_down,
):
    cell_r, cell_c, channels = raster.shape
    row_id = lax.axis_index("row")
    col_id = lax.axis_index("col")
    padded = extended(raster, (("row", 0), ("col", 1)), 2)
    grown_layer = jax.nn.relu(conv_valid(padded, conv_first))
    grid_rows = row_id * cell_r - 1 + lax.broadcasted_iota(jnp.int32, (cell_r + 2, cell_c + 2), 0)
    grid_cols = col_id * cell_c - 1 + lax.broadcasted_iota(jnp.int32, (cell_r + 2, cell_c + 2), 1)
    inside = (
        (grid_rows >= 0)
        & (grid_rows < cell_r * lax.axis_size("row"))
        & (grid_cols >= 0)
        & (grid_cols < cell_c * lax.axis_size("col"))
    )
    padded_first = jnp.where(inside[:, :, None], grown_layer, 0.0).astype(jnp.bfloat16)
    features = (raster.astype(jnp.float32) + conv_valid(padded_first, conv_second)).astype(
        jnp.bfloat16
    )
    rim_width = CROP - 1
    right_part = from_behind(features[:, :rim_width], "col", -1)
    lower_source = jnp.concatenate([features[:rim_width], right_part[:rim_width]], axis=1)
    lower_part = from_behind(lower_source, "row", -1)
    local_rows = crop_anchor[0] - row_id * cell_r
    local_cols = crop_anchor[1] - col_id * cell_c
    rows_main = select_matrix(local_rows, cell_r, 0)
    rows_low = select_matrix(local_rows, rim_width, cell_r)
    cols_main = select_matrix(local_cols, cell_c, 0)
    cols_right = select_matrix(local_cols, rim_width, cell_c)
    left_band = (
        jnp.einsum("ari,ijc->arjc", rows_main, features, preferred_element_type=jnp.float32)
        + jnp.einsum(
            "ari,ijc->arjc", rows_low, lower_part[:, :cell_c], preferred_element_type=jnp.float32
        )
    ).astype(jnp.bfloat16)
    right_band = (
        jnp.einsum("ari,ijc->arjc", rows_main, right_part, preferred_element_type=jnp.float32)
        + jnp.einsum(
            "ari,ijc->arjc", rows_low, lower_part[:, cell_c:], preferred_element_type=jnp.float32
        )
    ).astype(jnp.bfloat16)
    cut_crops = (
        jnp.einsum("abj,arjc->arbc", cols_main, left_band, preferred_element_type=jnp.float32)
        + jnp.einsum("abj,arjc->arbc", cols_right, right_band, preferred_element_type=jnp.float32)
    ).astype(jnp.bfloat16)
    col_count = lax.axis_size("col")
    slot_count = crop_anchor.shape[1]
    per_peer = slot_count // col_count
    pooled = lax.all_to_all(
        pool_crops(cut_crops).reshape(col_count, per_peer, -1),
        "col",
        split_axis=0,
        concat_axis=0,
        tiled=True,
    )
    pooled = pooled.reshape(slot_count, -1)
    embedded = jnp.dot(pooled, w_embed, preferred_element_type=jnp.float32)
    normed_attn = rms_scaled(embedded, gain_attn).astype(jnp.bfloat16)
    model_width = embedded.shape[1]
    unit_q = unit_heads(
        jnp.dot(normed_attn, w_qkv[:, :model_width], preferred_element_type=jnp.float32)
    )
    live_mask = agent_live.astype(jnp.bfloat16)
    pieces = sent_together((normed_attn, live_mask), ("row", "col"), 0, 1)
    key_piece, value_piece = keys_values(pieces[0], w_qkv)
    numerator, denominator = add_keys(unit_q, key_piece, value_piece, pieces[1])
    attended = (
        (numerator / denominator[:, :, None]).reshape(slot_count, model_width).astype(jnp.bfloat16)
    )
    after_attn = embedded + jnp.dot(attended, w_out, preferred_element_type=jnp.float32)
    normed_mlp = rms_scaled(after_attn, gain_mlp).astype(jnp.bfloat16)
    activated = jax.nn.gelu(jnp.dot(normed_mlp, w_up, preferred_element_type=jnp.float32)).astype(
        jnp.bfloat16
    )
    agent_out = (
        (after_attn + jnp.dot(activated, w_down, preferred_element_type=jnp.float32))
        * agent_live.astype(jnp.float32)[:, None]
    ).astype(jnp.bfloat16)
    return (features, agent_out)


def solution(mesh):
    in_specs = (
        P("row", "col", None),
        P(),
        P(),
        P(None, ("row", "col")),
        P(("row", "col")),
        P(),
        P(),
        P(),
        P(),
        P(),
        P(),
        P(),
    )
    out_specs = (P("row", "col", None), P(("row", "col"), None))
    return jax.shard_map(
        per_device, mesh=mesh, in_specs=in_specs, out_specs=out_specs, check_vma=False
    )
```

profile of v0, /device:TPU:1, one launch (start us, length us, event | category | flops | bytes accessed | tf_op | source)
XLA Modules:
  0.0 213.1 jit_solution(2081168845532161668)
XLA Ops:
  7.2 0.9 fusion.99
  8.1 5.6 %collective-permute-start = (bf16[2,64,128]{2,1,0:T(8,128)(2,1)S(1)}, bf16[2,64,128]{2,1,0:T(8,128)(2,1)S(1)}, u32[]{:S(2)}, u32[]{:S(2)}) collective-permute-start(bf16[2,64,128]{2,1,0:T(8,128)(2,1)S(1)} %get-tuple-element.9), channel_id=1, source_target_pairs={{0,16},{16,32},{32,48},{48,64},{64,80},{80,96},{96,112},{1,17},{17... | collective-permute-start | bytes 98312 | tf_op jit(solution)/shard_map/ppermute | solution.py:24
  13.8 1.3 collective-permute-start.1
  15.1 1.9 constant_dynamic-update-slice_fusion.1
  17.0 2.9 %collective-permute-done.1 = bf16[2,64,128]{2,1,0:T(8,128)(2,1)S(1)} collective-permute-done((bf16[2,64,128]{2,1,0:T(8,128)(2,1)S(1)}, bf16[2,64,128]{2,1,0:T(8,128)(2,1)S(1)}, u32[]{:S(2)}, u32[]{:S(2)}) %collective-permute-start.1) | collective-permute-done | bytes 32800 | tf_op jit(solution)/shard_map/ppermute | solution.py:25
  19.9 0.1 fusion.98
  20.0 4.0 %collective-permute-start.3 = (bf16[132,2,128]{2,1,0:T(2,128)(2,1)S(1)}, bf16[132,2,128]{2,1,0:T(2,128)(2,1)S(1)}, u32[]{:S(2)}, u32[]{:S(2)}) collective-permute-start(bf16[132,2,128]{2,1,0:T(2,128)(2,1)S(1)} %get-tuple-element.7), channel_id=1, source_target_pairs={{1,0},{2,1},{3,2},{4,3},{5,4},{6,5},{7,6},{8,7},{9,8},{10,9},{11,1... | collective-permute-start | bytes 202760 | tf_op jit(solution)/shard_map/ppermute | solution.py:25
  24.1 3.0 %collective-permute-start.2 = (bf16[132,2,128]{2,1,0:T(2,128)(2,1)S(1)}, bf16[132,2,128]{2,1,0:T(2,128)(2,1)S(1)}, u32[]{:S(2)}, u32[]{:S(2)}) collective-permute-start(bf16[132,2,128]{2,1,0:T(2,128)(2,1)S(1)} %get-tuple-element.6), channel_id=1, source_target_pairs={{0,1},{1,2},{2,3},{3,4},{4,5},{5,6},{6,7},{7,8},{8,9},{9,10},{10,1... | collective-permute-start | bytes 202760 | tf_op jit(solution)/shard_map/ppermute | solution.py:24
  27.1 0.1 and_and_fusion
  27.2 1.2 collective-permute-done.2
  28.4 1.6 maximum_bitcast_fusion
  30.0 0.3 copy.46
  30.4 0.2 pad.clone
  30.6 0.3 copy.31
  30.9 0.1 slice.75
  31.1 0.5 copy-done.9
  31.5 6.6 %select_maximum_fusion = bf16[130,8,9,128]{3,1,2,0:T(8,128)(2,1)S(1)} fusion(pred[8,9]{0,1:T(8,128)(4,1)S(1)} %copy-done.13, bf16[3,3,128,128]{3,2,1,0:T(8,128)(2,1)S(1)} %copy-done.9, bf16[132,1,7,2,128]{4,2,3,0,1:T(8,128)(2,1)S(1)} %slice.75, bf16[132,1,8,9,128]{4,2,3,0,1:T(8,128)(2,1)S(1)} %copy.31), kind=kOutput, calls=%fused_computation.14 | convolution fusion | flops 2772891648 | bytes 5597256 | tf_op jit(solution)/shard_map/conv_general_dilated | solution.py:48
  38.1 0.3 copy.32
  38.4 2.0 fusion.7
  40.4 0.2 pad.2
  40.7 0.3 copy.34
  41.0 0.1 slice.77
  41.1 0.5 copy-done.10
  41.6 5.7 %broadcast_select_fusion = f32[128,8,9,128]{3,1,2,0:T(8,128)S(1)} fusion(pred[8,9]{0,1:T(8,128)(4,1)S(1)} %copy-done.12, bf16[3,3,128,128]{3,2,1,0:T(8,128)(2,1)S(1)} %copy-done.10, bf16[130,1,7,2,128]{4,2,3,0,1:T(8,128)(2,1)S(1)} %slice.77, bf16[130,1,8,9,128]{4,2,3,0,1:T(8,128)(2,1)S(1)} %copy.34), kind=kOutput, calls=%fused_computation.39 | convolution fusion | flops 2727874560 | bytes 7875656 | tf_op jit(solution)/shard_map/conv_general_dilated | solution.py:48
  47.3 0.9 copy.35
  48.2 0.7 copy-done.3
  48.9 1.4 fusion.11
  50.3 1.9 collective-permute-start.4
  52.3 9.1 %collective-permute-done.4 = bf16[128,15,128]{2,0,1:T(8,128)(2,1)S(1)} collective-permute-done((bf16[128,15,128]{2,0,1:T(8,128)(2,1)S(1)}, bf16[128,15,128]{2,0,1:T(8,128)(2,1)S(1)}, u32[]{:S(2)}, u32[]{:S(2)}) %collective-permute-start.4) | collective-permute-done | bytes 491552 | tf_op jit(solution)/shard_map/ppermute | solution.py:33
  61.5 1.3 collective-permute-start.5
  62.8 2.4 %fusion.27 = f32[32,16,64,128]{3,1,2,0:T(8,128)S(1)} fusion(bf16[128,64,128]{2,0,1:T(8,128)(2,1)S(1)} %fusion.11, s32[32]{0:T(128)S(1)} %get-tuple-element.11), kind=kOutput, calls=%fused_computation.40 | convolution fusion | flops 1073872896 | bytes 18874496 | tf_op jit(solution)/shard_map/ari,ijc->arjc/dot_general | solution.py:147
  65.2 5.6 %collective-permute-done.5 = bf16[15,79,128]{2,0,1:T(8,128)(2,1)S(1)} collective-permute-done((bf16[15,79,128]{2,0,1:T(8,128)(2,1)S(1)}, bf16[15,79,128]{2,0,1:T(8,128)(2,1)S(1)}, u32[]{:S(2)}, u32[]{:S(2)}) %collective-permute-start.5) | collective-permute-done | bytes 303392 | tf_op jit(solution)/shard_map/ppermute | solution.py:33
  70.8 4.7 %add_convert_fusion = bf16[32,16,64,128]{3,1,2,0:T(8,128)(2,1)} fusion(f32[32,16,64,128]{3,1,2,0:T(8,128)S(1)} %fusion.27, bf16[15,79,128]{2,0,1:T(8,128)(2,1)S(1)} %collective-permute-done.5, s32[32]{0:T(128)S(1)} %get-tuple-element.11, s32[15]{0:T(128)S(1)} %iota_add_fusion.1), kind=kOutput, calls=%fused_computation | convolution fusion | flops 134233088 | bytes 25428992 | tf_op jit(solution)/shard_map/ari,ijc->arjc/dot_general | solution.py:148
  75.4 4.9 %fusion = f32[32,16,128,16]{2,3,1,0:T(8,128)S(1)} fusion(bf16[32,16,64,128]{3,1,2,0:T(8,128)(2,1)} %add_convert_fusion, s32[32]{0:T(128)S(1)} %get-tuple-element.10), kind=kOutput, calls=%fused_computation.2 | convolution fusion | flops 134283264 | bytes 12583040 | tf_op jit(solution)/shard_map/abj,arjc->arbc/dot_general | solution.py:159
  80.3 0.7 fusion.63
  81.0 0.7 add_convert_fusion.2
  81.7 2.8 %fusion.30 = f32[32,16,128,16]{2,3,1,0:T(8,128)} fusion(f32[32,16,128,16]{2,3,1,0:T(8,128)S(1)} %fusion, bf16[32,16,15,128]{3,1,2,0:T(8,128)(2,1)S(1)} %add_convert_fusion.2, s32[32]{0:T(128)S(1)} %get-tuple-element.10, s32[15]{0:T(128)S(1)} %iota_add_fusion), kind=kOutput, calls=%fused_computation.44 | convolution fusion | flops 34618368 | bytes 10354876 | tf_op jit(solution)/shard_map/abj,arjc->arbc/dot_general | solution.py:160
  84.5 3.8 %reduce_sum.54 = f32[32,4,4,128]{3,2,1,0:T(4,128)S(1)} reduce(f32[32,4,4,4,4,128]{5,4,3,2,1,0:T(4,128)} %bitcast.88, f32[]{:T(128)} %constant.13.clone.1), dimensions={2,4}, to_apply=%region_0.1 | reduce | flops 983040 | bytes 4456452 | tf_op jit(solution)/shard_map/reduce_sum | solution.py:65
  88.3 0.1 multiply_convert_fusion.2
  88.4 0.7 convert_element_type.97
  89.1 6.9 %all-to-all-start = ((bf16[16,2,2048]{2,1,0:T(2,128)(2,1)}), bf16[16,2,2048]{2,1,0:T(2,128)(2,1)S(1)}, u32[]{:S(2)}, u32[]{:S(2)}) async-start(bf16[16,2,2048]{2,1,0:T(2,128)(2,1)} %convert_element_type.97), calls=%async_computation | async-start | bytes 262144 | tf_op jit(solution)/shard_map/all_to_all | solution.py:165
  96.1 0.1 copy.38
  96.2 5.9 %all-to-all-done = bf16[16,2,2048]{2,1,0:T(2,128)(2,1)S(1)} async-done(((bf16[16,2,2048]{2,1,0:T(2,128)(2,1)}), bf16[16,2,2048]{2,1,0:T(2,128)(2,1)S(1)}, u32[]{:S(2)}, u32[]{:S(2)}) %all-to-all-start) | async-done | bytes 131104 | tf_op jit(solution)/shard_map/all_to_all | solution.py:165
  102.2 0.6 multiply_reduce_fusion.3
  102.8 0.1 multiply_convert_fusion.5
  102.8 0.6 pad_maximum_fusion.1
  103.5 4.3 %copy.41 = bf16[128,64,128]{2,1,0:T(8,128)(2,1)} copy(bf16[128,64,128]{2,0,1:T(8,128)(2,1)} %copy-done.2) | data formatting | bytes 4194304
  107.7 1.2 fusion.44
  109.0 0.1 reshape.130
  109.1 0.1 multiply_reduce_fusion.1
  109.2 0.1 multiply_convert_fusion.3
  109.3 64.1 %all-gather.2.cloned.1.call-done = bf16[4096,513]{1,0:T(8,128)(2,1)} async-done(((bf16[32,513]{1,0:T(8,128)(2,1)}), bf16[4096,513]{1,0:T(8,128)(2,1)}) %all-gather.2.cloned.1.call-update) | async-done | bytes 4202512 | tf_op jit(solution)/shard_map/all_gather | solution.py:39
  173.4 6.9 %fusion.8 = f32[4096,1024]{0,1:T(8,128)S(1)} fusion(bf16[4096,513]{1,0:T(8,128)(2,1)} %all-gather.2.cloned.1.call-done, bf16[512,1536]{1,0:T(8,128)(2,1)} %param.19), kind=kOutput, calls=%fused_computation.17 | convolution fusion | flops 4294967296 | bytes 22020096 | tf_op jit(solution)/shard_map/dot_general | solution.py:82
  180.2 5.7 %copy-done.1 = f32[4096,1024]{0,1:T(8,128)} copy-done((f32[4096,1024]{0,1:T(8,128)}, f32[4096,1024]{0,1:T(8,128)S(1)}, u32[]{:S(2)}) %copy-start.1) | copy-done | bytes 16777240
  186.0 2.6 %slice.111 = bf16[4096,512]{0,1:T(8,128)(2,1)} slice(f32[4096,1024]{0,1:T(8,128)S(1)} %fusion.8), slice={[0:4096], [512:1024]} | slice | bytes 8388608 | tf_op jit(solution)/shard_map/slice | solution.py:83
  188.6 3.9 %slice.86 = f32[4096,512]{0,1:T(8,128)S(1)} slice(f32[4096,1024]{0,1:T(8,128)} %copy-done.1), slice={[0:4096], [0:512]} | slice | bytes 16777216 | tf_op jit(solution)/shard_map/slice | solution.py:83
  192.5 4.5 %multiply_reduce_fusion = f32[4096,8]{0,1:T(8,128)S(1)} fusion(f32[4096,1024]{0,1:T(8,128)} %copy-done.1), kind=kLoop, calls=%fused_computation.5 | loop fusion | flops 4161536 | bytes 8519680 | tf_op jit(solution)/shard_map/reduce_sum | solution.py:75
  197.1 1.6 convert_reduce_fusion.1
  198.7 1.4 convert_reduce_fusion
  200.1 0.8 copy-done.4
  200.9 1.2 fusion.40
  202.1 0.1 convert_element_type.107
  202.2 0.3 multiply_reduce_fusion.2
  202.6 3.7 %fusion.42 = bf16[32,512]{1,0:T(8,128)(2,1)} fusion(f32[32,512]{1,0:T(8,128)S(1)} %get-tuple-element.19, bf16[2048,512]{1,0:T(8,128)(2,1)} %param.23, bf16[512,2048]{1,0:T(8,128)(2,1)} %param.22, f32[32]{0:T(128)S(1)} %get-tuple-element.12, f32[512]{0:T(512)S(1)} %copy-done.6, f32[32]{0:T(128)S(1)} %add_rsqrt_fusion.2), kind=kOutput, calls=%fused_computation.53 | convolution fusion | flops 134905856 | bytes 4294912 | tf_op jit(solution)/shard_map/dot_general | solution.py:192
  (45 shorter events, 0.4 us)
Async XLA Ops:
  7.2 95.0 %copy-start = (bf16[2048,512]{1,0:T(8,128)(2,1)S(1)}, bf16[2048,512]{1,0:T(8,128)(2,1)}, u32[]{:S(2)}) copy-start(bf16[2048,512]{1,0:T(8,128)(2,1)} %param.17) | copy-start | bytes 6291460
  8.1 7.0 %collective-permute-start = (bf16[2,64,128]{2,1,0:T(8,128)(2,1)S(1)}, bf16[2,64,128]{2,1,0:T(8,128)(2,1)S(1)}, u32[]{:S(2)}, u32[]{:S(2)}) collective-permute-start(bf16[2,64,128]{2,1,0:T(8,128)(2,1)S(1)} %get-tuple-element.9), channel_id=1, source_target_pairs={{0,16},{16,32},{32,48},{48,64},{64,80},{80,96},{96,112},{1,17},{17... | collective-permute-start | bytes 98312 | tf_op jit(solution)/shard_map/ppermute | solution.py:24
  13.8 6.2 %collective-permute-start.1 = (bf16[2,64,128]{2,1,0:T(8,128)(2,1)S(1)}, bf16[2,64,128]{2,1,0:T(8,128)(2,1)S(1)}, u32[]{:S(2)}, u32[]{:S(2)}) collective-permute-start(bf16[2,64,128]{2,1,0:T(8,128)(2,1)S(1)} %get-tuple-element.8), channel_id=1, source_target_pairs={{16,0},{32,16},{48,32},{64,48},{80,64},{96,80},{112,96},{17,1},{33... | collective-permute-start | bytes 98312 | tf_op jit(solution)/shard_map/ppermute | solution.py:25
  20.0 7.1 %collective-permute-start.3 = (bf16[132,2,128]{2,1,0:T(2,128)(2,1)S(1)}, bf16[132,2,128]{2,1,0:T(2,128)(2,1)S(1)}, u32[]{:S(2)}, u32[]{:S(2)}) collective-permute-start(bf16[132,2,128]{2,1,0:T(2,128)(2,1)S(1)} %get-tuple-element.7), channel_id=1, source_target_pairs={{1,0},{2,1},{3,2},{4,3},{5,4},{6,5},{7,6},{8,7},{9,8},{10,9},{11,1... | collective-permute-start | bytes 202760 | tf_op jit(solution)/shard_map/ppermute | solution.py:25
  24.1 4.4 %collective-permute-start.2 = (bf16[132,2,128]{2,1,0:T(2,128)(2,1)S(1)}, bf16[132,2,128]{2,1,0:T(2,128)(2,1)S(1)}, u32[]{:S(2)}, u32[]{:S(2)}) collective-permute-start(bf16[132,2,128]{2,1,0:T(2,128)(2,1)S(1)} %get-tuple-element.6), channel_id=1, source_target_pairs={{0,1},{1,2},{2,3},{3,4},{4,5},{5,6},{6,7},{7,8},{8,9},{9,10},{10,1... | collective-permute-start | bytes 202760 | tf_op jit(solution)/shard_map/ppermute | solution.py:24
  30.6 1.0 copy-start.9
  30.6 1.0 copy-start.13
  40.6 1.0 copy-start.10
  40.6 1.0 copy-start.12
  47.3 1.6 copy-start.3
  48.9 3.4 %copy-start.8 = (s32[2,32]{1,0:T(2,128)S(1)}, s32[2,32]{1,0:T(2,128)}, u32[]{:S(2)}) copy-start(s32[2,32]{1,0:T(2,128)} %param.15) | copy-start | bytes 772
  50.3 14.9 %copy-start.2 = (bf16[128,64,128]{2,0,1:T(8,128)(2,1)}, bf16[128,64,128]{2,0,1:T(8,128)(2,1)S(1)}, u32[]{:S(2)}) copy-start(bf16[128,64,128]{2,0,1:T(8,128)(2,1)S(1)} %fusion.11) | copy-start | bytes 6291460
  50.3 11.1 %collective-permute-start.4 = (bf16[128,15,128]{2,0,1:T(8,128)(2,1)S(1)}, bf16[128,15,128]{2,0,1:T(8,128)(2,1)S(1)}, u32[]{:S(2)}, u32[]{:S(2)}) collective-permute-start(bf16[128,15,128]{2,0,1:T(8,128)(2,1)S(1)} %slice.80), channel_id=1, source_target_pairs={{1,0},{2,1},{3,2},{4,3},{5,4},{6,5},{7,6},{8,7},{9,8},{10,9},{11,1... | collective-permute-start | bytes 1474568 | tf_op jit(solution)/shard_map/ppermute | solution.py:33
  61.5 9.3 %collective-permute-start.5 = (bf16[15,79,128]{2,0,1:T(8,128)(2,1)S(1)}, bf16[15,79,128]{2,0,1:T(8,128)(2,1)S(1)}, u32[]{:S(2)}, u32[]{:S(2)}) collective-permute-start(bf16[15,79,128]{2,0,1:T(8,128)(2,1)S(1)} %pad_maximum_fusion), channel_id=1, source_target_pairs={{16,0},{32,16},{48,32},{64,48},{80,64},{96,80},{112,96},{17,1},{33... | collective-permute-start | bytes 910088 | tf_op jit(solution)/shard_map/ppermute | solution.py:33
  84.5 11.5 %copy-start.11 = (s32[32]{0:T(128)S(1)}, s32[32]{0:T(128)}, u32[]{:S(2)}) copy-start(s32[32]{0:T(128)} %param.16) | copy-start | bytes 388
  84.5 18.2 %copy-start.7 = (f32[512]{0:T(512)S(1)}, f32[512]{0:T(512)}, u32[]{:S(2)}) copy-start(f32[512]{0:T(512)} %param.18) | copy-start | bytes 6148
  89.1 13.0 %all-to-all-start = ((bf16[16,2,2048]{2,1,0:T(2,128)(2,1)}), bf16[16,2,2048]{2,1,0:T(2,128)(2,1)S(1)}, u32[]{:S(2)}, u32[]{:S(2)}) async-start(bf16[16,2,2048]{2,1,0:T(2,128)(2,1)} %convert_element_type.97), calls=%async_computation | async-start | bytes 262144 | tf_op jit(solution)/shard_map/all_to_all | solution.py:165
  96.0 77.4 %all-gather.2.cloned.1.call-start = ((), (), s32[]{:S(2)}) async-start(), calls=%async_computation.1 | async-start | bytes 5283840 | tf_op jit(solution)/shard_map/all_gather | solution.py:39
  180.2 5.7 %copy-start.1 = (f32[4096,1024]{0,1:T(8,128)}, f32[4096,1024]{0,1:T(8,128)S(1)}, u32[]{:S(2)}) copy-start(f32[4096,1024]{0,1:T(8,128)S(1)} %fusion.8) | copy-start | bytes 50331652
  198.7 2.2 %copy-start.4 = (bf16[4096,512]{0,1:T(8,128)(2,1)S(1)}, bf16[4096,512]{0,1:T(8,128)(2,1)}, u32[]{:S(2)}) copy-start(bf16[4096,512]{0,1:T(8,128)(2,1)} %slice.111) | copy-start | bytes 12582916
  200.9 1.4 copy-start.5
  200.9 1.7 copy-start.6
Sparse Core Ops, SparseCore 0:
  103.6 69.7 all-gather.1
where the time goes:
time: 214 us; the launch traced here: 213 us
  waiting for transfers between devices  88.8 us (41%)
  matrix products  43.6 us (20%)
  local copies, waits for them, and re-layouts  25.9 us (12%)
  starting transfers between devices  24.2 us (11%)
  other arithmetic  16.1 us (8%)
  between operations  14.6 us (7%)
    all_gather x1, waiting for transfers between devices, sent_together(): out, at, done = (lax.all_gather(both, axis, axis=dim, tiled=True), 0, [])  64.1 us
    ppermute x2, waiting for transfers between devices, from_behind(): return lax.ppermute(x, axis, pairs)  14.6 us
    unnamed x32, local copies, waits for them, and re-layouts  14.6 us
    conv_general_dilated x2, matrix products, conv_valid(): lax.conv_general_dilated(padded[None], kernel, (1, 1), 'VALID', dimension...  12.2 us
    ppermute x2, starting transfers between devices, extended(): before = lax.ppermute(last, axis, up)  8.65 us
    all_to_all x1, starting transfers between devices, per_device(): lax.all_to_all(pool_crops(cut_crops).reshape(col_count, per_peer, -1), 'c...  6.94 us
    dot_general x1, matrix products, keys_values(): jnp.dot(normed, w_qkv[:, model_width:], preferred_element_type=jnp.float32)  6.85 us
    all_to_all x1, waiting for transfers between devices, per_device(): lax.all_to_all(pool_crops(cut_crops).reshape(col_count, per_peer, -1), 'c...  5.92 us
  transfers between devices with their start and end apart: 8, of which 6 were waited for; matrix products, arithmetic and copies ran while one was open for 5% of the time, Pallas kernels for 0%

commit v1 on v0

v1 whole, which is shorter than its diff:
```python
import jax
import jax.numpy as jnp
from jax import lax
from jax.experimental import pallas as pl
from jax.experimental.pallas import tpu as pltpu
from jax.sharding import PartitionSpec as P

HEADS = 8
HEAD_DIM = 64
CROP = 16
EPS = 1e-06
SCORE_SCALE = 3.0

ROWS, COLS, CH = 128, 64, 128
NEAR, FAR = 2, 17
SLOTS_X = 76
PAIRS_1 = 75
PAIRS_2 = 72
NB1, NB2 = 5, 4
WIDE_1, WIDE_2 = 96, 80
F32, BF16 = jnp.float32, jnp.bfloat16


def dot(a, b):
    return lax.dot_general(a, b, (((1,), (0,)), ((), ())), preferred_element_type=F32)


def dot_t(a, b):
    return lax.dot_general(a, b, (((1,), (1,)), ((), ())), preferred_element_type=F32)


def iota(shape, dim):
    return lax.broadcasted_iota(jnp.int32, shape, dim)


def band(kernel_ref, band_ref):
    zero = jnp.zeros((CH, CH), BF16)
    for a in range(4):
        for b in range(3):
            at = pl.ds((a * 3 + b) * CH, CH)
            band_ref[at, 0:CH] = kernel_ref[a * 3 + b] if a < 3 else zero
            band_ref[at, CH : 2 * CH] = kernel_ref[(a - 1) * 3 + b] if a > 0 else zero


def scene_kernel(
    anchor_ref,
    raster_hbm,
    above_hbm,
    below_hbm,
    left_ref,
    right_ref,
    conv1_ref,
    conv2_ref,
    flags_ref,
    gain_ref,
    w_embed_hbm,
    w_qkv_hbm,
    features_hbm,
    payload_ref,
    center,
    shifted_1,
    shifted_2,
    row_wide,
    row_first,
    wide_features,
    out_features,
    band_1,
    band_2,
    block_sum,
    pooled,
    w_embed,
    w_qkv,
    in_sem,
    w_sem,
    out_sem,
):
    row_id = lax.axis_index("row")
    col_id = lax.axis_index("col")
    copies = [
        pltpu.make_async_copy(above_hbm, center.at[pl.ds(0, NEAR)], in_sem.at[0]),
        pltpu.make_async_copy(raster_hbm, center.at[pl.ds(NEAR, ROWS)], in_sem.at[1]),
        pltpu.make_async_copy(below_hbm, center.at[pl.ds(NEAR + ROWS, FAR)], in_sem.at[2]),
    ]
    for copy in copies:
        copy.start()
    weight_copies = [
        pltpu.make_async_copy(w_embed_hbm, w_embed, w_sem.at[0]),
        pltpu.make_async_copy(w_qkv_hbm, w_qkv, w_sem.at[1]),
    ]
    for copy in weight_copies:
        copy.start()
    band(conv1_ref, band_1)
    band(conv2_ref, band_2)
    known = NEAR + ROWS + FAR
    center[pl.ds(known, 2 * SLOTS_X - known)] = jnp.zeros((2 * SLOTS_X - known, COLS, CH), BF16)
    row_wide[...] = jnp.zeros(row_wide.shape, F32)
    for copy in copies:
        copy.wait()

    def spread(slot, _):
        for par in range(2):
            u = slot * 2 + par
            safe = jnp.minimum(u, known - 1)
            row_wide[par, 14:16] = left_ref[safe].astype(F32)
            row_wide[par, 16:80] = center[u].astype(F32)
            row_wide[par, 80 : 80 + FAR] = right_ref[safe].astype(F32)
        for par in range(2):
            for b in range(3):
                lane = (par * 3 + b) * CH
                shifted_1[slot, :, lane : lane + CH] = row_wide[
                    par, 7 + b : 7 + b + WIDE_1
                ].astype(BF16)
        return _

    lax.fori_loop(0, SLOTS_X, spread, 0)

    column = col_id * COLS - 8 + iota((WIDE_1, CH), 0)
    column_in = (column >= 0) & (column < COLS * 16)

    def first(block, _):
        p0 = block * NB1
        low = shifted_1[pl.ds(p0, NB1)].reshape(NB1 * WIDE_1, 6 * CH)
        high = shifted_1[pl.ds(p0 + 1, NB1)].reshape(NB1 * WIDE_1, 6 * CH)
        total = dot(low, band_1[0 : 6 * CH]) + dot(high, band_1[6 * CH :])
        for i in range(NB1):
            for par in range(2):
                rho = row_id * ROWS - 1 + (p0 + i) * 2 + par
                row_in = (rho >= 0) & (rho < ROWS * 8)
                value = total[i * WIDE_1 : (i + 1) * WIDE_1, par * CH : (par + 1) * CH]
                keep = column_in & row_in
                row_first[2 * i + par] = jnp.where(keep, jnp.maximum(value, 0.0), 0.0)
        for i in range(NB1):
            for par in range(2):
                for b in range(3):
                    lane = (par * 3 + b) * CH
                    shifted_2[p0 + i, :, lane : lane + CH] = row_first[
                        2 * i + par, 7 + b : 7 + b + WIDE_2
                    ].astype(BF16)
        return _

    lax.fori_loop(0, PAIRS_1 // NB1, first, 0)

    def second(block, _):
        p0 = block * NB2
        low = shifted_2[pl.ds(p0, NB2)].reshape(NB2 * WIDE_2, 6 * CH)
        high = shifted_2[pl.ds(p0 + 1, NB2)].reshape(NB2 * WIDE_2, 6 * CH)
        total = dot(low, band_2[0 : 6 * CH]) + dot(high, band_2[6 * CH :])
        for i in range(NB2):
            for par in range(2):
                lane = (par * 3 + 1) * CH
                base = shifted_1[p0 + i + 1, :, lane : lane + CH].astype(F32)[8 : 8 + WIDE_2]
                value = total[i * WIDE_2 : (i + 1) * WIDE_2, par * CH : (par + 1) * CH] + base
                value = value.astype(BF16)
                at = pl.multiple_of(((p0 + i) * 2 + par) * WIDE_2, WIDE_2)
                wide_features[pl.ds(at, WIDE_2)] = value.astype(F32)
                out_features[(p0 + i) * 2 + par] = value[:COLS]
        return _

    lax.fori_loop(0, PAIRS_2 // NB2, second, 0)
    out_copy = pltpu.make_async_copy(out_features.at[pl.ds(0, ROWS)], features_hbm, out_sem)
    out_copy.start()

    def crop(agent, _):
        top = anchor_ref[0, agent] - row_id * ROWS
        left = anchor_ref[1, agent] - col_id * COLS
        for rb in range(4):
            start = (top + rb * 4) * WIDE_2 + left
            four = [wide_features[pl.ds(start + i * WIDE_2, CROP)] for i in range(4)]
            block_sum[rb] = (four[0] + four[1]) + (four[2] + four[3])
        for rb in range(4):
            cells = [block_sum[rb, pl.ds(k, 4, stride=4)] for k in range(4)]
            mean = ((cells[0] + cells[1]) + (cells[2] + cells[3])) * (1.0 / 16)
            pooled[pl.ds(rb * 4 * 32 + agent, 4, stride=32)] = mean
        return _

    lax.fori_loop(0, 32, crop, 0)
    for copy in weight_copies:
        copy.wait()
    agents = jnp.concatenate(
        [pooled[b * 32 : (b + 1) * 32].astype(BF16) for b in range(16)], axis=1
    )
    embedded = dot(agents, w_embed[...])
    power = jnp.mean(embedded * embedded, axis=1, keepdims=True)
    normed = (embedded * lax.rsqrt(power + EPS) * gain_ref[...]).astype(BF16)
    projected = dot(normed, w_qkv[...])
    lane_id = iota((32, CH), 1)
    lower = lane_id < HEAD_DIM

    def unit(x):
        squared = x * x
        first_half = jnp.sum(jnp.where(lower, squared, 0.0), axis=1, keepdims=True)
        second_half = jnp.sum(jnp.where(lower, 0.0, squared), axis=1, keepdims=True)
        scale = lax.rsqrt(jnp.where(lower, first_half, second_half) * (1.0 / HEAD_DIM) + EPS)
        return x * scale

    def turned(x):
        return pltpu.roll(x, HEAD_DIM, 1)

    shift = lax.rem(col_id // 4, 4)
    for pair in range(4):
        q_two = unit(projected[:, pair * CH : (pair + 1) * CH])
        k_two = unit(projected[:, 512 + pair * CH : 512 + (pair + 1) * CH])
        v_two = projected[:, 1024 + pair * CH : 1024 + (pair + 1) * CH]
        rolled = (turned(q_two), turned(k_two), turned(v_two))
        for half in range(2):
            h = pair * 2 + half
            q_h = rolled[0] if half else q_two
            k_h = rolled[1] if half else k_two
            v_h = v_two if half else rolled[2]
            kv = jnp.where(lower, k_h, v_h)
            for kp in range(4):
                chunk = h * 4 + kp
                source = embedded[:, (chunk // 8) * CH : (chunk // 8 + 1) * CH]
                offset = (chunk % 8) * 16
                piece = pltpu.roll(source, (HEAD_DIM - offset) % CH, 1)
                high = piece.astype(BF16).astype(F32)
                low = pltpu.roll(piece - high, 16, 1)
                extra = jnp.where(
                    lane_id < 80, high, jnp.where(lane_id < 96, low, flags_ref[...])
                )
                row = jnp.where(lower, q_h, extra)
                for gg in range(4):
                    g = lax.rem(gg + shift, 4)
                    both = jnp.concatenate(
                        [kv[kp * 8 : kp * 8 + 8], row[gg * 8 : gg * 8 + 8]], axis=0
                    )
                    payload_ref[chunk * 4 + g] = both.astype(BF16)
    out_copy.wait()


def attend_kernel(received_ref, out_ref, queries, partial):
    device = lax.axis_index("row") * 16 + lax.axis_index("col")
    quarter = lax.rem(device // 4, 4)
    g = lax.rem(device, 4)
    everything = received_ref[...].astype(F32)
    kv = everything[:, 0:8].reshape(1024, CH)
    q_rows = everything[:, 8:16].reshape(1024, CH)
    queries[...] = q_rows
    flags = queries[pl.ds(0, 128, stride=8)].astype(BF16)
    key = iota((1024, CH), 0)
    lane = iota((1024, CH), 1)
    source = (key // 128) * 16 + quarter * 4 + lax.rem(key // 2, 4)
    chosen = dot((lane == source).astype(F32).astype(BF16), flags)
    wanted = 96 + lax.rem(key // 8, 16) * 2 + lax.rem(key, 2)
    alone = jnp.where(lane == wanted, chosen, 0.0).astype(BF16)
    mask = dot(alone, jnp.ones((CH, CH), BF16))
    lower = lane < HEAD_DIM
    keys = jnp.where(lower, kv, 0.0).astype(BF16)
    values = (jnp.where(lower, 1.0, kv) * mask).astype(BF16)
    factor = SCORE_SCALE / HEAD_DIM**0.5
    step = 256
    lane_s = iota((step, CH), 1)
    for i in range(1024 // step):
        q = queries[i * step : (i + 1) * step]
        weights = jnp.exp(dot_t(q.astype(BF16), keys) * factor).astype(BF16)
        summed = pltpu.roll(dot(weights, values), HEAD_DIM, 1)
        high = summed.astype(BF16).astype(F32)
        partial[i * step : (i + 1) * step] = jnp.where(
            lane_s < HEAD_DIM,
            summed,
            jnp.where(lane_s < 96, q, jnp.where(lane_s < 112, high, summed - high)),
        )
    for r in range(8):
        for oh in range(4):
            dh = lax.rem(g - oh + 4, 4)
            for dl in range(4):
                base = (r * 4 + oh) * 32 + dl * 2
                rows = [partial[pl.ds(base + k, 4, stride=8)] for k in range(2)]
                out_ref[r * 16 + dh * 4 + dl] = jnp.concatenate(rows, axis=0).astype(BF16)


def agent_kernel(returned_ref, live_ref, gain_ref, w_out, w_up, w_down, out_ref):
    lane = iota((32, CH), 1)
    lower = lane < HEAD_DIM
    everything = returned_ref[...].astype(F32)
    attended = []
    embedded = []
    chunk_sum = None
    for h in range(HEADS):
        total = None
        for kp in range(4):
            chunk = h * 4 + kp
            block = everything[chunk * 4 : chunk * 4 + 4].reshape(32, CH)
            total = block if total is None else total + block
            whole = block + pltpu.roll(block, CH - 16, 1)
            placed = pltpu.roll(whole, (chunk % 8 * 16 - HEAD_DIM) % CH, 1)
            here = (lane // 16) == chunk % 8
            chunk_sum = jnp.where(here, placed, 0.0 if chunk % 8 == 0 else chunk_sum)
            if chunk % 8 == 7:
                embedded.append(chunk_sum)
        below = jnp.sum(jnp.where((lane == 96) | (lane == 112), total, 0.0), axis=1, keepdims=True)
        ratio = total / below
        if h % 2 == 0:
            even = ratio
        else:
            attended.append(jnp.where(lower, even, pltpu.roll(ratio, HEAD_DIM, 1)).astype(BF16))
    attended = jnp.concatenate(attended, axis=1)
    embedded = jnp.concatenate(embedded, axis=1)
    after = embedded + dot(attended, w_out[...])
    power = jnp.mean(after * after, axis=1, keepdims=True)
    normed = (after * lax.rsqrt(power + EPS) * gain_ref[...]).astype(BF16)
    activated = jax.nn.gelu(dot(normed, w_up[...])).astype(BF16)
    result = (after + dot(activated, w_down[...])).astype(BF16)
    dh = lax.axis_index("col") // 4
    slot = iota((32, 32), 0)
    at = iota((32, 32), 1)
    g = lax.rem(slot // 8 + dh, 4)
    place = g * 8 + lax.rem(slot, 2) * 4 + lax.rem(slot // 2, 4)
    order = (at == place).astype(F32).astype(BF16)
    out_ref[...] = (dot(order, result) * live_ref[...]).astype(BF16)


VMEM = pl.BlockSpec(memory_space=pltpu.VMEM)
SMEM = pl.BlockSpec(memory_space=pltpu.SMEM)
ANY = pl.BlockSpec(memory_space=pl.ANY)


def scene(anchor, raster, above, below, left, right, conv1, conv2, flags, gain, w_embed, w_qkv):
    return pl.pallas_call(
        scene_kernel,
        out_shape=(
            jax.ShapeDtypeStruct((ROWS, COLS, CH), BF16),
            jax.ShapeDtypeStruct((128, 16, CH), BF16),
        ),
        in_specs=[SMEM, ANY, ANY, ANY, VMEM, VMEM, VMEM, VMEM, VMEM, VMEM, ANY, ANY],
        out_specs=(ANY, VMEM),
        scratch_shapes=[
            pltpu.VMEM((2 * SLOTS_X, COLS, CH), BF16),
            pltpu.VMEM((SLOTS_X, WIDE_1, 6 * CH), BF16),
            pltpu.VMEM((SLOTS_X, WIDE_2, 6 * CH), BF16),
            pltpu.VMEM((2, 112, CH), F32),
            pltpu.VMEM((2 * NB1, WIDE_1, CH), F32),
            pltpu.VMEM((2 * PAIRS_2 * WIDE_2, CH), F32),
            pltpu.VMEM((2 * PAIRS_2, COLS, CH), BF16),
            pltpu.VMEM((12 * CH, 2 * CH), BF16),
            pltpu.VMEM((12 * CH, 2 * CH), BF16),
            pltpu.VMEM((4, CROP, CH), F32),
            pltpu.VMEM((16 * 32, CH), F32),
            pltpu.VMEM(w_embed.shape, BF16),
            pltpu.VMEM(w_qkv.shape, BF16),
            pltpu.SemaphoreType.DMA((3,)),
            pltpu.SemaphoreType.DMA((2,)),
            pltpu.SemaphoreType.DMA,
        ],
        compiler_params=pltpu.CompilerParams(vmem_limit_bytes=56 * 2**20),
        cost_estimate=pl.CostEstimate(flops=10**10, bytes_accessed=10**7, transcendentals=0),
        name="scene",
    )(anchor, raster, above, below, left, right, conv1, conv2, flags, gain, w_embed, w_qkv)


def attend(received):
    return pl.pallas_call(
        attend_kernel,
        out_shape=jax.ShapeDtypeStruct((128, 8, CH), BF16),
        in_specs=[VMEM],
        out_specs=VMEM,
        scratch_shapes=[pltpu.VMEM((1024, CH), F32), pltpu.VMEM((1024, CH), F32)],
        compiler_params=pltpu.CompilerParams(vmem_limit_bytes=40 * 2**20),
        name="attend",
    )(received)


def finish(returned, live, gain, w_out, w_up, w_down):
    return pl.pallas_call(
        agent_kernel,
        out_shape=jax.ShapeDtypeStruct((32, 512), BF16),
        in_specs=[VMEM] * 6,
        out_specs=VMEM,
        compiler_params=pltpu.CompilerParams(vmem_limit_bytes=40 * 2**20),
        name="agents",
    )(returned, live, gain, w_out, w_up, w_down)


def per_device(
    raster,
    conv_first,
    conv_second,
    crop_anchor,
    agent_live,
    w_embed,
    gain_attn,
    w_qkv,
    w_out,
    gain_mlp,
    w_up,
    w_down,
):
    def forward(n):
        return [(i, i + 1) for i in range(n - 1)]

    def backward(n):
        return [(i + 1, i) for i in range(n - 1)]

    above = lax.ppermute(raster[-NEAR:], "row", forward(8))
    below = lax.ppermute(raster[:FAR], "row", backward(8))
    last = jnp.concatenate([above[:, -NEAR:], raster[:, -NEAR:], below[:, -NEAR:]], axis=0)
    initial = jnp.concatenate([above[:, :FAR], raster[:, :FAR], below[:, :FAR]], axis=0)
    left = lax.ppermute(last, "col", forward(16))
    right = lax.ppermute(initial, "col", backward(16))
    flags = jnp.pad(agent_live.astype(F32)[None], ((0, 0), (96, 0)))
    features, payload = scene(
        crop_anchor,
        raster,
        above,
        below,
        left,
        right,
        conv_first.reshape(9, CH, CH),
        conv_second.reshape(9, CH, CH),
        flags,
        gain_attn[None],
        w_embed,
        w_qkv,
    )
    received = lax.all_to_all(payload, ("row", "col"), 0, 0, tiled=True)
    returned = lax.all_to_all(attend(received), ("row", "col"), 0, 0, tiled=True)
    live = agent_live.astype(F32)[:, None]
    agent_out = finish(returned, live, gain_mlp[None], w_out, w_up, w_down)
    return (features, agent_out)


def solution(mesh):
    in_specs = (
        P("row", "col", None),
        P(),
        P(),
        P(None, ("row", "col")),
        P(("row", "col")),
        P(),
        P(),
        P(),
        P(),
        P(),
        P(),
        P(),
    )
    out_specs = (P("row", "col", None), P(("row", "col"), None))
    return jax.shard_map(
        per_device, mesh=mesh, in_specs=in_specs, out_specs=out_specs, check_vma=False
    )
```

time: 214 us -> 101 us (0.47)
  waiting for transfers between devices: 88.8 us -> 19.8 us
  matrix products: 43.6 us -> 0 us
  Pallas kernels: 0 us -> 29.5 us
  blocking collectives: 0 us -> 25.5 us
  local copies, waits for them, and re-layouts: 25.9 us -> 6.06 us
  other arithmetic: 16.1 us -> 0.26 us
  between operations: 14.6 us -> 0.84 us
  starting transfers between devices: 24.2 us -> 18.5 us
    all_gather x1 -> x0, waiting for transfers between devices: 64.1 us -> none  [sent_together(): out, at, done = (lax.all_gather(both, axis, axis=dim, tiled=True), 0, [])]
    dot_general x13 -> x0, matrix products: 31.4 us -> none  [the longest x1 6.85 us: keys_values(): jnp.dot(normed, w_qkv[:, model_width:], preferred_element_type=jnp.float32)]
    pallas_call x0 -> x3, Pallas kernels: none -> 29.5 us  [the longest x1 25 us: scene(): pl.pallas_call(scene_kernel, out_shape=(jax.ShapeDtypeStruct((ROWS, COLS,...]
    all_to_all x0 -> x1, blocking collectives: none -> 25.5 us  [per_device(): received = lax.all_to_all(payload, ('row', 'col'), 0, 0, tiled=True)]
    unnamed x32 -> x19, local copies, waits for them, and re-layouts: 14.6 us -> 2.34 us
    conv_general_dilated x2 -> x0, matrix products: 12.2 us -> none  [conv_valid(): lax.conv_general_dilated(padded[None], kernel, (1, 1), 'VALID', dimension...]
    ppermute x6 -> x4, waiting for transfers between devices: 18.8 us -> 8.8 us  [the longest x1 5.55 us: per_device(): right = lax.ppermute(initial, 'col', backward(16))]
    reduce_sum x3 -> x0, other arithmetic: 8.41 us -> none  [the longest x2 4.62 us: unit_heads(): jnp.mean(shaped * shaped, axis=-1, keepdims=True) + EPS]
  transfers between devices with their start and end apart: 8 -> 5, of which waited for: 6 -> 4; matrix products, arithmetic and copies ran while one was open for 5% -> 3% of each run, Pallas kernels for 0% -> 0%
where the time goes in v1:
time: 101 us; the launch traced here: 100 us
  Pallas kernels  29.5 us (29%)
  blocking collectives  25.5 us (25%)
  waiting for transfers between devices  19.8 us (20%)
  starting transfers between devices  18.5 us (18%)
  local copies, waits for them, and re-layouts  6.06 us (6%)
    all_to_all x1, blocking collectives, per_device(): received = lax.all_to_all(payload, ('row', 'col'), 0, 0, tiled=True)  25.5 us
    pallas_call x1, Pallas kernels, scene(): pl.pallas_call(scene_kernel, out_shape=(jax.ShapeDtypeStruct((ROWS, COLS,...  25 us
    all_to_all x1, waiting for transfers between devices, per_device(): lax.all_to_all(attend(received), ('row', 'col'), 0, 0, tiled=True)  11 us
    ppermute x1, starting transfers between devices, per_device(): above = lax.ppermute(raster[-NEAR:], 'row', forward(8))  6.27 us
    ppermute x1, waiting for transfers between devices, per_device(): right = lax.ppermute(initial, 'col', backward(16))  5.55 us
    all_to_all x1, starting transfers between devices, per_device(): lax.all_to_all(attend(received), ('row', 'col'), 0, 0, tiled=True)  4.51 us
    ppermute x1, starting transfers between devices, per_device(): right = lax.ppermute(initial, 'col', backward(16))  3.41 us
    ppermute x1, starting transfers between devices, per_device(): left = lax.ppermute(last, 'col', forward(16))  3.06 us
  transfers between devices with their start and end apart: 5, of which 4 were waited for; matrix products, arithmetic and copies ran while one was open for 3% of the time, Pallas kernels for 0%

profile of v1, /device:TPU:1, one launch (start us, length us, event | category | flops | bytes accessed | tf_op | source)
XLA Modules:
  0.0 100.5 jit_solution(3857503422486985696)
XLA Ops:
  0.6 0.0 slice-start
  0.6 1.0 %slice.25 = bf16[17,64,128]{2,1,0:T(8,128)(2,1)S(1)} slice(bf16[128,64,128]{2,1,0:T(8,128)(2,1)} %raster_hbm.1), slice={[0:17], [0:64], [0:128]} | slice | bytes 557056 | tf_op jit(solution)/shard_map/slice | solution.py:395
  1.7 1.3 %collective-permute-start.1 = (bf16[17,64,128]{2,1,0:T(8,128)(2,1)S(1)}, bf16[17,64,128]{2,1,0:T(8,128)(2,1)S(1)}, u32[]{:S(2)}, u32[]{:S(2)}) collective-permute-start(bf16[17,64,128]{2,1,0:T(8,128)(2,1)S(1)} %slice.25), channel_id=1, source_target_pairs={{16,0},{32,16},{48,32},{64,48},{80,64},{96,80},{112,96},{17,1},{33... | collective-permute-start | bytes 835592 | tf_op jit(solution)/shard_map/ppermute | solution.py:395
  3.0 0.8 slice.24
  3.8 6.3 %collective-permute-start = (bf16[2,64,128]{2,1,0:T(8,128)(2,1)S(1)}, bf16[2,64,128]{2,1,0:T(8,128)(2,1)S(1)}, u32[]{:S(2)}, u32[]{:S(2)}) collective-permute-start(bf16[2,64,128]{2,1,0:T(8,128)(2,1)S(1)} %slice.24), channel_id=1, source_target_pairs={{0,16},{16,32},{32,48},{48,64},{64,80},{80,96},{96,112},{1,17},{17... | collective-permute-start | bytes 98312 | tf_op jit(solution)/shard_map/ppermute | solution.py:394
  10.0 0.0 slice-done
  10.0 0.0 copy-start.4
  10.1 0.0 copy-start.8
  10.1 0.1 copy.20
  10.2 0.9 collective-permute-done.above_hbm
  11.0 0.0 copy-start.6
  11.1 2.4 %collective-permute-done.1.below_hbm = bf16[17,64,128]{2,1,0:T(8,128)(2,1)S(1)} collective-permute-done((bf16[17,64,128]{2,1,0:T(8,128)(2,1)S(1)}, bf16[17,64,128]{2,1,0:T(8,128)(2,1)S(1)}, u32[]{:S(2)}, u32[]{:S(2)}) %collective-permute-start.1) | collective-permute-done | bytes 278560 | tf_op jit(solution)/shard_map/ppermute | solution.py:395
  13.4 0.0 copy-start.5
  13.5 0.2 pad_maximum_fusion
  13.7 3.4 %collective-permute-start.3 = (bf16[147,17,128]{2,0,1:T(8,128)(2,1)S(1)}, bf16[147,17,128]{2,0,1:T(8,128)(2,1)S(1)}, u32[]{:S(2)}, u32[]{:S(2)}) collective-permute-start(bf16[147,17,128]{2,0,1:T(8,128)(2,1)S(1)} %pad_maximum_fusion), channel_id=1, source_target_pairs={{1,0},{2,1},{3,2},{4,3},{5,4},{6,5},{7,6},{8,7},{9,8},{10,9},{11,1... | collective-permute-start | bytes 1919240 | tf_op jit(solution)/shard_map/ppermute | solution.py:399
  17.1 0.0 copy-done.4
  17.1 0.1 slice.27
  17.2 0.1 pad_maximum_fusion.1
  17.3 3.1 %collective-permute-start.2 = (bf16[147,2,128]{2,1,0:T(2,128)(2,1)S(1)}, bf16[147,2,128]{2,1,0:T(2,128)(2,1)S(1)}, u32[]{:S(2)}, u32[]{:S(2)}) collective-permute-start(bf16[147,2,128]{2,1,0:T(2,128)(2,1)S(1)} %pad_maximum_fusion.1), channel_id=1, source_target_pairs={{0,1},{1,2},{2,3},{3,4},{4,5},{5,6},{6,7},{7,8},{8,9},{9,10},{10,1... | collective-permute-start | bytes 225800 | tf_op jit(solution)/shard_map/ppermute | solution.py:398
  20.4 0.0 copy-done.8
  20.4 0.6 pad.4.flags_ref
  21.0 5.5 %collective-permute-done.3 = bf16[147,17,128]{2,0,1:T(8,128)(2,1)S(1)} collective-permute-done((bf16[147,17,128]{2,0,1:T(8,128)(2,1)S(1)}, bf16[147,17,128]{2,0,1:T(8,128)(2,1)S(1)}, u32[]{:S(2)}, u32[]{:S(2)}) %collective-permute-start.3) | collective-permute-done | bytes 639776 | tf_op jit(solution)/shard_map/ppermute | solution.py:399
  26.6 1.1 %copy.18.right_ref = bf16[147,17,128]{2,1,0:T(8,128)(2,1)} copy(bf16[147,17,128]{2,0,1:T(8,128)(2,1)S(1)} %collective-permute-done.3) | data formatting | bytes 1279488 | tf_op jit(solution)/shard_map/ppermute | solution.py:399
  27.6 0.0 copy-done.6
  27.6 0.0 copy-done.5
  27.6 0.0 collective-permute-done.2.left_ref
  27.6 0.0 copy-start.7
  27.6 0.6 copy-done.7
  28.3 0.0 copy-start.2
  28.3 25.0 %scene.1 = (bf16[128,64,128]{2,1,0:T(8,128)(2,1)}, bf16[128,16,128]{2,1,0:T(8,128)(2,1)}) custom-call(s32[2,32]{1,0:T(2,128)} %anchor_ref.1, bf16[128,64,128]{2,1,0:T(8,128)(2,1)} %raster_hbm.1, bf16[2,64,128]{2,1,0:T(8,128)(2,1)} %copy-done.6, bf16[17,64,128]{2,1,0:T(8,128)(2,1)} %copy-done.5, bf16[147,2,128]{2,1,0:T(2,128)(2,1)} %copy-done.7, ...), custom_call_target="tpu_custom_call" | custom-call | flops 10000000000 | bytes 10000000 | tf_op jit(solution)/shard_map/scene/pallas_call | solution.py:319
  53.3 0.0 copy-start
  53.3 0.0 copy-start.3
  53.3 25.5 %all_to_all.10.received_ref = bf16[128,16,128]{2,1,0:T(8,128)(2,1)S(1)} all-to-all(bf16[128,16,128]{2,1,0:T(8,128)(2,1)} %get-tuple-element.5), channel_id=1, replica_groups=mesh['row'=8,'col'=16] {'row','col'}, dimensions={0} | all-to-all | bytes 1048576 | tf_op jit(solution)/shard_map/all_to_all | solution.py:415
  78.8 2.4 %attend.1 = bf16[128,8,128]{2,1,0:T(8,128)(2,1)} custom-call(bf16[128,16,128]{2,1,0:T(8,128)(2,1)S(1)} %all_to_all.10.received_ref), custom_call_target="tpu_custom_call" | custom-call | tf_op jit(solution)/shard_map/attend/pallas_call | solution.py:352
  81.3 4.5 %all-to-all-start.1 = ((bf16[128,8,128]{2,1,0:T(8,128)(2,1)}), bf16[128,8,128]{2,1,0:T(8,128)(2,1)S(1)}, u32[]{:S(2)}, u32[]{:S(2)}) async-start(bf16[128,8,128]{2,1,0:T(8,128)(2,1)} %attend.1), calls=%async_computation.1 | async-start | bytes 524288 | tf_op jit(solution)/shard_map/all_to_all | solution.py:416
  85.8 0.1 copy.19.live_ref
  85.9 11.0 %all-to-all-done.1.returned_ref = bf16[128,8,128]{2,1,0:T(8,128)(2,1)S(1)} async-done(((bf16[128,8,128]{2,1,0:T(8,128)(2,1)}), bf16[128,8,128]{2,1,0:T(8,128)(2,1)S(1)}, u32[]{:S(2)}, u32[]{:S(2)}) %all-to-all-start.1) | async-done | bytes 262176 | tf_op jit(solution)/shard_map/all_to_all | solution.py:416
  96.9 0.0 copy-done.2
  96.9 0.0 copy-done
  96.9 0.0 copy-done.3
  96.9 0.0 copy-start.1
  96.9 1.6 %copy-done.1 = bf16[2048,512]{1,0:T(8,128)(2,1)S(1)} copy-done((bf16[2048,512]{1,0:T(8,128)(2,1)S(1)}, bf16[2048,512]{1,0:T(8,128)(2,1)}, u32[]{:S(2)}) %copy-start.1) | copy-done | bytes 2097176
  98.5 2.0 %agents.1 = bf16[32,512]{1,0:T(8,128)(2,1)} custom-call(bf16[128,8,128]{2,1,0:T(8,128)(2,1)S(1)} %all-to-all-done.1.returned_ref, f32[32,1]{1,0:T(8,128)S(1)} %copy.19.live_ref, f32[1,512]{1,0:T(1,128)S(1)} %bitcast.8, bf16[512,512]{1,0:T(8,128)(2,1)S(1)} %copy-done.2, bf16[512,2048]{1,0:T(8,128)(2,1)S(1)} %copy-done, bf16[2048,512]{1,0:T(8,128)(2,1)S(1)} %copy-done.1), custom_call_target="tpu_custom_call" | custom-call | tf_op jit(solution)/shard_map/agents/pallas_call | solution.py:364
  (7 shorter events, 0.1 us)
Async XLA Ops:
  0.6 9.4 %slice-start = ((bf16[128,64,128]{2,1,0:T(8,128)(2,1)}), bf16[128,17,128]{2,1,0:T(8,128)(2,1)S(1)}, s32[]{:S(2)}) async-start(bf16[128,64,128]{2,1,0:T(8,128)(2,1)} %raster_hbm.1), calls=%async_computation.2 | async-start | bytes 1572864 | tf_op jit(solution)/shard_map/slice | solution.py:397
  1.7 11.8 %collective-permute-start.1 = (bf16[17,64,128]{2,1,0:T(8,128)(2,1)S(1)}, bf16[17,64,128]{2,1,0:T(8,128)(2,1)S(1)}, u32[]{:S(2)}, u32[]{:S(2)}) collective-permute-start(bf16[17,64,128]{2,1,0:T(8,128)(2,1)S(1)} %slice.25), channel_id=1, source_target_pairs={{16,0},{32,16},{48,32},{64,48},{80,64},{96,80},{112,96},{17,1},{33... | collective-permute-start | bytes 835592 | tf_op jit(solution)/shard_map/ppermute | solution.py:395
  3.8 7.3 %collective-permute-start = (bf16[2,64,128]{2,1,0:T(8,128)(2,1)S(1)}, bf16[2,64,128]{2,1,0:T(8,128)(2,1)S(1)}, u32[]{:S(2)}, u32[]{:S(2)}) collective-permute-start(bf16[2,64,128]{2,1,0:T(8,128)(2,1)S(1)} %slice.24), channel_id=1, source_target_pairs={{0,16},{16,32},{32,48},{48,64},{64,80},{80,96},{96,112},{1,17},{17... | collective-permute-start | bytes 98312 | tf_op jit(solution)/shard_map/ppermute | solution.py:394
  10.0 7.1 %copy-start.4 = (bf16[128,64,128]{2,1,0:T(8,128)(2,1)S(1)}, bf16[128,64,128]{2,1,0:T(8,128)(2,1)}, u32[]{:S(2)}) copy-start(bf16[128,64,128]{2,1,0:T(8,128)(2,1)} %raster_hbm.1) | copy-start | bytes 6291460
  10.1 10.3 %copy-start.8 = (s32[32]{0:T(128)S(1)}, s32[32]{0:T(128)}, u32[]{:S(2)}) copy-start(s32[32]{0:T(128)} %param.16) | copy-start | bytes 388
  11.0 16.6 %copy-start.6 = (bf16[2,64,128]{2,1,0:T(8,128)(2,1)}, bf16[2,64,128]{2,1,0:T(8,128)(2,1)S(1)}, u32[]{:S(2)}) copy-start(bf16[2,64,128]{2,1,0:T(8,128)(2,1)S(1)} %collective-permute-done.above_hbm) | copy-start | bytes 98308
  13.4 14.2 %copy-start.5 = (bf16[17,64,128]{2,1,0:T(8,128)(2,1)}, bf16[17,64,128]{2,1,0:T(8,128)(2,1)S(1)}, u32[]{:S(2)}) copy-start(bf16[17,64,128]{2,1,0:T(8,128)(2,1)S(1)} %collective-permute-done.1.below_hbm) | copy-start | bytes 835588
  13.7 12.9 %collective-permute-start.3 = (bf16[147,17,128]{2,0,1:T(8,128)(2,1)S(1)}, bf16[147,17,128]{2,0,1:T(8,128)(2,1)S(1)}, u32[]{:S(2)}, u32[]{:S(2)}) collective-permute-start(bf16[147,17,128]{2,0,1:T(8,128)(2,1)S(1)} %pad_maximum_fusion), channel_id=1, source_target_pairs={{1,0},{2,1},{3,2},{4,3},{5,4},{6,5},{7,6},{8,7},{9,8},{10,9},{11,1... | collective-permute-start | bytes 1919240 | tf_op jit(solution)/shard_map/ppermute | solution.py:399
  17.3 10.3 %collective-permute-start.2 = (bf16[147,2,128]{2,1,0:T(2,128)(2,1)S(1)}, bf16[147,2,128]{2,1,0:T(2,128)(2,1)S(1)}, u32[]{:S(2)}, u32[]{:S(2)}) collective-permute-start(bf16[147,2,128]{2,1,0:T(2,128)(2,1)S(1)} %pad_maximum_fusion.1), channel_id=1, source_target_pairs={{0,1},{1,2},{2,3},{3,4},{4,5},{5,6},{6,7},{7,8},{8,9},{9,10},{10,1... | collective-permute-start | bytes 225800 | tf_op jit(solution)/shard_map/ppermute | solution.py:398
  27.6 0.6 copy-start.7
  28.3 68.6 %copy-start.2 = (bf16[512,512]{1,0:T(8,128)(2,1)S(1)}, bf16[512,512]{1,0:T(8,128)(2,1)}, u32[]{:S(2)}) copy-start(bf16[512,512]{1,0:T(8,128)(2,1)} %w_out.1) | copy-start | bytes 1572868
  53.3 43.6 %copy-start = (bf16[512,2048]{1,0:T(8,128)(2,1)S(1)}, bf16[512,2048]{1,0:T(8,128)(2,1)}, u32[]{:S(2)}) copy-start(bf16[512,2048]{1,0:T(8,128)(2,1)} %w_up.1) | copy-start | bytes 6291460
  53.3 43.6 %copy-start.3 = (f32[512]{0:T(512)S(1)}, f32[512]{0:T(512)}, u32[]{:S(2)}) copy-start(f32[512]{0:T(512)} %param.21) | copy-start | bytes 6148
  81.3 15.6 %all-to-all-start.1 = ((bf16[128,8,128]{2,1,0:T(8,128)(2,1)}), bf16[128,8,128]{2,1,0:T(8,128)(2,1)S(1)}, u32[]{:S(2)}, u32[]{:S(2)}) async-start(bf16[128,8,128]{2,1,0:T(8,128)(2,1)} %attend.1), calls=%async_computation.1 | async-start | bytes 524288 | tf_op jit(solution)/shard_map/all_to_all | solution.py:416
  96.9 1.6 %copy-start.1 = (bf16[2048,512]{1,0:T(8,128)(2,1)S(1)}, bf16[2048,512]{1,0:T(8,128)(2,1)}, u32[]{:S(2)}) copy-start(bf16[2048,512]{1,0:T(8,128)(2,1)} %w_down.1) | copy-start | bytes 6291460

commit v2 on v1

--- a/solution.py
+++ b/solution.py
@@ -3,6 +3,7 @@
 from jax import lax
 from jax.experimental import pallas as pl
 from jax.experimental.pallas import tpu as pltpu
+from jax.experimental.layout import Layout, with_layout_constraint
 from jax.sharding import PartitionSpec as P
 
 HEADS = 8
@@ -13,11 +14,14 @@
 
 ROWS, COLS, CH = 128, 64, 128
 NEAR, FAR = 2, 17
-SLOTS_X = 76
-PAIRS_1 = 75
+KNOWN = NEAR + ROWS + FAR
+PAIRS_1 = 76
 PAIRS_2 = 72
-NB1, NB2 = 5, 4
-WIDE_1, WIDE_2 = 96, 80
+SLOTS = 77
+NB1, NB2, NBS = 19, 18, 38
+WIDE = 80
+STRIP = 32
+TAPS = ((0, 0), (0, 2), (1, 0), (1, 2), (0, 1), (1, 1))
 F32, BF16 = jnp.float32, jnp.bfloat16
 
 
@@ -35,11 +39,88 @@
 
 def band(kernel_ref, band_ref):
     zero = jnp.zeros((CH, CH), BF16)
-    for a in range(4):
-        for b in range(3):
-            at = pl.ds((a * 3 + b) * CH, CH)
+    for slot in range(2):
+        for i, (par, b) in enumerate(TAPS):
+            a = slot * 2 + par
+            at = pl.ds((slot * 6 + i) * CH, CH)
             band_ref[at, 0:CH] = kernel_ref[a * 3 + b] if a < 3 else zero
             band_ref[at, CH : 2 * CH] = kernel_ref[(a - 1) * 3 + b] if a > 0 else zero
+
+
+def load_center(raster_hbm, above_hbm, below_hbm, center, sems):
+    return [
+        pltpu.make_async_copy(above_hbm, center.at[pl.ds(0, NEAR)], sems.at[0]),
+        pltpu.make_async_copy(raster_hbm, center.at[pl.ds(NEAR, ROWS)], sems.at[1]),
+        pltpu.make_async_copy(below_hbm, center.at[pl.ds(NEAR + ROWS, FAR)], sems.at[2]),
+    ]
+
+
+def row_inside(rho):
+    return (rho >= 0) & (rho < ROWS * 8)
+
+
+def first_kernel(
+    raster_hbm,
+    above_hbm,
+    below_hbm,
+    conv1_ref,
+    inner_hbm,
+    center,
+    shifted_a,
+    shifted_b,
+    row_wide,
+    inner,
+    band_1,
+    in_sem,
+    out_sem,
+):
+    row_id = lax.axis_index("row")
+    copies = load_center(raster_hbm, above_hbm, below_hbm, center, in_sem)
+    for copy in copies:
+        copy.start()
+    band(conv1_ref, band_1)
+    center[pl.ds(KNOWN, 2 * SLOTS - KNOWN)] = jnp.zeros((2 * SLOTS - KNOWN, COLS, CH), BF16)
+    row_wide[:, 0:8] = jnp.zeros((2 * NB1 + 2, 8, CH), F32)
+    row_wide[:, 72:80] = jnp.zeros((2 * NB1 + 2, 8, CH), F32)
+    for copy in copies:
+        copy.wait()
+
+    def spread(block, shifted):
+        for i in range(NB1 + 1):
+            for par in range(2):
+                wide = row_wide.at[2 * i + par]
+                wide[8:72] = center[(block * NB1 + i) * 2 + par].astype(F32)
+                shifted[i, :, (par * 2) * CH : (par * 2 + 1) * CH] = wide[7:71].astype(BF16)
+                shifted[i, :, (par * 2 + 1) * CH : (par * 2 + 2) * CH] = wide[9:73].astype(BF16)
+
+    def multiply(block, shifted):
+        def side(s):
+            plain = center[pl.ds((block * NB1 + s) * 2, 2 * NB1)].reshape(NB1, 2, COLS, CH)
+            parts = [shifted[s : s + NB1], plain[:, 0], plain[:, 1]]
+            return jnp.concatenate(parts, axis=2).reshape(NB1 * COLS, 6 * CH)
+
+        total = dot(side(0), band_1[0 : 6 * CH]) + dot(side(1), band_1[6 * CH :])
+        total = jnp.maximum(total, 0.0)
+        for i in range(NB1):
+            for par in range(2):
+                v = (block * NB1 + i) * 2 + par
+                value = total[i * COLS : (i + 1) * COLS, par * CH : (par + 1) * CH]
+                value = jnp.where(row_inside(row_id * ROWS - 1 + v), value, 0.0)
+                inner[v] = value.astype(BF16)
+
+    blocks = PAIRS_1 // NB1
+    buffers = (shifted_a, shifted_b)
+    spread(0, buffers[0])
+    copies = []
+    for block in range(blocks):
+        multiply(block, buffers[block % 2])
+        if block + 1 < blocks:
+            spread(block + 1, buffers[(block + 1) % 2])
+        part = pl.ds(block * NB1 * 2, NB1 * 2)
+        copies.append(pltpu.make_async_copy(inner.at[part], inner_hbm.at[part], out_sem.at[block]))
+        copies[-1].start()
+    for copy in copies:
+        copy.wait()
 
 
 def scene_kernel(
@@ -49,6 +130,7 @@
     below_hbm,
     left_ref,
     right_ref,
+    inner_hbm,
     conv1_ref,
     conv2_ref,
     flags_ref,
@@ -58,10 +140,13 @@
     features_hbm,
     payload_ref,
     center,
-    shifted_1,
-    shifted_2,
-    row_wide,
+    inner,
+    edge_wide,
+    edge_shifted,
+    edge_first,
     row_first,
+    shifted_a,
+    shifted_b,
     wide_features,
     out_features,
     band_1,
@@ -76,13 +161,11 @@
 ):
     row_id = lax.axis_index("row")
     col_id = lax.axis_index("col")
-    copies = [
-        pltpu.make_async_copy(above_hbm, center.at[pl.ds(0, NEAR)], in_sem.at[0]),
-        pltpu.make_async_copy(raster_hbm, center.at[pl.ds(NEAR, ROWS)], in_sem.at[1]),
-        pltpu.make_async_copy(below_hbm, center.at[pl.ds(NEAR + ROWS, FAR)], in_sem.at[2]),
-    ]
+    copies = load_center(raster_hbm, above_hbm, below_hbm, center, in_sem)
     for copy in copies:
         copy.start()
+    inner_copy = pltpu.make_async_copy(inner_hbm, inner, in_sem.at[3])
+    inner_copy.start()
     weight_copies = [
         pltpu.make_async_copy(w_embed_hbm, w_embed, w_sem.at[0]),
         pltpu.make_async_copy(w_qkv_hbm, w_qkv, w_sem.at[1]),
@@ -91,72 +174,89 @@
         copy.start()
     band(conv1_ref, band_1)
     band(conv2_ref, band_2)
-    known = NEAR + ROWS + FAR
-    center[pl.ds(known, 2 * SLOTS_X - known)] = jnp.zeros((2 * SLOTS_X - known, COLS, CH), BF16)
-    row_wide[...] = jnp.zeros(row_wide.shape, F32)
+    center[pl.ds(KNOWN, 2 * SLOTS - KNOWN)] = jnp.zeros((2 * SLOTS - KNOWN, COLS, CH), BF16)
+    edge_wide[pl.ds(KNOWN * 64, (2 * SLOTS - KNOWN) * 64)] = jnp.zeros(
+        ((2 * SLOTS - KNOWN) * 64, CH), F32
+    )
+    for c in range(NEAR):
+        edge_wide[pl.ds(6 + c, KNOWN, stride=64)] = left_ref[c].astype(F32)
+    for c in range(FAR):
+        edge_wide[pl.ds(32 + c, KNOWN, stride=64)] = right_ref[c].astype(F32)
     for copy in copies:
         copy.wait()
 
-    def spread(slot, _):
+    def edges(slot, _):
         for par in range(2):
             u = slot * 2 + par
-            safe = jnp.minimum(u, known - 1)
-            row_wide[par, 14:16] = left_ref[safe].astype(F32)
-            row_wide[par, 16:80] = center[u].astype(F32)
-            row_wide[par, 80 : 80 + FAR] = right_ref[safe].astype(F32)
-        for par in range(2):
-            for b in range(3):
-                lane = (par * 3 + b) * CH
-                shifted_1[slot, :, lane : lane + CH] = row_wide[
-                    par, 7 + b : 7 + b + WIDE_1
-                ].astype(BF16)
+            wide = edge_wide.at[pl.ds(pl.multiple_of(u * 64, 64), 64)]
+            wide[8:16] = center[u, 0:16].astype(F32)[0:8]
+            wide[24:32] = center[u, 48:64].astype(F32)[8:16]
+            wide[49:64] = jnp.zeros((15, CH), F32)
+        for i, (par, b) in enumerate(TAPS):
+            wide = edge_wide.at[pl.ds(pl.multiple_of((slot * 2 + par) * 64, 64), 64)]
+            both = jnp.concatenate([wide[6 + b : 14 + b], wide[30 + b : 54 + b]], axis=0)
+            edge_shifted[slot, :, i * CH : (i + 1) * CH] = both.astype(BF16)
         return _
 
-    lax.fori_loop(0, SLOTS_X, spread, 0)
-
-    column = col_id * COLS - 8 + iota((WIDE_1, CH), 0)
+    lax.fori_loop(0, SLOTS, edges, 0, unroll=7)
+    strip = iota((STRIP, CH), 0)
+    column = col_id * COLS + jnp.where(strip < 8, strip - 1, strip + 55)
     column_in = (column >= 0) & (column < COLS * 16)
 
-    def first(block, _):
-        p0 = block * NB1
-        low = shifted_1[pl.ds(p0, NB1)].reshape(NB1 * WIDE_1, 6 * CH)
-        high = shifted_1[pl.ds(p0 + 1, NB1)].reshape(NB1 * WIDE_1, 6 * CH)
-        total = dot(low, band_1[0 : 6 * CH]) + dot(high, band_1[6 * CH :])
-        for i in range(NB1):
+    def edge_multiply(block, _):
+        p0 = block * NBS
+
+        def side(s):
+            return edge_shifted[pl.ds(p0 + s, NBS)].reshape(NBS * STRIP, 6 * CH)
+
+        total = dot(side(0), band_1[0 : 6 * CH]) + dot(side(1), band_1[6 * CH :])
+        total = jnp.maximum(total, 0.0)
+        for i in range(NBS):
             for par in range(2):
-                rho = row_id * ROWS - 1 + (p0 + i) * 2 + par
-                row_in = (rho >= 0) & (rho < ROWS * 8)
-                value = total[i * WIDE_1 : (i + 1) * WIDE_1, par * CH : (par + 1) * CH]
-                keep = column_in & row_in
-                row_first[2 * i + par] = jnp.where(keep, jnp.maximum(value, 0.0), 0.0)
-        for i in range(NB1):
+                v = (p0 + i) * 2 + par
+                value = total[i * STRIP : (i + 1) * STRIP, par * CH : (par + 1) * CH]
+                keep = column_in & row_inside(row_id * ROWS - 1 + v)
+                edge_first[v] = jnp.where(keep, value, 0.0)
+        return _
+
+    lax.fori_loop(0, PAIRS_1 // NBS, edge_multiply, 0)
+    inner_copy.wait()
+
+    def assemble(block, shifted):
+        for i in range(NB2 + 1):
             for par in range(2):
-                for b in range(3):
-                    lane = (par * 3 + b) * CH
-                    shifted_2[p0 + i, :, lane : lane + CH] = row_first[
-                        2 * i + par, 7 + b : 7 + b + WIDE_2
-                    ].astype(BF16)
-        return _
-
-    lax.fori_loop(0, PAIRS_1 // NB1, first, 0)
-
-    def second(block, _):
-        p0 = block * NB2
-        low = shifted_2[pl.ds(p0, NB2)].reshape(NB2 * WIDE_2, 6 * CH)
-        high = shifted_2[pl.ds(p0 + 1, NB2)].reshape(NB2 * WIDE_2, 6 * CH)
-        total = dot(low, band_2[0 : 6 * CH]) + dot(high, band_2[6 * CH :])
+                v = (block * NB2 + i) * 2 + par
+                first = row_first.at[2 * i + par]
+                first[8:72] = inner[v].astype(F32)
+                first[7:9] = edge_first[v, 0:2]
+                first[71:95] = edge_first[v, 8:32]
+            for k, (par, b) in enumerate(TAPS):
+                window = row_first[2 * i + par, 7 + b : 7 + b + WIDE]
+                shifted[i, :, k * CH : (k + 1) * CH] = window.astype(BF16)
+
+    def multiply(block, shifted):
+        def side(s):
+            return shifted[s : s + NB2].reshape(NB2 * WIDE, 6 * CH)
+
+        total = dot(side(0), band_2[0 : 6 * CH]) + dot(side(1), band_2[6 * CH :])
         for i in range(NB2):
             for par in range(2):
-                lane = (par * 3 + 1) * CH
-                base = shifted_1[p0 + i + 1, :, lane : lane + CH].astype(F32)[8 : 8 + WIDE_2]
-                value = total[i * WIDE_2 : (i + 1) * WIDE_2, par * CH : (par + 1) * CH] + base
+                row = (block * NB2 + i) * 2 + par
+                u = row + NEAR
+                right = edge_wide[u * 64 + 32 : u * 64 + 48]
+                base = jnp.concatenate([center[u].astype(F32), right], axis=0)
+                value = total[i * WIDE : (i + 1) * WIDE, par * CH : (par + 1) * CH] + base
                 value = value.astype(BF16)
-                at = pl.multiple_of(((p0 + i) * 2 + par) * WIDE_2, WIDE_2)
-                wide_features[pl.ds(at, WIDE_2)] = value.astype(F32)
-                out_features[(p0 + i) * 2 + par] = value[:COLS]
-        return _
-
-    lax.fori_loop(0, PAIRS_2 // NB2, second, 0)
+                wide_features[row * WIDE : (row + 1) * WIDE] = value.astype(F32)
+                out_features[row] = value[:COLS]
+
+    blocks = PAIRS_2 // NB2
+    buffers = (shifted_a, shifted_b)
+    assemble(0, buffers[0])
+    for block in range(blocks):
+        multiply(block, buffers[block % 2])
+        if block + 1 < blocks:
+            assemble(block + 1, buffers[(block + 1) % 2])
     out_copy = pltpu.make_async_copy(out_features.at[pl.ds(0, ROWS)], features_hbm, out_sem)
     out_copy.start()
 
@@ -164,8 +264,8 @@
         top = anchor_ref[0, agent] - row_id * ROWS
         left = anchor_ref[1, agent] - col_id * COLS
         for rb in range(4):
-            start = (top + rb * 4) * WIDE_2 + left
-            four = [wide_features[pl.ds(start + i * WIDE_2, CROP)] for i in range(4)]
+            start = (top + rb * 4) * WIDE + left
+            four = [wide_features[pl.ds(start + i * WIDE, CROP)] for i in range(4)]
             block_sum[rb] = (four[0] + four[1]) + (four[2] + four[3])
         for rb in range(4):
             cells = [block_sum[rb, pl.ds(k, 4, stride=4)] for k in range(4)]
@@ -269,7 +369,11 @@
                 out_ref[r * 16 + dh * 4 + dl] = jnp.concatenate(rows, axis=0).astype(BF16)
 
 
-def agent_kernel(returned_ref, live_ref, gain_ref, w_out, w_up, w_down, out_ref):
+def agent_kernel(
+    returned_ref, live_ref, gain_ref, w_out, w_up, w_down_hbm, out_ref, w_down, w_sem
+):
+    w_copy = pltpu.make_async_copy(w_down_hbm, w_down, w_sem)
+    w_copy.start()
     lane = iota((32, CH), 1)
     lower = lane < HEAD_DIM
     everything = returned_ref[...].astype(F32)
@@ -300,6 +404,7 @@
     power = jnp.mean(after * after, axis=1, keepdims=True)
     normed = (after * lax.rsqrt(power + EPS) * gain_ref[...]).astype(BF16)
     activated = jax.nn.gelu(dot(normed, w_up[...])).astype(BF16)
+    w_copy.wait()
     result = (after + dot(activated, w_down[...])).astype(BF16)
     dh = lax.axis_index("col") // 4
     slot = iota((32, 32), 0)
@@ -313,24 +418,52 @@
 VMEM = pl.BlockSpec(memory_space=pltpu.VMEM)
 SMEM = pl.BlockSpec(memory_space=pltpu.SMEM)
 ANY = pl.BlockSpec(memory_space=pl.ANY)
-
-
-def scene(anchor, raster, above, below, left, right, conv1, conv2, flags, gain, w_embed, w_qkv):
+HBM = pl.BlockSpec(memory_space=pltpu.HBM)
+
+
+def first_layer(raster, above, below, conv1):
+    return pl.pallas_call(
+        first_kernel,
+        out_shape=jax.ShapeDtypeStruct((2 * PAIRS_1, COLS, CH), BF16),
+        in_specs=[HBM, ANY, ANY, VMEM],
+        out_specs=HBM,
+        scratch_shapes=[
+            pltpu.VMEM((2 * SLOTS, COLS, CH), BF16),
+            pltpu.VMEM((NB1 + 1, COLS, 4 * CH), BF16),
+            pltpu.VMEM((NB1 + 1, COLS, 4 * CH), BF16),
+            pltpu.VMEM((2 * NB1 + 2, 80, CH), F32),
+            pltpu.VMEM((2 * PAIRS_1, COLS, CH), BF16),
+            pltpu.VMEM((12 * CH, 2 * CH), BF16),
+            pltpu.SemaphoreType.DMA((3,)),
+            pltpu.SemaphoreType.DMA((PAIRS_1 // NB1,)),
+        ],
+        compiler_params=pltpu.CompilerParams(vmem_limit_bytes=32 * 2**20),
+        cost_estimate=pl.CostEstimate(flops=4 * 10**9, bytes_accessed=5 * 10**6, transcendentals=0),
+        name="first_layer",
+    )(raster, above, below, conv1)
+
+
+def scene(
+    anchor, raster, above, below, left, right, inner, conv1, conv2, flags, gain, w_embed, w_qkv
+):
     return pl.pallas_call(
         scene_kernel,
         out_shape=(
             jax.ShapeDtypeStruct((ROWS, COLS, CH), BF16),
             jax.ShapeDtypeStruct((128, 16, CH), BF16),
         ),
-        in_specs=[SMEM, ANY, ANY, ANY, VMEM, VMEM, VMEM, VMEM, VMEM, VMEM, ANY, ANY],
-        out_specs=(ANY, VMEM),
+        in_specs=[SMEM, HBM, ANY, ANY, VMEM, VMEM, HBM, VMEM, VMEM, VMEM, VMEM, HBM, HBM],
+        out_specs=(HBM, VMEM),
         scratch_shapes=[
-            pltpu.VMEM((2 * SLOTS_X, COLS, CH), BF16),
-            pltpu.VMEM((SLOTS_X, WIDE_1, 6 * CH), BF16),
-            pltpu.VMEM((SLOTS_X, WIDE_2, 6 * CH), BF16),
-            pltpu.VMEM((2, 112, CH), F32),
-            pltpu.VMEM((2 * NB1, WIDE_1, CH), F32),
-            pltpu.VMEM((2 * PAIRS_2 * WIDE_2, CH), F32),
+            pltpu.VMEM((2 * SLOTS, COLS, CH), BF16),
+            pltpu.VMEM((2 * PAIRS_1, COLS, CH), BF16),
+            pltpu.VMEM((2 * SLOTS * 64, CH), F32),
+            pltpu.VMEM((SLOTS, STRIP, 6 * CH), BF16),
+            pltpu.VMEM((2 * PAIRS_1, STRIP, CH), F32),
+            pltpu.VMEM((2 * NB2 + 2, 96, CH), F32),
+            pltpu.VMEM((NB2 + 1, WIDE, 6 * CH), BF16),
+            pltpu.VMEM((NB2 + 1, WIDE, 6 * CH), BF16),
+            pltpu.VMEM((2 * PAIRS_2 * WIDE, CH), F32),
             pltpu.VMEM((2 * PAIRS_2, COLS, CH), BF16),
             pltpu.VMEM((12 * CH, 2 * CH), BF16),
             pltpu.VMEM((12 * CH, 2 * CH), BF16),
@@ -338,14 +471,28 @@
             pltpu.VMEM((16 * 32, CH), F32),
             pltpu.VMEM(w_embed.shape, BF16),
             pltpu.VMEM(w_qkv.shape, BF16),
-            pltpu.SemaphoreType.DMA((3,)),
+            pltpu.SemaphoreType.DMA((4,)),
             pltpu.SemaphoreType.DMA((2,)),
             pltpu.SemaphoreType.DMA,
         ],
-        compiler_params=pltpu.CompilerParams(vmem_limit_bytes=56 * 2**20),
+        compiler_params=pltpu.CompilerParams(vmem_limit_bytes=44 * 2**20),
         cost_estimate=pl.CostEstimate(flops=10**10, bytes_accessed=10**7, transcendentals=0),
         name="scene",
-    )(anchor, raster, above, below, left, right, conv1, conv2, flags, gain, w_embed, w_qkv)
+    )(
+        anchor,
+        raster,
+        above,
+        below,
+        left,
+        right,
+        inner,
+        conv1,
+        conv2,
+        flags,
+        gain,
+        w_embed,
+        w_qkv,
+    )
 
 
 def attend(received):
@@ -355,7 +502,7 @@
         in_specs=[VMEM],
         out_specs=VMEM,
         scratch_shapes=[pltpu.VMEM((1024, CH), F32), pltpu.VMEM((1024, CH), F32)],
-        compiler_params=pltpu.CompilerParams(vmem_limit_bytes=40 * 2**20),
+        compiler_params=pltpu.CompilerParams(vmem_limit_bytes=24 * 2**20),
         name="attend",
     )(received)
 
@@ -364,9 +511,10 @@
     return pl.pallas_call(
         agent_kernel,
         out_shape=jax.ShapeDtypeStruct((32, 512), BF16),
-        in_specs=[VMEM] * 6,
+        in_specs=[VMEM] * 5 + [HBM],
         out_specs=VMEM,
-        compiler_params=pltpu.CompilerParams(vmem_limit_bytes=40 * 2**20),
+        scratch_shapes=[pltpu.VMEM(w_down.shape, BF16), pltpu.SemaphoreType.DMA],
+        compiler_params=pltpu.CompilerParams(vmem_limit_bytes=24 * 2**20),
         name="agents",
     )(returned, live, gain, w_out, w_up, w_down)
 
@@ -391,12 +539,18 @@
     def backward(n):
         return [(i + 1, i) for i in range(n - 1)]
 
-    above = lax.ppermute(raster[-NEAR:], "row", forward(8))
-    below = lax.ppermute(raster[:FAR], "row", backward(8))
-    last = jnp.concatenate([above[:, -NEAR:], raster[:, -NEAR:], below[:, -NEAR:]], axis=0)
-    initial = jnp.concatenate([above[:, :FAR], raster[:, :FAR], below[:, :FAR]], axis=0)
+    def plain(x):
+        return with_layout_constraint(x, Layout(major_to_minor=(0, 1, 2)))
+
+    below = plain(lax.ppermute(plain(raster[:FAR]), "row", backward(8)))
+    above = plain(lax.ppermute(plain(raster[-NEAR:]), "row", forward(8)))
+    parts = (above, raster, below)
+    last = jnp.concatenate([p[:, -NEAR:].transpose(1, 0, 2) for p in parts], axis=1)
+    initial = jnp.concatenate([p[:, :FAR].transpose(1, 0, 2) for p in parts], axis=1)
+    right = lax.ppermute(initial, "col", backward(16))
     left = lax.ppermute(last, "col", forward(16))
-    right = lax.ppermute(initial, "col", backward(16))
+    conv1 = conv_first.reshape(9, CH, CH)
+    inner = first_layer(raster, above, below, conv1)
     flags = jnp.pad(agent_live.astype(F32)[None], ((0, 0), (96, 0)))
     features, payload = scene(
         crop_anchor,
@@ -405,7 +559,8 @@
         below,
         left,
         right,
-        conv_first.reshape(9, CH, CH),
+        inner,
+        conv1,
         conv_second.reshape(9, CH, CH),
         flags,
         gain_attn[None],

time: 101 us -> 94.1 us (0.932)
  waiting for transfers between devices: 19.8 us -> 12.8 us
    pallas_call x1, Pallas kernels: 25 us -> 14 us  [scene(): pl.pallas_call(scene_kernel, out_shape=(jax.ShapeDtypeStruct((ROWS, COLS,...]
    pallas_call x0 -> x1, Pallas kernels: none -> 10.2 us  [first_layer(): pl.pallas_call(first_kernel, out_shape=jax.ShapeDtypeStruct((2 * PAIRS_1,...]
    ppermute x1, waiting for transfers between devices: 5.55 us -> 0.01 us  [per_device(): right = lax.ppermute(initial, 'col', backward(16))]
    ppermute x2, waiting for transfers between devices: 3.25 us -> 1.77 us  [the longest x1 1.77 us: per_device(): below = plain(lax.ppermute(plain(raster[:FAR]), 'row', backward(8)))]
    slice x11 -> x8, local copies, waits for them, and re-layouts: 1.96 us -> 3.23 us  [the longest x3 1.25 us: per_device(): p[:, :FAR].transpose(1, 0, 2)]
    ppermute x1 -> x0, local copies, waits for them, and re-layouts: 1.05 us -> none  [per_device(): right = lax.ppermute(initial, 'col', backward(16))]
    unnamed x19 -> x32, local copies, waits for them, and re-layouts: 2.34 us -> 3.28 us
  transfers between devices with their start and end apart: 5 -> 5, of which waited for: 4 -> 2; matrix products, arithmetic and copies ran while one was open for 3% -> 3% of each run, Pallas kernels for 0% -> 11%
where the time goes in v2:
time: 94.1 us; the launch traced here: 93.7 us
  Pallas kernels  28.9 us (31%)
  blocking collectives  25.3 us (27%)
  starting transfers between devices  18.7 us (20%)
  waiting for transfers between devices  12.8 us (14%)
  local copies, waits for them, and re-layouts  6.67 us (7%)
  between operations  1.11 us (1%)
    all_to_all x1, blocking collectives, per_device(): received = lax.all_to_all(payload, ('row', 'col'), 0, 0, tiled=True)  25.3 us
    pallas_call x1, Pallas kernels, scene(): pl.pallas_call(scene_kernel, out_shape=(jax.ShapeDtypeStruct((ROWS, COLS,...  14 us
    all_to_all x1, waiting for transfers between devices, per_device(): lax.all_to_all(attend(received), ('row', 'col'), 0, 0, tiled=True)  11 us
    pallas_call x1, Pallas kernels, first_layer(): pl.pallas_call(first_kernel, out_shape=jax.ShapeDtypeStruct((2 * PAIRS_1,...  10.2 us
    ppermute x1, starting transfers between devices, per_device(): above = plain(lax.ppermute(plain(raster[-NEAR:]), 'row', forward(8)))  6.4 us
    all_to_all x1, starting transfers between devices, per_device(): lax.all_to_all(attend(received), ('row', 'col'), 0, 0, tiled=True)  4.51 us
    ppermute x1, starting transfers between devices, per_device(): right = lax.ppermute(initial, 'col', backward(16))  3.41 us
    unnamed x32, local copies, waits for them, and re-layouts  3.28 us
  transfers between devices with their start and end apart: 5, of which 2 were waited for; matrix products, arithmetic and copies ran while one was open for 3% of the time, Pallas kernels for 11%

profile of v2, /device:TPU:1, one launch (start us, length us, event | category | flops | bytes accessed | tf_op | source)
XLA Modules:
  0.0 93.7 jit_solution(7048241474814064190)
XLA Ops:
  0.6 0.0 copy-start.2
  0.6 1.1 %slice.25 = bf16[17,64,128]{2,1,0:T(8,128)(2,1)S(1)} slice(bf16[128,64,128]{2,1,0:T(8,128)(2,1)} %raster_hbm.3), slice={[0:17], [0:64], [0:128]} | slice | bytes 557056 | tf_op jit(solution)/shard_map/slice | solution.py:545
  1.8 1.3 %collective-permute-start.1 = (bf16[17,64,128]{2,1,0:T(8,128)(2,1)S(1)}, bf16[17,64,128]{2,1,0:T(8,128)(2,1)S(1)}, u32[]{:S(2)}, u32[]{:S(2)}) collective-permute-start(bf16[17,64,128]{2,1,0:T(8,128)(2,1)S(1)} %slice.25), channel_id=1, source_target_pairs={{16,0},{32,16},{48,32},{64,48},{80,64},{96,80},{112,96},{17,1},{33... | collective-permute-start | bytes 835592 | tf_op jit(solution)/shard_map/ppermute | solution.py:545
  3.1 0.8 slice.24
  3.8 0.0 copy-start.12
  3.8 6.4 %collective-permute-start = (bf16[2,64,128]{2,1,0:T(8,128)(2,1)S(1)}, bf16[2,64,128]{2,1,0:T(8,128)(2,1)S(1)}, u32[]{:S(2)}, u32[]{:S(2)}) collective-permute-start(bf16[2,64,128]{2,1,0:T(8,128)(2,1)S(1)} %slice.24), channel_id=1, source_target_pairs={{0,16},{16,32},{32,48},{48,64},{64,80},{80,96},{96,112},{1,17},{17... | collective-permute-start | bytes 98312 | tf_op jit(solution)/shard_map/ppermute | solution.py:546
  10.2 1.2 %slice.30 = bf16[128,17,128]{2,1,0:T(8,128)(2,1)S(1)} slice(bf16[128,64,128]{2,1,0:T(8,128)(2,1)} %raster_hbm.3), slice={[0:128], [0:17], [0:128]} | slice | bytes 1114112 | tf_op jit(solution)/shard_map/slice | solution.py:549
  11.5 0.0 copy-done.2
  11.5 0.0 copy-start.7
  11.5 0.1 slice.27
  11.6 0.1 copy.33
  11.7 0.0 collective-permute-done.above_hbm
  11.8 1.8 %collective-permute-done.1.below_hbm = bf16[17,64,128]{2,1,0:T(8,128)(2,1)S(1)} collective-permute-done((bf16[17,64,128]{2,1,0:T(8,128)(2,1)S(1)}, bf16[17,64,128]{2,1,0:T(8,128)(2,1)S(1)}, u32[]{:S(2)}, u32[]{:S(2)}) %collective-permute-start.1) | collective-permute-done | bytes 278560 | tf_op jit(solution)/shard_map/ppermute | solution.py:545
  13.6 0.2 pad_maximum_fusion
  13.8 3.4 %collective-permute-start.3 = (bf16[17,147,128]{2,1,0:T(8,128)(2,1)S(1)}, bf16[17,147,128]{2,1,0:T(8,128)(2,1)S(1)}, u32[]{:S(2)}, u32[]{:S(2)}) collective-permute-start(bf16[17,147,128]{2,1,0:T(8,128)(2,1)S(1)} %pad_maximum_fusion), channel_id=1, source_target_pairs={{1,0},{2,1},{3,2},{4,3},{5,4},{6,5},{7,6},{8,7},{9,8},{10,9},{11,1... | collective-permute-start | bytes 1919240 | tf_op jit(solution)/shard_map/ppermute | solution.py:550
  17.2 0.0 copy-done.12
  17.2 0.1 pad.4.flags_ref
  17.4 3.1 %collective-permute-start.2 = (bf16[2,147,128]{2,1,0:T(8,128)(2,1)S(1)}, bf16[2,147,128]{2,1,0:T(8,128)(2,1)S(1)}, u32[]{:S(2)}, u32[]{:S(2)}) collective-permute-start(bf16[2,147,128]{2,1,0:T(8,128)(2,1)S(1)} %pad_maximum_fusion.1), channel_id=1, source_target_pairs={{0,1},{1,2},{2,3},{3,4},{4,5},{5,6},{6,7},{7,8},{8,9},{9,10},{10,1... | collective-permute-start | bytes 225800 | tf_op jit(solution)/shard_map/ppermute | solution.py:551
  20.4 0.0 copy-done.7
  20.4 0.0 copy-start.5
  20.5 0.0 copy-start.6
  20.5 0.0 copy-start.8
  20.5 0.0 copy-start.9
  20.5 0.0 copy-start.10
  20.5 10.2 %first_layer.1.inner_hbm = bf16[152,64,128]{2,1,0:T(8,128)(2,1)S(1)} custom-call(bf16[128,64,128]{2,1,0:T(8,128)(2,1)S(1)} %copy-done.2, bf16[2,64,128]{2,1,0:T(8,128)(2,1)S(1)} %collective-permute-done.above_hbm, bf16[17,64,128]{2,1,0:T(8,128)(2,1)S(1)} %collective-permute-done.1.below_hbm, bf16[9,128,128]{2,1,0:T(8,128)(2,1)S(1)} %bitcast.27), custom_call_target="tpu_custom_call" | custom-call | flops 4000000000 | bytes 5000000 | tf_op jit(solution)/shard_map/first_layer/pallas_call | solution.py:425
  30.7 0.0 copy-start.11
  30.7 1.5 %copy-done.11 = bf16[152,64,128]{2,1,0:T(8,128)(2,1)} copy-done((bf16[152,64,128]{2,1,0:T(8,128)(2,1)}, bf16[152,64,128]{2,1,0:T(8,128)(2,1)S(1)}, u32[]{:S(2)}) %copy-start.11) | copy-done | bytes 2490392
  32.2 0.0 collective-permute-done.2.left_ref
  32.2 0.0 collective-permute-done.3.right_ref
  32.2 0.0 copy-done.5
  32.2 0.0 copy-done.6
  32.2 0.0 copy-done.8
  32.2 0.0 copy-done.9
  32.2 0.0 copy-done.10
  32.2 0.0 copy-start.3
  32.2 14.0 %scene.1 = (bf16[128,64,128]{2,1,0:T(8,128)(2,1)}, bf16[128,16,128]{2,1,0:T(8,128)(2,1)S(1)}) custom-call(s32[2,32]{1,0:T(2,128)S(1)} %copy-done.10, bf16[128,64,128]{2,1,0:T(8,128)(2,1)S(1)} %copy-done.2, bf16[2,64,128]{2,1,0:T(8,128)(2,1)S(1)} %collective-permute-done.above_hbm, bf16[17,64,128]{2,1,0:T(8,128)(2,1)S(1)} %collective-permute-done.1.below_hbm, ...), custom_call_target="tpu_custom_call" | custom-call | flops 10000000000 | bytes 10000000 | tf_op jit(solution)/shard_map/scene/pallas_call | solution.py:449
  46.2 0.0 copy-start
  46.3 0.0 copy-start.4
  46.3 25.3 %all_to_all.10.received_ref = bf16[128,16,128]{2,1,0:T(8,128)(2,1)S(1)} all-to-all(bf16[128,16,128]{2,1,0:T(8,128)(2,1)S(1)} %get-tuple-element.5), channel_id=1, replica_groups=mesh['row'=8,'col'=16] {'row','col'}, dimensions={0} | all-to-all | bytes 1048576 | tf_op jit(solution)/shard_map/all_to_all | solution.py:570
  71.6 2.4 %attend.1 = bf16[128,8,128]{2,1,0:T(8,128)(2,1)} custom-call(bf16[128,16,128]{2,1,0:T(8,128)(2,1)S(1)} %all_to_all.10.received_ref), custom_call_target="tpu_custom_call" | custom-call | tf_op jit(solution)/shard_map/attend/pallas_call | solution.py:499
  74.0 4.5 %all-to-all-start.1 = ((bf16[128,8,128]{2,1,0:T(8,128)(2,1)}), bf16[128,8,128]{2,1,0:T(8,128)(2,1)S(1)}, u32[]{:S(2)}, u32[]{:S(2)}) async-start(bf16[128,8,128]{2,1,0:T(8,128)(2,1)} %attend.1), calls=%async_computation.1 | async-start | bytes 524288 | tf_op jit(solution)/shard_map/all_to_all | solution.py:571
  78.5 0.1 copy.20.live_ref
  78.6 11.0 %all-to-all-done.1.returned_ref = bf16[128,8,128]{2,1,0:T(8,128)(2,1)S(1)} async-done(((bf16[128,8,128]{2,1,0:T(8,128)(2,1)}), bf16[128,8,128]{2,1,0:T(8,128)(2,1)S(1)}, u32[]{:S(2)}, u32[]{:S(2)}) %all-to-all-start.1) | async-done | bytes 262176 | tf_op jit(solution)/shard_map/all_to_all | solution.py:571
  89.6 0.0 copy-done.3
  89.6 0.0 copy-done
  89.6 0.0 copy-done.4
  89.6 0.0 copy-start.1
  89.7 1.6 %copy-done.1 = bf16[2048,512]{1,0:T(8,128)(2,1)S(1)} copy-done((bf16[2048,512]{1,0:T(8,128)(2,1)S(1)}, bf16[2048,512]{1,0:T(8,128)(2,1)}, u32[]{:S(2)}) %copy-start.1) | copy-done | bytes 2097176
  91.2 2.3 %agents.1 = bf16[32,512]{1,0:T(8,128)(2,1)} custom-call(bf16[128,8,128]{2,1,0:T(8,128)(2,1)S(1)} %all-to-all-done.1.returned_ref, f32[32,1]{1,0:T(8,128)S(1)} %copy.20.live_ref, f32[1,512]{1,0:T(1,128)S(1)} %bitcast.26, bf16[512,512]{1,0:T(8,128)(2,1)S(1)} %copy-done.3, bf16[512,2048]{1,0:T(8,128)(2,1)S(1)} %copy-done, bf16[2048,512]{1,0:T(8,128)(2,1)S(1)} %copy-done.1), custom_call_target="tpu_custom_call" | custom-call | tf_op jit(solution)/shard_map/agents/pallas_call | solution.py:511
  (11 shorter events, 0.1 us)
Async XLA Ops:
  0.6 10.8 %copy-start.2 = (bf16[128,64,128]{2,1,0:T(8,128)(2,1)S(1)}, bf16[128,64,128]{2,1,0:T(8,128)(2,1)}, u32[]{:S(2)}) copy-start(bf16[128,64,128]{2,1,0:T(8,128)(2,1)} %raster_hbm.3) | copy-start | bytes 6291460
  1.8 11.8 %collective-permute-start.1 = (bf16[17,64,128]{2,1,0:T(8,128)(2,1)S(1)}, bf16[17,64,128]{2,1,0:T(8,128)(2,1)S(1)}, u32[]{:S(2)}, u32[]{:S(2)}) collective-permute-start(bf16[17,64,128]{2,1,0:T(8,128)(2,1)S(1)} %slice.25), channel_id=1, source_target_pairs={{16,0},{32,16},{48,32},{64,48},{80,64},{96,80},{112,96},{17,1},{33... | collective-permute-start | bytes 835592 | tf_op jit(solution)/shard_map/ppermute | solution.py:545
  3.8 13.3 %copy-start.12 = (s32[32]{0:T(128)S(1)}, s32[32]{0:T(128)}, u32[]{:S(2)}) copy-start(s32[32]{0:T(128)} %param.16) | copy-start | bytes 388
  3.8 7.9 %collective-permute-start = (bf16[2,64,128]{2,1,0:T(8,128)(2,1)S(1)}, bf16[2,64,128]{2,1,0:T(8,128)(2,1)S(1)}, u32[]{:S(2)}, u32[]{:S(2)}) collective-permute-start(bf16[2,64,128]{2,1,0:T(8,128)(2,1)S(1)} %slice.24), channel_id=1, source_target_pairs={{0,16},{16,32},{32,48},{48,64},{64,80},{80,96},{96,112},{1,17},{17... | collective-permute-start | bytes 98312 | tf_op jit(solution)/shard_map/ppermute | solution.py:546
  11.5 8.9 %copy-start.7 = (bf16[3,3,128,128]{3,2,1,0:T(8,128)(2,1)S(1)}, bf16[3,3,128,128]{3,2,1,0:T(8,128)(2,1)}, u32[]{:S(2)}) copy-start(bf16[3,3,128,128]{3,2,1,0:T(8,128)(2,1)} %param.13) | copy-start | bytes 884740
  13.8 18.4 %collective-permute-start.3 = (bf16[17,147,128]{2,1,0:T(8,128)(2,1)S(1)}, bf16[17,147,128]{2,1,0:T(8,128)(2,1)S(1)}, u32[]{:S(2)}, u32[]{:S(2)}) collective-permute-start(bf16[17,147,128]{2,1,0:T(8,128)(2,1)S(1)} %pad_maximum_fusion), channel_id=1, source_target_pairs={{1,0},{2,1},{3,2},{4,3},{5,4},{6,5},{7,6},{8,7},{9,8},{10,9},{11,1... | collective-permute-start | bytes 1919240 | tf_op jit(solution)/shard_map/ppermute | solution.py:550
  17.4 14.8 %collective-permute-start.2 = (bf16[2,147,128]{2,1,0:T(8,128)(2,1)S(1)}, bf16[2,147,128]{2,1,0:T(8,128)(2,1)S(1)}, u32[]{:S(2)}, u32[]{:S(2)}) collective-permute-start(bf16[2,147,128]{2,1,0:T(8,128)(2,1)S(1)} %pad_maximum_fusion.1), channel_id=1, source_target_pairs={{0,1},{1,2},{2,3},{3,4},{4,5},{5,6},{6,7},{7,8},{8,9},{9,10},{10,1... | collective-permute-start | bytes 225800 | tf_op jit(solution)/shard_map/ppermute | solution.py:551
  20.4 11.8 %copy-start.5 = (bf16[2048,512]{1,0:T(8,128)(2,1)S(1)}, bf16[2048,512]{1,0:T(8,128)(2,1)}, u32[]{:S(2)}) copy-start(bf16[2048,512]{1,0:T(8,128)(2,1)} %w_embed_hbm.1) | copy-start | bytes 6291460
  20.5 11.7 %copy-start.6 = (bf16[512,1536]{1,0:T(8,128)(2,1)S(1)}, bf16[512,1536]{1,0:T(8,128)(2,1)}, u32[]{:S(2)}) copy-start(bf16[512,1536]{1,0:T(8,128)(2,1)} %w_qkv_hbm.1) | copy-start | bytes 4718596
  20.5 11.7 %copy-start.8 = (bf16[3,3,128,128]{3,2,1,0:T(8,128)(2,1)S(1)}, bf16[3,3,128,128]{3,2,1,0:T(8,128)(2,1)}, u32[]{:S(2)}) copy-start(bf16[3,3,128,128]{3,2,1,0:T(8,128)(2,1)} %param.14) | copy-start | bytes 884740
  20.5 11.7 %copy-start.9 = (f32[512]{0:T(512)S(1)}, f32[512]{0:T(512)}, u32[]{:S(2)}) copy-start(f32[512]{0:T(512)} %param.18) | copy-start | bytes 6148
  20.5 11.7 %copy-start.10 = (s32[2,32]{1,0:T(2,128)S(1)}, s32[2,32]{1,0:T(2,128)}, u32[]{:S(2)}) copy-start(s32[2,32]{1,0:T(2,128)} %anchor_ref.1) | copy-start | bytes 772
  30.7 1.5 %copy-start.11 = (bf16[152,64,128]{2,1,0:T(8,128)(2,1)}, bf16[152,64,128]{2,1,0:T(8,128)(2,1)S(1)}, u32[]{:S(2)}) copy-start(bf16[152,64,128]{2,1,0:T(8,128)(2,1)S(1)} %first_layer.1.inner_hbm) | copy-start | bytes 7471108
  32.2 57.4 %copy-start.3 = (bf16[512,512]{1,0:T(8,128)(2,1)S(1)}, bf16[512,512]{1,0:T(8,128)(2,1)}, u32[]{:S(2)}) copy-start(bf16[512,512]{1,0:T(8,128)(2,1)} %w_out.1) | copy-start | bytes 1572868
  46.2 43.4 %copy-start = (bf16[512,2048]{1,0:T(8,128)(2,1)S(1)}, bf16[512,2048]{1,0:T(8,128)(2,1)}, u32[]{:S(2)}) copy-start(bf16[512,2048]{1,0:T(8,128)(2,1)} %w_up.1) | copy-start | bytes 6291460
  46.3 43.4 %copy-start.4 = (f32[512]{0:T(512)S(1)}, f32[512]{0:T(512)}, u32[]{:S(2)}) copy-start(f32[512]{0:T(512)} %param.21) | copy-start | bytes 6148
  74.0 15.6 %all-to-all-start.1 = ((bf16[128,8,128]{2,1,0:T(8,128)(2,1)}), bf16[128,8,128]{2,1,0:T(8,128)(2,1)S(1)}, u32[]{:S(2)}, u32[]{:S(2)}) async-start(bf16[128,8,128]{2,1,0:T(8,128)(2,1)} %attend.1), calls=%async_computation.1 | async-start | bytes 524288 | tf_op jit(solution)/shard_map/all_to_all | solution.py:571
  89.6 1.6 %copy-start.1 = (bf16[2048,512]{1,0:T(8,128)(2,1)S(1)}, bf16[2048,512]{1,0:T(8,128)(2,1)}, u32[]{:S(2)}) copy-start(bf16[2048,512]{1,0:T(8,128)(2,1)} %w_down_hbm.1) | copy-start | bytes 6291460

commit v3 on v2

--- a/solution.py
+++ b/solution.py
@@ -18,7 +18,7 @@
 PAIRS_1 = 76
 PAIRS_2 = 72
 SLOTS = 77
-NB1, NB2, NBS = 19, 18, 38
+NB1, NB2 = 19, 18
 WIDE = 80
 STRIP = 32
 TAPS = ((0, 0), (0, 2), (1, 0), (1, 2), (0, 1), (1, 1))
@@ -47,55 +47,66 @@
             band_ref[at, CH : 2 * CH] = kernel_ref[(a - 1) * 3 + b] if a > 0 else zero
 
 
-def load_center(raster_hbm, above_hbm, below_hbm, center, sems):
-    return [
-        pltpu.make_async_copy(above_hbm, center.at[pl.ds(0, NEAR)], sems.at[0]),
-        pltpu.make_async_copy(raster_hbm, center.at[pl.ds(NEAR, ROWS)], sems.at[1]),
-        pltpu.make_async_copy(below_hbm, center.at[pl.ds(NEAR + ROWS, FAR)], sems.at[2]),
-    ]
+def rows_between(low, high, above_ref, raster_ref, below_ref):
+    parts = []
+    for ref, first, count in (
+        (above_ref, 0, NEAR),
+        (raster_ref, NEAR, ROWS),
+        (below_ref, NEAR + ROWS, FAR),
+    ):
+        start, stop = max(low, first), min(high, first + count)
+        if start < stop:
+            parts.append(ref[start - first : stop - first])
+    if high > KNOWN:
+        parts.append(jnp.zeros((high - max(low, KNOWN), COLS, CH), BF16))
+    return parts[0] if len(parts) == 1 else jnp.concatenate(parts, axis=0)
 
 
 def row_inside(rho):
     return (rho >= 0) & (rho < ROWS * 8)
 
 
+def slice_kernel(raster_hbm, top_ref, bottom_ref, sems):
+    copies = [
+        pltpu.make_async_copy(raster_hbm.at[pl.ds(0, FAR)], top_ref, sems.at[0]),
+        pltpu.make_async_copy(raster_hbm.at[pl.ds(ROWS - NEAR, NEAR)], bottom_ref, sems.at[1]),
+    ]
+    for copy in copies:
+        copy.start()
+    for copy in copies:
+        copy.wait()
+
+
 def first_kernel(
-    raster_hbm,
-    above_hbm,
-    below_hbm,
+    raster_ref,
+    above_ref,
+    below_ref,
     conv1_ref,
-    inner_hbm,
-    center,
+    inner_ref,
     shifted_a,
     shifted_b,
     row_wide,
-    inner,
     band_1,
-    in_sem,
-    out_sem,
 ):
     row_id = lax.axis_index("row")
-    copies = load_center(raster_hbm, above_hbm, below_hbm, center, in_sem)
-    for copy in copies:
-        copy.start()
+    center = (above_ref, raster_ref, below_ref)
     band(conv1_ref, band_1)
-    center[pl.ds(KNOWN, 2 * SLOTS - KNOWN)] = jnp.zeros((2 * SLOTS - KNOWN, COLS, CH), BF16)
     row_wide[:, 0:8] = jnp.zeros((2 * NB1 + 2, 8, CH), F32)
     row_wide[:, 72:80] = jnp.zeros((2 * NB1 + 2, 8, CH), F32)
-    for copy in copies:
-        copy.wait()
 
     def spread(block, shifted):
         for i in range(NB1 + 1):
             for par in range(2):
+                u = (block * NB1 + i) * 2 + par
                 wide = row_wide.at[2 * i + par]
-                wide[8:72] = center[(block * NB1 + i) * 2 + par].astype(F32)
+                wide[8:72] = rows_between(u, u + 1, *center)[0].astype(F32)
                 shifted[i, :, (par * 2) * CH : (par * 2 + 1) * CH] = wide[7:71].astype(BF16)
                 shifted[i, :, (par * 2 + 1) * CH : (par * 2 + 2) * CH] = wide[9:73].astype(BF16)
 
     def multiply(block, shifted):
         def side(s):
-            plain = center[pl.ds((block * NB1 + s) * 2, 2 * NB1)].reshape(NB1, 2, COLS, CH)
+            u = (block * NB1 + s) * 2
+            plain = rows_between(u, u + 2 * NB1, *center).reshape(NB1, 2, COLS, CH)
             parts = [shifted[s : s + NB1], plain[:, 0], plain[:, 1]]
             return jnp.concatenate(parts, axis=2).reshape(NB1 * COLS, 6 * CH)
 
@@ -105,44 +116,38 @@
             for par in range(2):
                 v = (block * NB1 + i) * 2 + par
                 value = total[i * COLS : (i + 1) * COLS, par * CH : (par + 1) * CH]
-                value = jnp.where(row_inside(row_id * ROWS - 1 + v), value, 0.0)
-                inner[v] = value.astype(BF16)
+                if v == 0 or v > ROWS:
+                    value = jnp.where(row_inside(row_id * ROWS - 1 + v), value, 0.0)
+                inner_ref[v] = value.astype(BF16)
 
     blocks = PAIRS_1 // NB1
     buffers = (shifted_a, shifted_b)
     spread(0, buffers[0])
-    copies = []
     for block in range(blocks):
         multiply(block, buffers[block % 2])
         if block + 1 < blocks:
             spread(block + 1, buffers[(block + 1) % 2])
-        part = pl.ds(block * NB1 * 2, NB1 * 2)
-        copies.append(pltpu.make_async_copy(inner.at[part], inner_hbm.at[part], out_sem.at[block]))
-        copies[-1].start()
-    for copy in copies:
-        copy.wait()
 
 
 def scene_kernel(
     anchor_ref,
-    raster_hbm,
-    above_hbm,
-    below_hbm,
+    raster_ref,
+    above_ref,
+    below_ref,
     left_ref,
     right_ref,
-    inner_hbm,
+    inner_ref,
     conv1_ref,
     conv2_ref,
     flags_ref,
     gain_ref,
-    w_embed_hbm,
-    w_qkv_hbm,
+    w_embed,
+    w_qkv,
     features_hbm,
     payload_ref,
-    center,
-    inner,
     edge_wide,
-    edge_shifted,
+    edge_a,
+    edge_b,
     edge_first,
     row_first,
     shifted_a,
@@ -153,81 +158,63 @@
     band_2,
     block_sum,
     pooled,
-    w_embed,
-    w_qkv,
-    in_sem,
-    w_sem,
     out_sem,
 ):
     row_id = lax.axis_index("row")
     col_id = lax.axis_index("col")
-    copies = load_center(raster_hbm, above_hbm, below_hbm, center, in_sem)
-    for copy in copies:
-        copy.start()
-    inner_copy = pltpu.make_async_copy(inner_hbm, inner, in_sem.at[3])
-    inner_copy.start()
-    weight_copies = [
-        pltpu.make_async_copy(w_embed_hbm, w_embed, w_sem.at[0]),
-        pltpu.make_async_copy(w_qkv_hbm, w_qkv, w_sem.at[1]),
-    ]
-    for copy in weight_copies:
-        copy.start()
+    center = (above_ref, raster_ref, below_ref)
     band(conv1_ref, band_1)
     band(conv2_ref, band_2)
-    center[pl.ds(KNOWN, 2 * SLOTS - KNOWN)] = jnp.zeros((2 * SLOTS - KNOWN, COLS, CH), BF16)
-    edge_wide[pl.ds(KNOWN * 64, (2 * SLOTS - KNOWN) * 64)] = jnp.zeros(
-        ((2 * SLOTS - KNOWN) * 64, CH), F32
-    )
+    for u in range(2 * SLOTS):
+        edge_wide[u * 64 + 48 : u * 64 + 56] = jnp.zeros((8, CH), F32)
     for c in range(NEAR):
         edge_wide[pl.ds(6 + c, KNOWN, stride=64)] = left_ref[c].astype(F32)
-    for c in range(FAR):
-        edge_wide[pl.ds(32 + c, KNOWN, stride=64)] = right_ref[c].astype(F32)
-    for copy in copies:
-        copy.wait()
-
-    def edges(slot, _):
-        for par in range(2):
-            u = slot * 2 + par
-            wide = edge_wide.at[pl.ds(pl.multiple_of(u * 64, 64), 64)]
-            wide[8:16] = center[u, 0:16].astype(F32)[0:8]
-            wide[24:32] = center[u, 48:64].astype(F32)[8:16]
-            wide[49:64] = jnp.zeros((15, CH), F32)
-        for i, (par, b) in enumerate(TAPS):
-            wide = edge_wide.at[pl.ds(pl.multiple_of((slot * 2 + par) * 64, 64), 64)]
-            both = jnp.concatenate([wide[6 + b : 14 + b], wide[30 + b : 54 + b]], axis=0)
-            edge_shifted[slot, :, i * CH : (i + 1) * CH] = both.astype(BF16)
-        return _
-
-    lax.fori_loop(0, SLOTS, edges, 0, unroll=7)
+    last = right_ref[KNOWN : KNOWN + 10].reshape(160, CH).astype(F32)
+    edge_wide[pl.ds(48, KNOWN, stride=64)] = last[:KNOWN]
+
+    def edges(block, shifted):
+        for i in range(NB1 + 1):
+            for par in range(2):
+                u = (block * NB1 + i) * 2 + par
+                if u < KNOWN:
+                    row = rows_between(u, u + 1, *center)[0]
+                    edge_wide[u * 64 + 8 : u * 64 + 16] = row[0:16].astype(F32)[0:8]
+                    edge_wide[u * 64 + 24 : u * 64 + 32] = row[48:64].astype(F32)[8:16]
+                    edge_wide[u * 64 + 32 : u * 64 + 48] = right_ref[u].astype(F32)
+                else:
+                    edge_wide[u * 64 : u * 64 + 56] = jnp.zeros((56, CH), F32)
+            for k, (par, b) in enumerate(TAPS):
+                at = ((block * NB1 + i) * 2 + par) * 64 + b
+                both = jnp.concatenate(
+                    [edge_wide[at + 6 : at + 14], edge_wide[at + 30 : at + 54]], axis=0
+                )
+                shifted[i, :, k * CH : (k + 1) * CH] = both.astype(BF16)
+
     strip = iota((STRIP, CH), 0)
     column = col_id * COLS + jnp.where(strip < 8, strip - 1, strip + 55)
     column_in = (column >= 0) & (column < COLS * 16)
 
-    def edge_multiply(block, _):
-        p0 = block * NBS
-
+    def edge_multiply(block, shifted):
         def side(s):
-            return edge_shifted[pl.ds(p0 + s, NBS)].reshape(NBS * STRIP, 6 * CH)
+            return shifted[s : s + NB1].reshape(NB1 * STRIP, 6 * CH)
 
         total = dot(side(0), band_1[0 : 6 * CH]) + dot(side(1), band_1[6 * CH :])
         total = jnp.maximum(total, 0.0)
-        for i in range(NBS):
+        for i in range(NB1):
             for par in range(2):
-                v = (p0 + i) * 2 + par
+                v = (block * NB1 + i) * 2 + par
                 value = total[i * STRIP : (i + 1) * STRIP, par * CH : (par + 1) * CH]
-                keep = column_in & row_inside(row_id * ROWS - 1 + v)
+                keep = column_in
+                if v == 0 or v > ROWS:
+                    keep = keep & row_inside(row_id * ROWS - 1 + v)
                 edge_first[v] = jnp.where(keep, value, 0.0)
-        return _
-
-    lax.fori_loop(0, PAIRS_1 // NBS, edge_multiply, 0)
-    inner_copy.wait()
 
     def assemble(block, shifted):
         for i in range(NB2 + 1):
             for par in range(2):
                 v = (block * NB2 + i) * 2 + par
                 first = row_first.at[2 * i + par]
-                first[8:72] = inner[v].astype(F32)
+                first[8:72] = inner_ref[v].astype(F32)
                 first[7:9] = edge_first[v, 0:2]
                 first[71:95] = edge_first[v, 8:32]
             for k, (par, b) in enumerate(TAPS):
@@ -243,13 +230,20 @@
             for par in range(2):
                 row = (block * NB2 + i) * 2 + par
                 u = row + NEAR
-                right = edge_wide[u * 64 + 32 : u * 64 + 48]
-                base = jnp.concatenate([center[u].astype(F32), right], axis=0)
+                middle = rows_between(u, u + 1, *center)[0].astype(F32)
+                base = jnp.concatenate([middle, right_ref[u].astype(F32)], axis=0)
                 value = total[i * WIDE : (i + 1) * WIDE, par * CH : (par + 1) * CH] + base
                 value = value.astype(BF16)
                 wide_features[row * WIDE : (row + 1) * WIDE] = value.astype(F32)
                 out_features[row] = value[:COLS]
 
+    blocks = PAIRS_1 // NB1
+    buffers = (edge_a, edge_b)
+    edges(0, buffers[0])
+    for block in range(blocks):
+        edge_multiply(block, buffers[block % 2])
+        if block + 1 < blocks:
+            edges(block + 1, buffers[(block + 1) % 2])
     blocks = PAIRS_2 // NB2
     buffers = (shifted_a, shifted_b)
     assemble(0, buffers[0])
@@ -274,8 +268,6 @@
         return _
 
     lax.fori_loop(0, 32, crop, 0)
-    for copy in weight_copies:
-        copy.wait()
     agents = jnp.concatenate(
         [pooled[b * 32 : (b + 1) * 32].astype(BF16) for b in range(16)], axis=1
     )
@@ -328,7 +320,9 @@
     out_copy.wait()
 
 
-def attend_kernel(received_ref, out_ref, queries, partial):
+def attend_kernel(received_ref, w_down_hbm, out_ref, w_down_ref, queries, partial, w_sem):
+    w_copy = pltpu.make_async_copy(w_down_hbm, w_down_ref, w_sem)
+    w_copy.start()
     device = lax.axis_index("row") * 16 + lax.axis_index("col")
     quarter = lax.rem(device // 4, 4)
     g = lax.rem(device, 4)
@@ -367,13 +361,10 @@
                 base = (r * 4 + oh) * 32 + dl * 2
                 rows = [partial[pl.ds(base + k, 4, stride=8)] for k in range(2)]
                 out_ref[r * 16 + dh * 4 + dl] = jnp.concatenate(rows, axis=0).astype(BF16)
-
-
-def agent_kernel(
-    returned_ref, live_ref, gain_ref, w_out, w_up, w_down_hbm, out_ref, w_down, w_sem
-):
-    w_copy = pltpu.make_async_copy(w_down_hbm, w_down, w_sem)
-    w_copy.start()
+    w_copy.wait()
+
+
+def agent_kernel(returned_ref, live_ref, gain_ref, w_out, w_up, w_down, out_ref):
     lane = iota((32, CH), 1)
     lower = lane < HEAD_DIM
     everything = returned_ref[...].astype(F32)
@@ -404,7 +395,6 @@
     power = jnp.mean(after * after, axis=1, keepdims=True)
     normed = (after * lax.rsqrt(power + EPS) * gain_ref[...]).astype(BF16)
     activated = jax.nn.gelu(dot(normed, w_up[...])).astype(BF16)
-    w_copy.wait()
     result = (after + dot(activated, w_down[...])).astype(BF16)
     dh = lax.axis_index("col") // 4
     slot = iota((32, 32), 0)
@@ -417,25 +407,34 @@
 
 VMEM = pl.BlockSpec(memory_space=pltpu.VMEM)
 SMEM = pl.BlockSpec(memory_space=pltpu.SMEM)
-ANY = pl.BlockSpec(memory_space=pl.ANY)
 HBM = pl.BlockSpec(memory_space=pltpu.HBM)
+
+
+def row_slices(raster):
+    return pl.pallas_call(
+        slice_kernel,
+        out_shape=(
+            jax.ShapeDtypeStruct((FAR, COLS, CH), BF16),
+            jax.ShapeDtypeStruct((NEAR, COLS, CH), BF16),
+        ),
+        in_specs=[HBM],
+        out_specs=(VMEM, VMEM),
+        scratch_shapes=[pltpu.SemaphoreType.DMA((2,))],
+        name="row_slices",
+    )(raster)
 
 
 def first_layer(raster, above, below, conv1):
     return pl.pallas_call(
         first_kernel,
         out_shape=jax.ShapeDtypeStruct((2 * PAIRS_1, COLS, CH), BF16),
-        in_specs=[HBM, ANY, ANY, VMEM],
-        out_specs=HBM,
+        in_specs=[VMEM] * 4,
+        out_specs=VMEM,
         scratch_shapes=[
-            pltpu.VMEM((2 * SLOTS, COLS, CH), BF16),
             pltpu.VMEM((NB1 + 1, COLS, 4 * CH), BF16),
             pltpu.VMEM((NB1 + 1, COLS, 4 * CH), BF16),
             pltpu.VMEM((2 * NB1 + 2, 80, CH), F32),
-            pltpu.VMEM((2 * PAIRS_1, COLS, CH), BF16),
             pltpu.VMEM((12 * CH, 2 * CH), BF16),
-            pltpu.SemaphoreType.DMA((3,)),
-            pltpu.SemaphoreType.DMA((PAIRS_1 // NB1,)),
         ],
         compiler_params=pltpu.CompilerParams(vmem_limit_bytes=32 * 2**20),
         cost_estimate=pl.CostEstimate(flops=4 * 10**9, bytes_accessed=5 * 10**6, transcendentals=0),
@@ -452,13 +451,12 @@
             jax.ShapeDtypeStruct((ROWS, COLS, CH), BF16),
             jax.ShapeDtypeStruct((128, 16, CH), BF16),
         ),
-        in_specs=[SMEM, HBM, ANY, ANY, VMEM, VMEM, HBM, VMEM, VMEM, VMEM, VMEM, HBM, HBM],
+        in_specs=[SMEM] + [VMEM] * 12,
         out_specs=(HBM, VMEM),
         scratch_shapes=[
-            pltpu.VMEM((2 * SLOTS, COLS, CH), BF16),
-            pltpu.VMEM((2 * PAIRS_1, COLS, CH), BF16),
             pltpu.VMEM((2 * SLOTS * 64, CH), F32),
-            pltpu.VMEM((SLOTS, STRIP, 6 * CH), BF16),
+            pltpu.VMEM((NB1 + 1, STRIP, 6 * CH), BF16),
+            pltpu.VMEM((NB1 + 1, STRIP, 6 * CH), BF16),
             pltpu.VMEM((2 * PAIRS_1, STRIP, CH), F32),
             pltpu.VMEM((2 * NB2 + 2, 96, CH), F32),
             pltpu.VMEM((NB2 + 1, WIDE, 6 * CH), BF16),
@@ -469,10 +467,6 @@
             pltpu.VMEM((12 * CH, 2 * CH), BF16),
             pltpu.VMEM((4, CROP, CH), F32),
             pltpu.VMEM((16 * 32, CH), F32),
-            pltpu.VMEM(w_embed.shape, BF16),
-            pltpu.VMEM(w_qkv.shape, BF16),
-            pltpu.SemaphoreType.DMA((4,)),
-            pltpu.SemaphoreType.DMA((2,)),
             pltpu.SemaphoreType.DMA,
         ],
         compiler_params=pltpu.CompilerParams(vmem_limit_bytes=44 * 2**20),
@@ -495,25 +489,34 @@
     )
 
 
-def attend(received):
+def attend(received, w_down):
     return pl.pallas_call(
         attend_kernel,
-        out_shape=jax.ShapeDtypeStruct((128, 8, CH), BF16),
-        in_specs=[VMEM],
-        out_specs=VMEM,
-        scratch_shapes=[pltpu.VMEM((1024, CH), F32), pltpu.VMEM((1024, CH), F32)],
+        out_shape=(
+            jax.ShapeDtypeStruct((128, 8, CH), BF16),
+            jax.ShapeDtypeStruct(w_down.shape, BF16),
+        ),
+        in_specs=[VMEM, HBM],
+        out_specs=(VMEM, VMEM),
+        scratch_shapes=[
+            pltpu.VMEM((1024, CH), F32),
+            pltpu.VMEM((1024, CH), F32),
+            pltpu.SemaphoreType.DMA,
+        ],
         compiler_params=pltpu.CompilerParams(vmem_limit_bytes=24 * 2**20),
+        cost_estimate=pl.CostEstimate(
+            flops=10**9, bytes_accessed=10**6, transcendentals=2 * 10**6
+        ),
         name="attend",
-    )(received)
+    )(received, w_down)
 
 
 def finish(returned, live, gain, w_out, w_up, w_down):
     return pl.pallas_call(
         agent_kernel,
         out_shape=jax.ShapeDtypeStruct((32, 512), BF16),
-        in_specs=[VMEM] * 5 + [HBM],
+        in_specs=[VMEM] * 6,
         out_specs=VMEM,
-        scratch_shapes=[pltpu.VMEM(w_down.shape, BF16), pltpu.SemaphoreType.DMA],
         compiler_params=pltpu.CompilerParams(vmem_limit_bytes=24 * 2**20),
         name="agents",
     )(returned, live, gain, w_out, w_up, w_down)
@@ -542,12 +545,15 @@
     def plain(x):
         return with_layout_constraint(x, Layout(major_to_minor=(0, 1, 2)))
 
-    below = plain(lax.ppermute(plain(raster[:FAR]), "row", backward(8)))
-    above = plain(lax.ppermute(plain(raster[-NEAR:]), "row", forward(8)))
+    top, bottom = row_slices(raster)
+    below = plain(lax.ppermute(top, "row", backward(8)))
+    above = plain(lax.ppermute(bottom, "row", forward(8)))
     parts = (above, raster, below)
     last = jnp.concatenate([p[:, -NEAR:].transpose(1, 0, 2) for p in parts], axis=1)
-    initial = jnp.concatenate([p[:, :FAR].transpose(1, 0, 2) for p in parts], axis=1)
-    right = lax.ppermute(initial, "col", backward(16))
+    extra = jnp.concatenate([p[:, FAR - 1] for p in parts], axis=0)
+    extra = jnp.pad(extra, ((0, 160 - KNOWN), (0, 0))).reshape(10, 16, CH)
+    initial = jnp.concatenate([p[:, : FAR - 1] for p in parts] + [extra], axis=0)
+    right = plain(lax.ppermute(plain(initial), "col", backward(16)))
     left = lax.ppermute(last, "col", forward(16))
     conv1 = conv_first.reshape(9, CH, CH)
     inner = first_layer(raster, above, below, conv1)
@@ -568,7 +574,8 @@
         w_qkv,
     )
     received = lax.all_to_all(payload, ("row", "col"), 0, 0, tiled=True)
-    returned = lax.all_to_all(attend(received), ("row", "col"), 0, 0, tiled=True)
+    partial, w_down = attend(received, w_down)
+    returned = lax.all_to_all(partial, ("row", "col"), 0, 0, tiled=True)
     live = agent_live.astype(F32)[:, None]
     agent_out = finish(returned, live, gain_mlp[None], w_out, w_up, w_down)
     return (features, agent_out)

time: 94.1 us -> 87.8 us (0.933)
  Pallas kernels: 28.9 us -> 22.7 us
  waiting for transfers between devices: 12.8 us -> 16.3 us
  local copies, waits for them, and re-layouts: 6.67 us -> 3.38 us
    pallas_call x1, Pallas kernels: 10.2 us -> 4.77 us  [first_layer(): pl.pallas_call(first_kernel, out_shape=jax.ShapeDtypeStruct((2 * PAIRS_1,...]
    ppermute x3, waiting for transfers between devices: 1.77 us -> 5.31 us  [the longest x1 3.04 us: per_device(): below = plain(lax.ppermute(top, 'row', backward(8)))]
    slice x5 -> x7, local copies, waits for them, and re-layouts: 3.13 us -> 0.11 us  [the longest x3 0.09 us: per_device(): extra = jnp.concatenate([p[:, FAR - 1] for p in parts], axis=0)]
    pallas_call x1, Pallas kernels: 14 us -> 11.5 us  [scene(): pl.pallas_call(scene_kernel, out_shape=(jax.ShapeDtypeStruct((ROWS, COLS,...]
    pallas_call x1 -> x2, Pallas kernels: 2.43 us -> 4.42 us  [the longest x1 2.58 us: attend(): pl.pallas_call(attend_kernel, out_shape=(jax.ShapeDtypeStruct((128, 8, CH...]
    unnamed x32 -> x34, local copies, waits for them, and re-layouts: 3.28 us -> 3.02 us
  transfers between devices with their start and end apart: 5 -> 5, of which waited for: 2 -> 4; matrix products, arithmetic and copies ran while one was open for 3% -> 0% of each run, Pallas kernels for 11% -> 5%
where the time goes in v3:
time: 87.8 us; the launch traced here: 87.5 us
  blocking collectives  25.1 us (29%)
  Pallas kernels  22.7 us (26%)
  starting transfers between devices  18.9 us (22%)
  waiting for transfers between devices  16.3 us (19%)
  local copies, waits for them, and re-layouts  3.38 us (4%)
  between operations  0.97 us (1%)
    all_to_all x1, blocking collectives, per_device(): received = lax.all_to_all(payload, ('row', 'col'), 0, 0, tiled=True)  25.1 us
    pallas_call x1, Pallas kernels, scene(): pl.pallas_call(scene_kernel, out_shape=(jax.ShapeDtypeStruct((ROWS, COLS,...  11.5 us
    all_to_all x1, waiting for transfers between devices, per_device(): returned = lax.all_to_all(partial, ('row', 'col'), 0, 0, tiled=True)  11 us
    ppermute x1, starting transfers between devices, per_device(): above = plain(lax.ppermute(bottom, 'row', forward(8)))  6.28 us
    pallas_call x1, Pallas kernels, first_layer(): pl.pallas_call(first_kernel, out_shape=jax.ShapeDtypeStruct((2 * PAIRS_1,...  4.77 us
    all_to_all x1, starting transfers between devices, per_device(): returned = lax.all_to_all(partial, ('row', 'col'), 0, 0, tiled=True)  4.51 us
    ppermute x1, starting transfers between devices, per_device(): right = plain(lax.ppermute(plain(initial), 'col', backward(16)))  3.54 us
    ppermute x1, starting transfers between devices, per_device(): left = lax.ppermute(last, 'col', forward(16))  3.1 us
  transfers between devices with their start and end apart: 5, of which 4 were waited for; matrix products, arithmetic and copies ran while one was open for 0% of the time, Pallas kernels for 5%

profile of v3, /device:TPU:1, one launch (start us, length us, event | category | flops | bytes accessed | tf_op | source)
XLA Modules:
  0.0 87.5 jit_solution(12740316054617849079)
XLA Ops:
  0.6 0.0 copy-start
  0.6 0.0 slice-start
  0.6 0.0 copy-start.13
  0.7 1.8 %row_slices.1 = (bf16[17,64,128]{2,1,0:T(8,128)(2,1)}, bf16[2,64,128]{2,1,0:T(8,128)(2,1)}) custom-call(bf16[128,64,128]{2,1,0:T(8,128)(2,1)} %raster_ref.3), custom_call_target="tpu_custom_call" | custom-call | tf_op jit(solution)/shard_map/row_slices/pallas_call | solution.py:414
  2.5 0.0 copy-start.9
  2.5 1.4 %collective-permute-start.1 = (bf16[17,64,128]{2,1,0:T(8,128)(2,1)}, bf16[17,64,128]{2,1,0:T(8,128)(2,1)S(1)}, u32[]{:S(2)}, u32[]{:S(2)}) collective-permute-start(bf16[17,64,128]{2,1,0:T(8,128)(2,1)} %get-tuple-element.9), channel_id=1, source_target_pairs={{16,0},{32,16},{48,32},{64,48},{80,64},{96,80},{112,96},{17,1},{33... | collective-permute-start | bytes 835592 | tf_op jit(solution)/shard_map/ppermute | solution.py:549
  3.9 6.3 %collective-permute-start = (bf16[2,64,128]{2,1,0:T(8,128)(2,1)}, bf16[2,64,128]{2,1,0:T(8,128)(2,1)S(1)}, u32[]{:S(2)}, u32[]{:S(2)}) collective-permute-start(bf16[2,64,128]{2,1,0:T(8,128)(2,1)} %get-tuple-element.8), channel_id=1, source_target_pairs={{0,16},{16,32},{32,48},{48,64},{64,80},{80,96},{96,112},{1,17},{17... | collective-permute-start | bytes 98312 | tf_op jit(solution)/shard_map/ppermute | solution.py:550
  10.2 0.0 copy-done
  10.2 0.1 slice.34
  10.3 0.1 slice.28
  10.4 1.1 %collective-permute-done.above_ref = bf16[2,64,128]{2,1,0:T(8,128)(2,1)S(1)} collective-permute-done((bf16[2,64,128]{2,1,0:T(8,128)(2,1)}, bf16[2,64,128]{2,1,0:T(8,128)(2,1)S(1)}, u32[]{:S(2)}, u32[]{:S(2)}) %collective-permute-start) | collective-permute-done | bytes 32800 | tf_op jit(solution)/shard_map/ppermute | solution.py:550
  11.6 3.0 %collective-permute-done.1.below_ref = bf16[17,64,128]{2,1,0:T(8,128)(2,1)S(1)} collective-permute-done((bf16[17,64,128]{2,1,0:T(8,128)(2,1)}, bf16[17,64,128]{2,1,0:T(8,128)(2,1)S(1)}, u32[]{:S(2)}, u32[]{:S(2)}) %collective-permute-start.1) | collective-permute-done | bytes 278560 | tf_op jit(solution)/shard_map/ppermute | solution.py:549
  14.7 0.0 slice-done
  14.7 0.1 pad_maximum_fusion
  14.8 3.5 %collective-permute-start.3 = (bf16[157,16,128]{2,1,0:T(8,128)(2,1)S(1)}, bf16[157,16,128]{2,1,0:T(8,128)(2,1)S(1)}, u32[]{:S(2)}, u32[]{:S(2)}) collective-permute-start(bf16[157,16,128]{2,1,0:T(8,128)(2,1)S(1)} %pad_maximum_fusion), channel_id=1, source_target_pairs={{1,0},{2,1},{3,2},{4,3},{5,4},{6,5},{7,6},{8,7},{9,8},{10,9},{11,1... | collective-permute-start | bytes 1929224 | tf_op jit(solution)/shard_map/ppermute | solution.py:556
  18.4 0.0 copy-done.13
  18.4 0.1 pad.9.flags_ref
  18.5 3.1 %collective-permute-start.2 = (bf16[2,147,128]{2,1,0:T(8,128)(2,1)S(1)}, bf16[2,147,128]{2,1,0:T(8,128)(2,1)S(1)}, u32[]{:S(2)}, u32[]{:S(2)}) collective-permute-start(bf16[2,147,128]{2,1,0:T(8,128)(2,1)S(1)} %pad_maximum_fusion.1), channel_id=1, source_target_pairs={{0,1},{1,2},{2,3},{3,4},{4,5},{5,6},{6,7},{7,8},{8,9},{9,10},{10,1... | collective-permute-start | bytes 225800 | tf_op jit(solution)/shard_map/ppermute | solution.py:557
  21.6 0.0 copy-done.9
  21.7 0.0 copy-start.6
  21.7 0.0 copy-start.8
  21.7 0.0 copy-start.10
  21.7 0.0 copy-start.11
  21.7 0.0 copy-start.12
  21.7 4.8 %first_layer.1.inner_ref = bf16[152,64,128]{2,1,0:T(8,128)(2,1)S(1)} custom-call(bf16[128,64,128]{2,1,0:T(8,128)(2,1)S(1)} %copy-done, bf16[2,64,128]{2,1,0:T(8,128)(2,1)S(1)} %collective-permute-done.above_ref, bf16[17,64,128]{2,1,0:T(8,128)(2,1)S(1)} %collective-permute-done.1.below_ref, bf16[9,128,128]{2,1,0:T(8,128)(2,1)S(1)} %bitcast.28), custom_call_target="tpu_custom_call" | custom-call | flops 4000000000 | bytes 5000000 | tf_op jit(solution)/shard_map/first_layer/pallas_call | solution.py:428
  26.5 0.0 collective-permute-done.2.left_ref
  26.5 1.2 %collective-permute-done.3.right_ref = bf16[157,16,128]{2,1,0:T(8,128)(2,1)S(1)} collective-permute-done((bf16[157,16,128]{2,1,0:T(8,128)(2,1)S(1)}, bf16[157,16,128]{2,1,0:T(8,128)(2,1)S(1)}, u32[]{:S(2)}, u32[]{:S(2)}) %collective-permute-start.3) | collective-permute-done | bytes 643104 | tf_op jit(solution)/shard_map/ppermute | solution.py:556
  27.7 0.0 copy-done.6
  27.7 0.0 copy-done.8
  27.7 0.0 copy-done.10
  27.7 0.0 copy-done.11
  27.7 0.0 copy-done.12
  27.7 0.0 copy-start.7
  27.7 11.5 %scene.1 = (bf16[128,64,128]{2,1,0:T(8,128)(2,1)}, bf16[128,16,128]{2,1,0:T(8,128)(2,1)S(1)}) custom-call(s32[2,32]{1,0:T(2,128)S(1)} %copy-done.12, bf16[128,64,128]{2,1,0:T(8,128)(2,1)S(1)} %copy-done, bf16[2,64,128]{2,1,0:T(8,128)(2,1)S(1)} %collective-permute-done.above_ref, bf16[17,64,128]{2,1,0:T(8,128)(2,1)S(1)} %collective-permute-done.1.below_ref, ...), custom_call_target="tpu_custom_call" | custom-call | flops 10000000000 | bytes 10000000 | tf_op jit(solution)/shard_map/scene/pallas_call | solution.py:448
  39.2 25.1 %all_to_all.10.received_ref = bf16[128,16,128]{2,1,0:T(8,128)(2,1)S(1)} all-to-all(bf16[128,16,128]{2,1,0:T(8,128)(2,1)S(1)} %get-tuple-element.11), channel_id=1, replica_groups=mesh['row'=8,'col'=16] {'row','col'}, dimensions={0} | all-to-all | bytes 1048576 | tf_op jit(solution)/shard_map/all_to_all | solution.py:576
  64.3 0.0 copy-done.7
  64.3 0.0 copy-start.1
  64.4 0.0 copy-start.4
  64.4 0.0 copy-start.5
  64.4 2.6 %attend.1 = (bf16[128,8,128]{2,1,0:T(8,128)(2,1)}, bf16[2048,512]{1,0:T(8,128)(2,1)S(1)}) custom-call(bf16[128,16,128]{2,1,0:T(8,128)(2,1)S(1)} %all_to_all.10.received_ref, bf16[2048,512]{1,0:T(8,128)(2,1)S(1)} %copy-done.7), custom_call_target="tpu_custom_call" | custom-call | flops 1000000000 | bytes 1000000 | tf_op jit(solution)/shard_map/attend/pallas_call | solution.py:493
  66.9 0.0 copy-start.2
  67.0 1.3 %copy-done.2 = bf16[2048,512]{1,0:T(8,128)(2,1)} copy-done((bf16[2048,512]{1,0:T(8,128)(2,1)}, bf16[2048,512]{1,0:T(8,128)(2,1)S(1)}, u32[]{:S(2)}) %copy-start.2) | copy-done | bytes 2097176
  68.3 4.5 %all-to-all-start.1 = ((bf16[128,8,128]{2,1,0:T(8,128)(2,1)}), bf16[128,8,128]{2,1,0:T(8,128)(2,1)S(1)}, u32[]{:S(2)}, u32[]{:S(2)}) async-start(bf16[128,8,128]{2,1,0:T(8,128)(2,1)} %get-tuple-element.12), calls=%async_computation.1 | async-start | bytes 524288 | tf_op jit(solution)/shard_map/all_to_all | solution.py:578
  72.8 0.1 copy.22.live_ref
  72.9 11.0 %all-to-all-done.1.returned_ref = bf16[128,8,128]{2,1,0:T(8,128)(2,1)S(1)} async-done(((bf16[128,8,128]{2,1,0:T(8,128)(2,1)}), bf16[128,8,128]{2,1,0:T(8,128)(2,1)S(1)}, u32[]{:S(2)}, u32[]{:S(2)}) %all-to-all-start.1) | async-done | bytes 262176 | tf_op jit(solution)/shard_map/all_to_all | solution.py:578
  83.9 0.0 copy-done.1
  83.9 0.0 copy-done.4
  83.9 0.0 copy-done.5
  83.9 0.0 copy-start.3
  83.9 1.6 %copy-done.3 = bf16[2048,512]{1,0:T(8,128)(2,1)S(1)} copy-done((bf16[2048,512]{1,0:T(8,128)(2,1)S(1)}, bf16[2048,512]{1,0:T(8,128)(2,1)}, u32[]{:S(2)}) %copy-start.3) | copy-done | bytes 2097176
  85.5 2.0 %agents.1 = bf16[32,512]{1,0:T(8,128)(2,1)} custom-call(bf16[128,8,128]{2,1,0:T(8,128)(2,1)S(1)} %all-to-all-done.1.returned_ref, f32[32,1]{1,0:T(8,128)S(1)} %copy.22.live_ref, f32[1,512]{1,0:T(1,128)S(1)} %bitcast.27, bf16[512,512]{1,0:T(8,128)(2,1)S(1)} %copy-done.4, bf16[512,2048]{1,0:T(8,128)(2,1)S(1)} %copy-done.1, bf16[2048,512]{1,0:T(8,128)(2,1)S(1)} %copy-done.3), custom_call_target="tpu_custom_call" | custom-call | tf_op jit(solution)/shard_map/agents/pallas_call | solution.py:515
  (15 shorter events, 0.1 us)
Async XLA Ops:
  0.6 9.6 %copy-start = (bf16[128,64,128]{2,1,0:T(8,128)(2,1)S(1)}, bf16[128,64,128]{2,1,0:T(8,128)(2,1)}, u32[]{:S(2)}) copy-start(bf16[128,64,128]{2,1,0:T(8,128)(2,1)} %raster_ref.3) | copy-start | bytes 6291460
  0.6 14.0 %slice-start = ((bf16[128,64,128]{2,1,0:T(8,128)(2,1)}), bf16[128,16,128]{2,1,0:T(8,128)(2,1)S(1)}, s32[]{:S(2)}) async-start(bf16[128,64,128]{2,1,0:T(8,128)(2,1)} %raster_ref.3), calls=%async_computation.2 | async-start | bytes 1048576 | tf_op jit(solution)/shard_map/slice | solution.py:555
  0.6 17.7 %copy-start.13 = (s32[32]{0:T(128)S(1)}, s32[32]{0:T(128)}, u32[]{:S(2)}) copy-start(s32[32]{0:T(128)} %param.16) | copy-start | bytes 388
  2.5 19.1 %copy-start.9 = (bf16[3,3,128,128]{3,2,1,0:T(8,128)(2,1)S(1)}, bf16[3,3,128,128]{3,2,1,0:T(8,128)(2,1)}, u32[]{:S(2)}) copy-start(bf16[3,3,128,128]{3,2,1,0:T(8,128)(2,1)} %param.13) | copy-start | bytes 884740
  2.5 12.1 %collective-permute-start.1 = (bf16[17,64,128]{2,1,0:T(8,128)(2,1)}, bf16[17,64,128]{2,1,0:T(8,128)(2,1)S(1)}, u32[]{:S(2)}, u32[]{:S(2)}) collective-permute-start(bf16[17,64,128]{2,1,0:T(8,128)(2,1)} %get-tuple-element.9), channel_id=1, source_target_pairs={{16,0},{32,16},{48,32},{64,48},{80,64},{96,80},{112,96},{17,1},{33... | collective-permute-start | bytes 835592 | tf_op jit(solution)/shard_map/ppermute | solution.py:549
  3.9 7.6 %collective-permute-start = (bf16[2,64,128]{2,1,0:T(8,128)(2,1)}, bf16[2,64,128]{2,1,0:T(8,128)(2,1)S(1)}, u32[]{:S(2)}, u32[]{:S(2)}) collective-permute-start(bf16[2,64,128]{2,1,0:T(8,128)(2,1)} %get-tuple-element.8), channel_id=1, source_target_pairs={{0,16},{16,32},{32,48},{48,64},{64,80},{80,96},{96,112},{1,17},{17... | collective-permute-start | bytes 98312 | tf_op jit(solution)/shard_map/ppermute | solution.py:550
  14.8 12.9 %collective-permute-start.3 = (bf16[157,16,128]{2,1,0:T(8,128)(2,1)S(1)}, bf16[157,16,128]{2,1,0:T(8,128)(2,1)S(1)}, u32[]{:S(2)}, u32[]{:S(2)}) collective-permute-start(bf16[157,16,128]{2,1,0:T(8,128)(2,1)S(1)} %pad_maximum_fusion), channel_id=1, source_target_pairs={{1,0},{2,1},{3,2},{4,3},{5,4},{6,5},{7,6},{8,7},{9,8},{10,9},{11,1... | collective-permute-start | bytes 1929224 | tf_op jit(solution)/shard_map/ppermute | solution.py:556
  18.5 8.0 %collective-permute-start.2 = (bf16[2,147,128]{2,1,0:T(8,128)(2,1)S(1)}, bf16[2,147,128]{2,1,0:T(8,128)(2,1)S(1)}, u32[]{:S(2)}, u32[]{:S(2)}) collective-permute-start(bf16[2,147,128]{2,1,0:T(8,128)(2,1)S(1)} %pad_maximum_fusion.1), channel_id=1, source_target_pairs={{0,1},{1,2},{2,3},{3,4},{4,5},{5,6},{6,7},{7,8},{8,9},{9,10},{10,1... | collective-permute-start | bytes 225800 | tf_op jit(solution)/shard_map/ppermute | solution.py:557
  21.7 6.0 %copy-start.6 = (bf16[2048,512]{1,0:T(8,128)(2,1)S(1)}, bf16[2048,512]{1,0:T(8,128)(2,1)}, u32[]{:S(2)}) copy-start(bf16[2048,512]{1,0:T(8,128)(2,1)} %w_embed.1) | copy-start | bytes 6291460
  21.7 6.0 %copy-start.8 = (bf16[512,1536]{1,0:T(8,128)(2,1)S(1)}, bf16[512,1536]{1,0:T(8,128)(2,1)}, u32[]{:S(2)}) copy-start(bf16[512,1536]{1,0:T(8,128)(2,1)} %w_qkv.1) | copy-start | bytes 4718596
  21.7 6.0 %copy-start.10 = (bf16[3,3,128,128]{3,2,1,0:T(8,128)(2,1)S(1)}, bf16[3,3,128,128]{3,2,1,0:T(8,128)(2,1)}, u32[]{:S(2)}) copy-start(bf16[3,3,128,128]{3,2,1,0:T(8,128)(2,1)} %param.14) | copy-start | bytes 884740
  21.7 6.0 %copy-start.11 = (f32[512]{0:T(512)S(1)}, f32[512]{0:T(512)}, u32[]{:S(2)}) copy-start(f32[512]{0:T(512)} %param.18) | copy-start | bytes 6148
  21.7 6.0 %copy-start.12 = (s32[2,32]{1,0:T(2,128)S(1)}, s32[2,32]{1,0:T(2,128)}, u32[]{:S(2)}) copy-start(s32[2,32]{1,0:T(2,128)} %anchor_ref.1) | copy-start | bytes 772
  27.7 36.7 %copy-start.7 = (bf16[2048,512]{1,0:T(8,128)(2,1)S(1)}, bf16[2048,512]{1,0:T(8,128)(2,1)}, u32[]{:S(2)}) copy-start(bf16[2048,512]{1,0:T(8,128)(2,1)} %w_down_hbm.1) | copy-start | bytes 6291460
  64.3 19.5 %copy-start.1 = (bf16[512,2048]{1,0:T(8,128)(2,1)S(1)}, bf16[512,2048]{1,0:T(8,128)(2,1)}, u32[]{:S(2)}) copy-start(bf16[512,2048]{1,0:T(8,128)(2,1)} %w_up.1) | copy-start | bytes 6291460
  64.4 19.5 %copy-start.4 = (bf16[512,512]{1,0:T(8,128)(2,1)S(1)}, bf16[512,512]{1,0:T(8,128)(2,1)}, u32[]{:S(2)}) copy-start(bf16[512,512]{1,0:T(8,128)(2,1)} %w_out.1) | copy-start | bytes 1572868
  64.4 19.6 %copy-start.5 = (f32[512]{0:T(512)S(1)}, f32[512]{0:T(512)}, u32[]{:S(2)}) copy-start(f32[512]{0:T(512)} %param.21) | copy-start | bytes 6148
  66.9 1.3 %copy-start.2 = (bf16[2048,512]{1,0:T(8,128)(2,1)}, bf16[2048,512]{1,0:T(8,128)(2,1)S(1)}, u32[]{:S(2)}) copy-start(bf16[2048,512]{1,0:T(8,128)(2,1)S(1)} %get-tuple-element.13.w_down) | copy-start | bytes 6291460
  68.3 15.6 %all-to-all-start.1 = ((bf16[128,8,128]{2,1,0:T(8,128)(2,1)}), bf16[128,8,128]{2,1,0:T(8,128)(2,1)S(1)}, u32[]{:S(2)}, u32[]{:S(2)}) async-start(bf16[128,8,128]{2,1,0:T(8,128)(2,1)} %get-tuple-element.12), calls=%async_computation.1 | async-start | bytes 524288 | tf_op jit(solution)/shard_map/all_to_all | solution.py:578
  83.9 1.6 %copy-start.3 = (bf16[2048,512]{1,0:T(8,128)(2,1)S(1)}, bf16[2048,512]{1,0:T(8,128)(2,1)}, u32[]{:S(2)}) copy-start(bf16[2048,512]{1,0:T(8,128)(2,1)} %copy-done.2) | copy-start | bytes 6291460

commit v4 on v3

--- a/solution.py
+++ b/solution.py
@@ -320,9 +320,7 @@
     out_copy.wait()
 
 
-def attend_kernel(received_ref, w_down_hbm, out_ref, w_down_ref, queries, partial, w_sem):
-    w_copy = pltpu.make_async_copy(w_down_hbm, w_down_ref, w_sem)
-    w_copy.start()
+def attend_kernel(received_ref, out_ref, queries, partial):
     device = lax.axis_index("row") * 16 + lax.axis_index("col")
     quarter = lax.rem(device // 4, 4)
     g = lax.rem(device, 4)
@@ -361,10 +359,13 @@
                 base = (r * 4 + oh) * 32 + dl * 2
                 rows = [partial[pl.ds(base + k, 4, stride=8)] for k in range(2)]
                 out_ref[r * 16 + dh * 4 + dl] = jnp.concatenate(rows, axis=0).astype(BF16)
-    w_copy.wait()
-
-
-def agent_kernel(returned_ref, live_ref, gain_ref, w_out, w_up, w_down, out_ref):
+
+
+def agent_kernel(
+    returned_ref, live_ref, gain_ref, w_out, w_up, w_down_hbm, out_ref, w_down, w_sem
+):
+    w_copy = pltpu.make_async_copy(w_down_hbm, w_down, w_sem)
+    w_copy.start()
     lane = iota((32, CH), 1)
     lower = lane < HEAD_DIM
     everything = returned_ref[...].astype(F32)
@@ -395,6 +396,7 @@
     power = jnp.mean(after * after, axis=1, keepdims=True)
     normed = (after * lax.rsqrt(power + EPS) * gain_ref[...]).astype(BF16)
     activated = jax.nn.gelu(dot(normed, w_up[...])).astype(BF16)
+    w_copy.wait()
     result = (after + dot(activated, w_down[...])).astype(BF16)
     dh = lax.axis_index("col") // 4
     slot = iota((32, 32), 0)
@@ -489,35 +491,29 @@
     )
 
 
-def attend(received, w_down):
+def attend(received):
     return pl.pallas_call(
         attend_kernel,
-        out_shape=(
-            jax.ShapeDtypeStruct((128, 8, CH), BF16),
-            jax.ShapeDtypeStruct(w_down.shape, BF16),
-        ),
-        in_specs=[VMEM, HBM],
-        out_specs=(VMEM, VMEM),
-        scratch_shapes=[
-            pltpu.VMEM((1024, CH), F32),
-            pltpu.VMEM((1024, CH), F32),
-            pltpu.SemaphoreType.DMA,
-        ],
+        out_shape=jax.ShapeDtypeStruct((128, 8, CH), BF16),
+        in_specs=[VMEM],
+        out_specs=VMEM,
+        scratch_shapes=[pltpu.VMEM((1024, CH), F32), pltpu.VMEM((1024, CH), F32)],
         compiler_params=pltpu.CompilerParams(vmem_limit_bytes=24 * 2**20),
         cost_estimate=pl.CostEstimate(
-            flops=10**9, bytes_accessed=10**6, transcendentals=2 * 10**6
+            flops=10**10, bytes_accessed=10**6, transcendentals=2 * 10**6
         ),
         name="attend",
-    )(received, w_down)
+    )(received)
 
 
 def finish(returned, live, gain, w_out, w_up, w_down):
     return pl.pallas_call(
         agent_kernel,
         out_shape=jax.ShapeDtypeStruct((32, 512), BF16),
-        in_specs=[VMEM] * 6,
+        in_specs=[VMEM] * 5 + [HBM],
         out_specs=VMEM,
-        compiler_params=pltpu.CompilerParams(vmem_limit_bytes=24 * 2**20),
+        scratch_shapes=[pltpu.VMEM(w_down.shape, BF16), pltpu.SemaphoreType.DMA],
+        compiler_params=pltpu.CompilerParams(vmem_limit_bytes=50 * 2**20),
         name="agents",
     )(returned, live, gain, w_out, w_up, w_down)
 
@@ -574,8 +570,7 @@
         w_qkv,
     )
     received = lax.all_to_all(payload, ("row", "col"), 0, 0, tiled=True)
-    partial, w_down = attend(received, w_down)
-    returned = lax.all_to_all(partial, ("row", "col"), 0, 0, tiled=True)
+    returned = lax.all_to_all(attend(received), ("row", "col"), 0, 0, tiled=True)
     live = agent_live.astype(F32)[:, None]
     agent_out = finish(returned, live, gain_mlp[None], w_out, w_up, w_down)
     return (features, agent_out)

time: 87.8 us -> 86.4 us (0.984)
  local copies, waits for them, and re-layouts: 3.38 us -> 0.46 us
  Pallas kernels: 22.7 us -> 24.1 us
    unnamed x34 -> x28, local copies, waits for them, and re-layouts: 3.02 us -> 0.1 us
    pallas_call x1, Pallas kernels: 1.99 us -> 3.57 us  [finish(): pl.pallas_call(agent_kernel, out_shape=jax.ShapeDtypeStruct((32, 512), BF...]
  transfers between devices with their start and end apart: 5 -> 5, of which waited for: 4 -> 4; matrix products, arithmetic and copies ran while one was open for 0% -> 0% of each run, Pallas kernels for 5% -> 6%
where the time goes in v4:
time: 86.4 us; the launch traced here: 86.1 us
  blocking collectives  25.1 us (29%)
  Pallas kernels  24.1 us (28%)
  starting transfers between devices  18.9 us (22%)
  waiting for transfers between devices  16.3 us (19%)
  between operations  1.09 us (1%)
    all_to_all x1, blocking collectives, per_device(): received = lax.all_to_all(payload, ('row', 'col'), 0, 0, tiled=True)  25.1 us
    pallas_call x1, Pallas kernels, scene(): pl.pallas_call(scene_kernel, out_shape=(jax.ShapeDtypeStruct((ROWS, COLS,...  11.5 us
    all_to_all x1, waiting for transfers between devices, per_device(): lax.all_to_all(attend(received), ('row', 'col'), 0, 0, tiled=True)  11 us
    ppermute x1, starting transfers between devices, per_device(): above = plain(lax.ppermute(bottom, 'row', forward(8)))  6.28 us
    pallas_call x1, Pallas kernels, first_layer(): pl.pallas_call(first_kernel, out_shape=jax.ShapeDtypeStruct((2 * PAIRS_1,...  4.77 us
    all_to_all x1, starting transfers between devices, per_device(): lax.all_to_all(attend(received), ('row', 'col'), 0, 0, tiled=True)  4.51 us
    pallas_call x1, Pallas kernels, finish(): pl.pallas_call(agent_kernel, out_shape=jax.ShapeDtypeStruct((32, 512), BF...  3.57 us
    ppermute x1, starting transfers between devices, per_device(): right = plain(lax.ppermute(plain(initial), 'col', backward(16)))  3.54 us
  transfers between devices with their start and end apart: 5, of which 4 were waited for; matrix products, arithmetic and copies ran while one was open for 0% of the time, Pallas kernels for 6%

profile of v4, /device:TPU:1, one launch (start us, length us, event | category | flops | bytes accessed | tf_op | source)
XLA Modules:
  0.0 86.1 jit_solution(3006635205490721654)
XLA Ops:
  0.6 0.0 copy-start
  0.6 0.0 slice-start
  0.6 0.0 copy-start.10
  0.7 1.8 %row_slices.1 = (bf16[17,64,128]{2,1,0:T(8,128)(2,1)}, bf16[2,64,128]{2,1,0:T(8,128)(2,1)}) custom-call(bf16[128,64,128]{2,1,0:T(8,128)(2,1)} %raster_ref.3), custom_call_target="tpu_custom_call" | custom-call | tf_op jit(solution)/shard_map/row_slices/pallas_call | solution.py:416
  2.5 0.0 copy-start.6
  2.5 1.4 %collective-permute-start.1 = (bf16[17,64,128]{2,1,0:T(8,128)(2,1)}, bf16[17,64,128]{2,1,0:T(8,128)(2,1)S(1)}, u32[]{:S(2)}, u32[]{:S(2)}) collective-permute-start(bf16[17,64,128]{2,1,0:T(8,128)(2,1)} %get-tuple-element.7), channel_id=1, source_target_pairs={{16,0},{32,16},{48,32},{64,48},{80,64},{96,80},{112,96},{17,1},{33... | collective-permute-start | bytes 835592 | tf_op jit(solution)/shard_map/ppermute | solution.py:545
  3.9 6.3 %collective-permute-start = (bf16[2,64,128]{2,1,0:T(8,128)(2,1)}, bf16[2,64,128]{2,1,0:T(8,128)(2,1)S(1)}, u32[]{:S(2)}, u32[]{:S(2)}) collective-permute-start(bf16[2,64,128]{2,1,0:T(8,128)(2,1)} %get-tuple-element.6), channel_id=1, source_target_pairs={{0,16},{16,32},{32,48},{48,64},{64,80},{80,96},{96,112},{1,17},{17... | collective-permute-start | bytes 98312 | tf_op jit(solution)/shard_map/ppermute | solution.py:546
  10.2 0.0 copy-done
  10.2 0.1 slice.34
  10.3 0.1 slice.28
  10.4 1.1 %collective-permute-done.above_ref = bf16[2,64,128]{2,1,0:T(8,128)(2,1)S(1)} collective-permute-done((bf16[2,64,128]{2,1,0:T(8,128)(2,1)}, bf16[2,64,128]{2,1,0:T(8,128)(2,1)S(1)}, u32[]{:S(2)}, u32[]{:S(2)}) %collective-permute-start) | collective-permute-done | bytes 32800 | tf_op jit(solution)/shard_map/ppermute | solution.py:546
  11.6 3.0 %collective-permute-done.1.below_ref = bf16[17,64,128]{2,1,0:T(8,128)(2,1)S(1)} collective-permute-done((bf16[17,64,128]{2,1,0:T(8,128)(2,1)}, bf16[17,64,128]{2,1,0:T(8,128)(2,1)S(1)}, u32[]{:S(2)}, u32[]{:S(2)}) %collective-permute-start.1) | collective-permute-done | bytes 278560 | tf_op jit(solution)/shard_map/ppermute | solution.py:545
  14.7 0.0 slice-done
  14.7 0.1 pad_maximum_fusion
  14.8 3.5 %collective-permute-start.3 = (bf16[157,16,128]{2,1,0:T(8,128)(2,1)S(1)}, bf16[157,16,128]{2,1,0:T(8,128)(2,1)S(1)}, u32[]{:S(2)}, u32[]{:S(2)}) collective-permute-start(bf16[157,16,128]{2,1,0:T(8,128)(2,1)S(1)} %pad_maximum_fusion), channel_id=1, source_target_pairs={{1,0},{2,1},{3,2},{4,3},{5,4},{6,5},{7,6},{8,7},{9,8},{10,9},{11,1... | collective-permute-start | bytes 1929224 | tf_op jit(solution)/shard_map/ppermute | solution.py:552
  18.4 0.0 copy-done.10
  18.4 0.1 pad.9.flags_ref
  18.5 3.1 %collective-permute-start.2 = (bf16[2,147,128]{2,1,0:T(8,128)(2,1)S(1)}, bf16[2,147,128]{2,1,0:T(8,128)(2,1)S(1)}, u32[]{:S(2)}, u32[]{:S(2)}) collective-permute-start(bf16[2,147,128]{2,1,0:T(8,128)(2,1)S(1)} %pad_maximum_fusion.1), channel_id=1, source_target_pairs={{0,1},{1,2},{2,3},{3,4},{4,5},{5,6},{6,7},{7,8},{8,9},{9,10},{10,1... | collective-permute-start | bytes 225800 | tf_op jit(solution)/shard_map/ppermute | solution.py:553
  21.6 0.0 copy-done.6
  21.7 0.0 copy-start.4
  21.7 0.0 copy-start.5
  21.7 0.0 copy-start.7
  21.7 0.0 copy-start.8
  21.7 0.0 copy-start.9
  21.7 4.8 %first_layer.1.inner_ref = bf16[152,64,128]{2,1,0:T(8,128)(2,1)S(1)} custom-call(bf16[128,64,128]{2,1,0:T(8,128)(2,1)S(1)} %copy-done, bf16[2,64,128]{2,1,0:T(8,128)(2,1)S(1)} %collective-permute-done.above_ref, bf16[17,64,128]{2,1,0:T(8,128)(2,1)S(1)} %collective-permute-done.1.below_ref, bf16[9,128,128]{2,1,0:T(8,128)(2,1)S(1)} %bitcast.28), custom_call_target="tpu_custom_call" | custom-call | flops 4000000000 | bytes 5000000 | tf_op jit(solution)/shard_map/first_layer/pallas_call | solution.py:430
  26.5 0.0 collective-permute-done.2.left_ref
  26.5 1.2 %collective-permute-done.3.right_ref = bf16[157,16,128]{2,1,0:T(8,128)(2,1)S(1)} collective-permute-done((bf16[157,16,128]{2,1,0:T(8,128)(2,1)S(1)}, bf16[157,16,128]{2,1,0:T(8,128)(2,1)S(1)}, u32[]{:S(2)}, u32[]{:S(2)}) %collective-permute-start.3) | collective-permute-done | bytes 643104 | tf_op jit(solution)/shard_map/ppermute | solution.py:552
  27.7 0.0 copy-done.4
  27.7 0.0 copy-done.5
  27.7 0.0 copy-done.7
  27.7 0.0 copy-done.8
  27.7 0.0 copy-done.9
  27.7 11.5 %scene.1 = (bf16[128,64,128]{2,1,0:T(8,128)(2,1)}, bf16[128,16,128]{2,1,0:T(8,128)(2,1)S(1)}) custom-call(s32[2,32]{1,0:T(2,128)S(1)} %copy-done.9, bf16[128,64,128]{2,1,0:T(8,128)(2,1)S(1)} %copy-done, bf16[2,64,128]{2,1,0:T(8,128)(2,1)S(1)} %collective-permute-done.above_ref, bf16[17,64,128]{2,1,0:T(8,128)(2,1)S(1)} %collective-permute-done.1.below_ref, ...), custom_call_target="tpu_custom_call" | custom-call | flops 10000000000 | bytes 10000000 | tf_op jit(solution)/shard_map/scene/pallas_call | solution.py:450
  39.2 25.1 %all_to_all.10.received_ref = bf16[128,16,128]{2,1,0:T(8,128)(2,1)S(1)} all-to-all(bf16[128,16,128]{2,1,0:T(8,128)(2,1)S(1)} %get-tuple-element.9), channel_id=1, replica_groups=mesh['row'=8,'col'=16] {'row','col'}, dimensions={0} | all-to-all | bytes 1048576 | tf_op jit(solution)/shard_map/all_to_all | solution.py:572
  64.3 0.0 copy-start.1
  64.3 0.0 copy-start.2
  64.3 0.0 copy-start.3
  64.3 2.4 %attend.1 = bf16[128,8,128]{2,1,0:T(8,128)(2,1)} custom-call(bf16[128,16,128]{2,1,0:T(8,128)(2,1)S(1)} %all_to_all.10.received_ref), custom_call_target="tpu_custom_call" | custom-call | flops 10000000000 | bytes 1000000 | tf_op jit(solution)/shard_map/attend/pallas_call | solution.py:495
  66.8 4.5 %all-to-all-start.1 = ((bf16[128,8,128]{2,1,0:T(8,128)(2,1)}), bf16[128,8,128]{2,1,0:T(8,128)(2,1)S(1)}, u32[]{:S(2)}, u32[]{:S(2)}) async-start(bf16[128,8,128]{2,1,0:T(8,128)(2,1)} %attend.1), calls=%async_computation.1 | async-start | bytes 524288 | tf_op jit(solution)/shard_map/all_to_all | solution.py:573
  71.3 0.1 copy.22.live_ref
  71.4 11.0 %all-to-all-done.1.returned_ref = bf16[128,8,128]{2,1,0:T(8,128)(2,1)S(1)} async-done(((bf16[128,8,128]{2,1,0:T(8,128)(2,1)}), bf16[128,8,128]{2,1,0:T(8,128)(2,1)S(1)}, u32[]{:S(2)}, u32[]{:S(2)}) %all-to-all-start.1) | async-done | bytes 262176 | tf_op jit(solution)/shard_map/all_to_all | solution.py:573
  82.4 0.0 copy-done.1
  82.4 0.0 copy-done.2
  82.4 0.0 copy-done.3
  82.4 3.6 %agents.1 = bf16[32,512]{1,0:T(8,128)(2,1)} custom-call(bf16[128,8,128]{2,1,0:T(8,128)(2,1)S(1)} %all-to-all-done.1.returned_ref, f32[32,1]{1,0:T(8,128)S(1)} %copy.22.live_ref, f32[1,512]{1,0:T(1,128)S(1)} %bitcast.27, bf16[512,512]{1,0:T(8,128)(2,1)S(1)} %copy-done.2, bf16[512,2048]{1,0:T(8,128)(2,1)S(1)} %copy-done.1, bf16[2048,512]{1,0:T(8,128)(2,1)} %w_down_hbm.1), custom_call_target="tpu_custom_call" | custom-call | tf_op jit(solution)/shard_map/agents/pallas_call | solution.py:510
  (15 shorter events, 0.1 us)
Async XLA Ops:
  0.6 9.6 %copy-start = (bf16[128,64,128]{2,1,0:T(8,128)(2,1)S(1)}, bf16[128,64,128]{2,1,0:T(8,128)(2,1)}, u32[]{:S(2)}) copy-start(bf16[128,64,128]{2,1,0:T(8,128)(2,1)} %raster_ref.3) | copy-start | bytes 6291460
  0.6 14.0 %slice-start = ((bf16[128,64,128]{2,1,0:T(8,128)(2,1)}), bf16[128,16,128]{2,1,0:T(8,128)(2,1)S(1)}, s32[]{:S(2)}) async-start(bf16[128,64,128]{2,1,0:T(8,128)(2,1)} %raster_ref.3), calls=%async_computation.2 | async-start | bytes 1048576 | tf_op jit(solution)/shard_map/slice | solution.py:551
  0.6 17.7 %copy-start.10 = (s32[32]{0:T(128)S(1)}, s32[32]{0:T(128)}, u32[]{:S(2)}) copy-start(s32[32]{0:T(128)} %param.16) | copy-start | bytes 388
  2.5 19.1 %copy-start.6 = (bf16[3,3,128,128]{3,2,1,0:T(8,128)(2,1)S(1)}, bf16[3,3,128,128]{3,2,1,0:T(8,128)(2,1)}, u32[]{:S(2)}) copy-start(bf16[3,3,128,128]{3,2,1,0:T(8,128)(2,1)} %param.13) | copy-start | bytes 884740
  2.5 12.1 %collective-permute-start.1 = (bf16[17,64,128]{2,1,0:T(8,128)(2,1)}, bf16[17,64,128]{2,1,0:T(8,128)(2,1)S(1)}, u32[]{:S(2)}, u32[]{:S(2)}) collective-permute-start(bf16[17,64,128]{2,1,0:T(8,128)(2,1)} %get-tuple-element.7), channel_id=1, source_target_pairs={{16,0},{32,16},{48,32},{64,48},{80,64},{96,80},{112,96},{17,1},{33... | collective-permute-start | bytes 835592 | tf_op jit(solution)/shard_map/ppermute | solution.py:545
  3.9 7.6 %collective-permute-start = (bf16[2,64,128]{2,1,0:T(8,128)(2,1)}, bf16[2,64,128]{2,1,0:T(8,128)(2,1)S(1)}, u32[]{:S(2)}, u32[]{:S(2)}) collective-permute-start(bf16[2,64,128]{2,1,0:T(8,128)(2,1)} %get-tuple-element.6), channel_id=1, source_target_pairs={{0,16},{16,32},{32,48},{48,64},{64,80},{80,96},{96,112},{1,17},{17... | collective-permute-start | bytes 98312 | tf_op jit(solution)/shard_map/ppermute | solution.py:546
  14.8 12.9 %collective-permute-start.3 = (bf16[157,16,128]{2,1,0:T(8,128)(2,1)S(1)}, bf16[157,16,128]{2,1,0:T(8,128)(2,1)S(1)}, u32[]{:S(2)}, u32[]{:S(2)}) collective-permute-start(bf16[157,16,128]{2,1,0:T(8,128)(2,1)S(1)} %pad_maximum_fusion), channel_id=1, source_target_pairs={{1,0},{2,1},{3,2},{4,3},{5,4},{6,5},{7,6},{8,7},{9,8},{10,9},{11,1... | collective-permute-start | bytes 1929224 | tf_op jit(solution)/shard_map/ppermute | solution.py:552
  18.5 8.0 %collective-permute-start.2 = (bf16[2,147,128]{2,1,0:T(8,128)(2,1)S(1)}, bf16[2,147,128]{2,1,0:T(8,128)(2,1)S(1)}, u32[]{:S(2)}, u32[]{:S(2)}) collective-permute-start(bf16[2,147,128]{2,1,0:T(8,128)(2,1)S(1)} %pad_maximum_fusion.1), channel_id=1, source_target_pairs={{0,1},{1,2},{2,3},{3,4},{4,5},{5,6},{6,7},{7,8},{8,9},{9,10},{10,1... | collective-permute-start | bytes 225800 | tf_op jit(solution)/shard_map/ppermute | solution.py:553
  21.7 6.0 %copy-start.4 = (bf16[2048,512]{1,0:T(8,128)(2,1)S(1)}, bf16[2048,512]{1,0:T(8,128)(2,1)}, u32[]{:S(2)}) copy-start(bf16[2048,512]{1,0:T(8,128)(2,1)} %w_embed.1) | copy-start | bytes 6291460
  21.7 6.0 %copy-start.5 = (bf16[512,1536]{1,0:T(8,128)(2,1)S(1)}, bf16[512,1536]{1,0:T(8,128)(2,1)}, u32[]{:S(2)}) copy-start(bf16[512,1536]{1,0:T(8,128)(2,1)} %w_qkv.1) | copy-start | bytes 4718596
  21.7 6.0 %copy-start.7 = (bf16[3,3,128,128]{3,2,1,0:T(8,128)(2,1)S(1)}, bf16[3,3,128,128]{3,2,1,0:T(8,128)(2,1)}, u32[]{:S(2)}) copy-start(bf16[3,3,128,128]{3,2,1,0:T(8,128)(2,1)} %param.14) | copy-start | bytes 884740
  21.7 6.0 %copy-start.8 = (f32[512]{0:T(512)S(1)}, f32[512]{0:T(512)}, u32[]{:S(2)}) copy-start(f32[512]{0:T(512)} %param.18) | copy-start | bytes 6148
  21.7 6.0 %copy-start.9 = (s32[2,32]{1,0:T(2,128)S(1)}, s32[2,32]{1,0:T(2,128)}, u32[]{:S(2)}) copy-start(s32[2,32]{1,0:T(2,128)} %anchor_ref.1) | copy-start | bytes 772
  64.3 18.1 %copy-start.1 = (bf16[512,2048]{1,0:T(8,128)(2,1)S(1)}, bf16[512,2048]{1,0:T(8,128)(2,1)}, u32[]{:S(2)}) copy-start(bf16[512,2048]{1,0:T(8,128)(2,1)} %w_up.1) | copy-start | bytes 6291460
  64.3 18.1 %copy-start.2 = (bf16[512,512]{1,0:T(8,128)(2,1)S(1)}, bf16[512,512]{1,0:T(8,128)(2,1)}, u32[]{:S(2)}) copy-start(bf16[512,512]{1,0:T(8,128)(2,1)} %w_out.1) | copy-start | bytes 1572868
  64.3 18.1 %copy-start.3 = (f32[512]{0:T(512)S(1)}, f32[512]{0:T(512)}, u32[]{:S(2)}) copy-start(f32[512]{0:T(512)} %param.21) | copy-start | bytes 6148
  66.8 15.6 %all-to-all-start.1 = ((bf16[128,8,128]{2,1,0:T(8,128)(2,1)}), bf16[128,8,128]{2,1,0:T(8,128)(2,1)S(1)}, u32[]{:S(2)}, u32[]{:S(2)}) async-start(bf16[128,8,128]{2,1,0:T(8,128)(2,1)} %attend.1), calls=%async_computation.1 | async-start | bytes 524288 | tf_op jit(solution)/shard_map/all_to_all | solution.py:573

commit v5 on v4

--- a/solution.py
+++ b/solution.py
@@ -20,6 +20,7 @@
 SLOTS = 77
 NB1, NB2 = 19, 18
 WIDE = 80
+TOGETHER = 4
 STRIP = 32
 TAPS = ((0, 0), (0, 2), (1, 0), (1, 2), (0, 1), (1, 1))
 F32, BF16 = jnp.float32, jnp.bfloat16
@@ -164,7 +165,6 @@
     col_id = lax.axis_index("col")
     center = (above_ref, raster_ref, below_ref)
     band(conv1_ref, band_1)
-    band(conv2_ref, band_2)
     for u in range(2 * SLOTS):
         edge_wide[u * 64 + 48 : u * 64 + 56] = jnp.zeros((8, CH), F32)
     for c in range(NEAR):
@@ -242,6 +242,8 @@
     edges(0, buffers[0])
     for block in range(blocks):
         edge_multiply(block, buffers[block % 2])
+        if block == 0:
+            band(conv2_ref, band_2)
         if block + 1 < blocks:
             edges(block + 1, buffers[(block + 1) % 2])
     blocks = PAIRS_2 // NB2
@@ -254,20 +256,24 @@
     out_copy = pltpu.make_async_copy(out_features.at[pl.ds(0, ROWS)], features_hbm, out_sem)
     out_copy.start()
 
-    def crop(agent, _):
-        top = anchor_ref[0, agent] - row_id * ROWS
-        left = anchor_ref[1, agent] - col_id * COLS
-        for rb in range(4):
-            start = (top + rb * 4) * WIDE + left
-            four = [wide_features[pl.ds(start + i * WIDE, CROP)] for i in range(4)]
-            block_sum[rb] = (four[0] + four[1]) + (four[2] + four[3])
-        for rb in range(4):
-            cells = [block_sum[rb, pl.ds(k, 4, stride=4)] for k in range(4)]
-            mean = ((cells[0] + cells[1]) + (cells[2] + cells[3])) * (1.0 / 16)
-            pooled[pl.ds(rb * 4 * 32 + agent, 4, stride=32)] = mean
+    def crop(group, _):
+        for sub in range(TOGETHER):
+            agent = group * TOGETHER + sub
+            top = anchor_ref[0, agent] - row_id * ROWS
+            left = anchor_ref[1, agent] - col_id * COLS
+            for rb in range(4):
+                start = (top + rb * 4) * WIDE + left
+                four = [wide_features[pl.ds(start + i * WIDE, CROP)] for i in range(4)]
+                block_sum[sub * 4 + rb] = (four[0] + four[1]) + (four[2] + four[3])
+        for sub in range(TOGETHER):
+            agent = group * TOGETHER + sub
+            for rb in range(4):
+                cells = [block_sum[sub * 4 + rb, pl.ds(k, 4, stride=4)] for k in range(4)]
+                mean = ((cells[0] + cells[1]) + (cells[2] + cells[3])) * (1.0 / 16)
+                pooled[pl.ds(rb * 4 * 32 + agent, 4, stride=32)] = mean
         return _
 
-    lax.fori_loop(0, 32, crop, 0)
+    lax.fori_loop(0, 32 // TOGETHER, crop, 0)
     agents = jnp.concatenate(
         [pooled[b * 32 : (b + 1) * 32].astype(BF16) for b in range(16)], axis=1
     )
@@ -288,6 +294,16 @@
     def turned(x):
         return pltpu.roll(x, HEAD_DIM, 1)
 
+    odd = lax.rem(lane_id // 16, 2) == 1
+    flags = jnp.broadcast_to(flags_ref[...], (32, CH))
+    flags = flags + pltpu.roll(flags, CH - 32, 1)
+    extras = []
+    for group in range(4):
+        source = embedded[:, group * CH : (group + 1) * CH]
+        high = source.astype(BF16).astype(F32)
+        low = source - high
+        low = jnp.where(odd, pltpu.roll(low, 16, 1), pltpu.roll(low, CH - 16, 1))
+        extras.append(((turned(high), turned(low)), (high, low)))
     shift = lax.rem(col_id // 4, 4)
     for pair in range(4):
         q_two = unit(projected[:, pair * CH : (pair + 1) * CH])
@@ -302,14 +318,10 @@
             kv = jnp.where(lower, k_h, v_h)
             for kp in range(4):
                 chunk = h * 4 + kp
-                source = embedded[:, (chunk // 8) * CH : (chunk // 8 + 1) * CH]
-                offset = (chunk % 8) * 16
-                piece = pltpu.roll(source, (HEAD_DIM - offset) % CH, 1)
-                high = piece.astype(BF16).astype(F32)
-                low = pltpu.roll(piece - high, 16, 1)
-                extra = jnp.where(
-                    lane_id < 80, high, jnp.where(lane_id < 96, low, flags_ref[...])
-                )
+                high, low = extras[chunk // 8][chunk % 8 // 4]
+                place = lane_id // 16
+                at = 4 + chunk % 4
+                extra = jnp.where(place == at, high, jnp.where(place == at ^ 1, low, flags))
                 row = jnp.where(lower, q_h, extra)
                 for gg in range(4):
                     g = lax.rem(gg + shift, 4)
@@ -333,7 +345,8 @@
     lane = iota((1024, CH), 1)
     source = (key // 128) * 16 + quarter * 4 + lax.rem(key // 2, 4)
     chosen = dot((lane == source).astype(F32).astype(BF16), flags)
-    wanted = 96 + lax.rem(key // 8, 16) * 2 + lax.rem(key, 2)
+    first_flag = jnp.where(lax.rem(device // 4, 4) < 2, 96, 64)
+    wanted = first_flag + lax.rem(key // 8, 16) * 2 + lax.rem(key, 2)
     alone = jnp.where(lane == wanted, chosen, 0.0).astype(BF16)
     mask = dot(alone, jnp.ones((CH, CH), BF16))
     lower = lane < HEAD_DIM
@@ -342,6 +355,8 @@
     factor = SCORE_SCALE / HEAD_DIM**0.5
     step = 256
     lane_s = iota((step, CH), 1)
+    plain = (lane_s < first_flag) | (lane_s >= first_flag + 32)
+    rounded = lane_s < first_flag + 16
     for i in range(1024 // step):
         q = queries[i * step : (i + 1) * step]
         weights = jnp.exp(dot_t(q.astype(BF16), keys) * factor).astype(BF16)
@@ -350,7 +365,7 @@
         partial[i * step : (i + 1) * step] = jnp.where(
             lane_s < HEAD_DIM,
             summed,
-            jnp.where(lane_s < 96, q, jnp.where(lane_s < 112, high, summed - high)),
+            jnp.where(plain, q, jnp.where(rounded, high, summed - high)),
         )
     for r in range(8):
         for oh in range(4):
@@ -364,8 +379,14 @@
 def agent_kernel(
     returned_ref, live_ref, gain_ref, w_out, w_up, w_down_hbm, out_ref, w_down, w_sem
 ):
-    w_copy = pltpu.make_async_copy(w_down_hbm, w_down, w_sem)
-    w_copy.start()
+    quarter = w_down.shape[0] // 4
+    parts = [pl.ds(i * quarter, quarter) for i in range(4)]
+    w_copies = [
+        pltpu.make_async_copy(w_down_hbm.at[part], w_down.at[part], w_sem.at[i])
+        for i, part in enumerate(parts)
+    ]
+    for w_copy in w_copies:
+        w_copy.start()
     lane = iota((32, CH), 1)
     lower = lane < HEAD_DIM
     everything = returned_ref[...].astype(F32)
@@ -373,19 +394,21 @@
     embedded = []
     chunk_sum = None
     for h in range(HEADS):
-        total = None
+        halves = [0.0, 0.0]
         for kp in range(4):
             chunk = h * 4 + kp
             block = everything[chunk * 4 : chunk * 4 + 4].reshape(32, CH)
-            total = block if total is None else total + block
-            whole = block + pltpu.roll(block, CH - 16, 1)
-            placed = pltpu.roll(whole, (chunk % 8 * 16 - HEAD_DIM) % CH, 1)
+            halves[kp // 2] += block
+            placed = block + pltpu.roll(block, 16 if chunk % 2 else CH - 16, 1)
+            if chunk % 8 < 4:
+                placed = pltpu.roll(placed, HEAD_DIM, 1)
             here = (lane // 16) == chunk % 8
             chunk_sum = jnp.where(here, placed, 0.0 if chunk % 8 == 0 else chunk_sum)
             if chunk % 8 == 7:
                 embedded.append(chunk_sum)
-        below = jnp.sum(jnp.where((lane == 96) | (lane == 112), total, 0.0), axis=1, keepdims=True)
-        ratio = total / below
+        parts = jnp.where((lane == 96) | (lane == 112), halves[0], 0.0)
+        parts += jnp.where((lane == 64) | (lane == 80), halves[1], 0.0)
+        ratio = (halves[0] + halves[1]) / jnp.sum(parts, axis=1, keepdims=True)
         if h % 2 == 0:
             even = ratio
         else:
@@ -396,7 +419,8 @@
     power = jnp.mean(after * after, axis=1, keepdims=True)
     normed = (after * lax.rsqrt(power + EPS) * gain_ref[...]).astype(BF16)
     activated = jax.nn.gelu(dot(normed, w_up[...])).astype(BF16)
-    w_copy.wait()
+    for w_copy in w_copies:
+        w_copy.wait()
     result = (after + dot(activated, w_down[...])).astype(BF16)
     dh = lax.axis_index("col") // 4
     slot = iota((32, 32), 0)
@@ -467,7 +491,7 @@
             pltpu.VMEM((2 * PAIRS_2, COLS, CH), BF16),
             pltpu.VMEM((12 * CH, 2 * CH), BF16),
             pltpu.VMEM((12 * CH, 2 * CH), BF16),
-            pltpu.VMEM((4, CROP, CH), F32),
+            pltpu.VMEM((4 * TOGETHER, CROP, CH), F32),
             pltpu.VMEM((16 * 32, CH), F32),
             pltpu.SemaphoreType.DMA,
         ],
@@ -512,7 +536,7 @@
         out_shape=jax.ShapeDtypeStruct((32, 512), BF16),
         in_specs=[VMEM] * 5 + [HBM],
         out_specs=VMEM,
-        scratch_shapes=[pltpu.VMEM(w_down.shape, BF16), pltpu.SemaphoreType.DMA],
+        scratch_shapes=[pltpu.VMEM(w_down.shape, BF16), pltpu.SemaphoreType.DMA((4,))],
         compiler_params=pltpu.CompilerParams(vmem_limit_bytes=50 * 2**20),
         name="agents",
     )(returned, live, gain, w_out, w_up, w_down)

time: 86.4 us -> 86.1 us (level)
  no operation moved by 1% of the time
where the time goes in v5:
time: 86.1 us; the launch traced here: 85.8 us
  blocking collectives  25.1 us (29%)
  Pallas kernels  23.8 us (28%)
  starting transfers between devices  18.9 us (22%)
  waiting for transfers between devices  16.3 us (19%)
  between operations  1.09 us (1%)
    all_to_all x1, blocking collectives, per_device(): received = lax.all_to_all(payload, ('row', 'col'), 0, 0, tiled=True)  25.1 us
    pallas_call x1, Pallas kernels, scene(): pl.pallas_call(scene_kernel, out_shape=(jax.ShapeDtypeStruct((ROWS, COLS,...  11.2 us
    all_to_all x1, waiting for transfers between devices, per_device(): lax.all_to_all(attend(received), ('row', 'col'), 0, 0, tiled=True)  11 us
    ppermute x1, starting transfers between devices, per_device(): above = plain(lax.ppermute(bottom, 'row', forward(8)))  6.28 us
    pallas_call x1, Pallas kernels, first_layer(): pl.pallas_call(first_kernel, out_shape=jax.ShapeDtypeStruct((2 * PAIRS_1,...  4.77 us
    all_to_all x1, starting transfers between devices, per_device(): lax.all_to_all(attend(received), ('row', 'col'), 0, 0, tiled=True)  4.51 us
    ppermute x1, starting transfers between devices, per_device(): right = plain(lax.ppermute(plain(initial), 'col', backward(16)))  3.54 us
    pallas_call x1, Pallas kernels, finish(): pl.pallas_call(agent_kernel, out_shape=jax.ShapeDtypeStruct((32, 512), BF...  3.52 us
  transfers between devices with their start and end apart: 5, of which 4 were waited for; matrix products, arithmetic and copies ran while one was open for 0% of the time, Pallas kernels for 6%

profile of v5, /device:TPU:1, one launch (start us, length us, event | category | flops | bytes accessed | tf_op | source)
XLA Modules:
  0.0 85.8 jit_solution(16220369387651012477)
XLA Ops:
  0.6 0.0 copy-start
  0.6 0.0 slice-start
  0.6 0.0 copy-start.10
  0.7 1.8 %row_slices.1 = (bf16[17,64,128]{2,1,0:T(8,128)(2,1)}, bf16[2,64,128]{2,1,0:T(8,128)(2,1)}) custom-call(bf16[128,64,128]{2,1,0:T(8,128)(2,1)} %raster_ref.3), custom_call_target="tpu_custom_call" | custom-call | tf_op jit(solution)/shard_map/row_slices/pallas_call | solution.py:440
  2.5 0.0 copy-start.6
  2.5 1.4 %collective-permute-start.1 = (bf16[17,64,128]{2,1,0:T(8,128)(2,1)}, bf16[17,64,128]{2,1,0:T(8,128)(2,1)S(1)}, u32[]{:S(2)}, u32[]{:S(2)}) collective-permute-start(bf16[17,64,128]{2,1,0:T(8,128)(2,1)} %get-tuple-element.7), channel_id=1, source_target_pairs={{16,0},{32,16},{48,32},{64,48},{80,64},{96,80},{112,96},{17,1},{33... | collective-permute-start | bytes 835592 | tf_op jit(solution)/shard_map/ppermute | solution.py:569
  3.9 6.3 %collective-permute-start = (bf16[2,64,128]{2,1,0:T(8,128)(2,1)}, bf16[2,64,128]{2,1,0:T(8,128)(2,1)S(1)}, u32[]{:S(2)}, u32[]{:S(2)}) collective-permute-start(bf16[2,64,128]{2,1,0:T(8,128)(2,1)} %get-tuple-element.6), channel_id=1, source_target_pairs={{0,16},{16,32},{32,48},{48,64},{64,80},{80,96},{96,112},{1,17},{17... | collective-permute-start | bytes 98312 | tf_op jit(solution)/shard_map/ppermute | solution.py:570
  10.2 0.0 copy-done
  10.2 0.1 slice.34
  10.3 0.1 slice.28
  10.4 1.1 %collective-permute-done.above_ref = bf16[2,64,128]{2,1,0:T(8,128)(2,1)S(1)} collective-permute-done((bf16[2,64,128]{2,1,0:T(8,128)(2,1)}, bf16[2,64,128]{2,1,0:T(8,128)(2,1)S(1)}, u32[]{:S(2)}, u32[]{:S(2)}) %collective-permute-start) | collective-permute-done | bytes 32800 | tf_op jit(solution)/shard_map/ppermute | solution.py:570
  11.6 3.0 %collective-permute-done.1.below_ref = bf16[17,64,128]{2,1,0:T(8,128)(2,1)S(1)} collective-permute-done((bf16[17,64,128]{2,1,0:T(8,128)(2,1)}, bf16[17,64,128]{2,1,0:T(8,128)(2,1)S(1)}, u32[]{:S(2)}, u32[]{:S(2)}) %collective-permute-start.1) | collective-permute-done | bytes 278560 | tf_op jit(solution)/shard_map/ppermute | solution.py:569
  14.7 0.0 slice-done
  14.7 0.1 pad_maximum_fusion
  14.8 3.5 %collective-permute-start.3 = (bf16[157,16,128]{2,1,0:T(8,128)(2,1)S(1)}, bf16[157,16,128]{2,1,0:T(8,128)(2,1)S(1)}, u32[]{:S(2)}, u32[]{:S(2)}) collective-permute-start(bf16[157,16,128]{2,1,0:T(8,128)(2,1)S(1)} %pad_maximum_fusion), channel_id=1, source_target_pairs={{1,0},{2,1},{3,2},{4,3},{5,4},{6,5},{7,6},{8,7},{9,8},{10,9},{11,1... | collective-permute-start | bytes 1929224 | tf_op jit(solution)/shard_map/ppermute | solution.py:576
  18.4 0.0 copy-done.10
  18.4 0.1 pad.9.flags_ref
  18.5 3.1 %collective-permute-start.2 = (bf16[2,147,128]{2,1,0:T(8,128)(2,1)S(1)}, bf16[2,147,128]{2,1,0:T(8,128)(2,1)S(1)}, u32[]{:S(2)}, u32[]{:S(2)}) collective-permute-start(bf16[2,147,128]{2,1,0:T(8,128)(2,1)S(1)} %pad_maximum_fusion.1), channel_id=1, source_target_pairs={{0,1},{1,2},{2,3},{3,4},{4,5},{5,6},{6,7},{7,8},{8,9},{9,10},{10,1... | collective-permute-start | bytes 225800 | tf_op jit(solution)/shard_map/ppermute | solution.py:577
  21.6 0.0 copy-done.6
  21.7 0.0 copy-start.4
  21.7 0.0 copy-start.5
  21.7 0.0 copy-start.7
  21.7 0.0 copy-start.8
  21.7 0.0 copy-start.9
  21.7 4.8 %first_layer.1.inner_ref = bf16[152,64,128]{2,1,0:T(8,128)(2,1)S(1)} custom-call(bf16[128,64,128]{2,1,0:T(8,128)(2,1)S(1)} %copy-done, bf16[2,64,128]{2,1,0:T(8,128)(2,1)S(1)} %collective-permute-done.above_ref, bf16[17,64,128]{2,1,0:T(8,128)(2,1)S(1)} %collective-permute-done.1.below_ref, bf16[9,128,128]{2,1,0:T(8,128)(2,1)S(1)} %bitcast.28), custom_call_target="tpu_custom_call" | custom-call | flops 4000000000 | bytes 5000000 | tf_op jit(solution)/shard_map/first_layer/pallas_call | solution.py:454
  26.5 0.0 collective-permute-done.2.left_ref
  26.5 1.2 %collective-permute-done.3.right_ref = bf16[157,16,128]{2,1,0:T(8,128)(2,1)S(1)} collective-permute-done((bf16[157,16,128]{2,1,0:T(8,128)(2,1)S(1)}, bf16[157,16,128]{2,1,0:T(8,128)(2,1)S(1)}, u32[]{:S(2)}, u32[]{:S(2)}) %collective-permute-start.3) | collective-permute-done | bytes 643104 | tf_op jit(solution)/shard_map/ppermute | solution.py:576
  27.7 0.0 copy-done.4
  27.7 0.0 copy-done.5
  27.7 0.0 copy-done.7
  27.7 0.0 copy-done.8
  27.7 0.0 copy-done.9
  27.7 11.2 %scene.1 = (bf16[128,64,128]{2,1,0:T(8,128)(2,1)}, bf16[128,16,128]{2,1,0:T(8,128)(2,1)S(1)}) custom-call(s32[2,32]{1,0:T(2,128)S(1)} %copy-done.9, bf16[128,64,128]{2,1,0:T(8,128)(2,1)S(1)} %copy-done, bf16[2,64,128]{2,1,0:T(8,128)(2,1)S(1)} %collective-permute-done.above_ref, bf16[17,64,128]{2,1,0:T(8,128)(2,1)S(1)} %collective-permute-done.1.below_ref, ...), custom_call_target="tpu_custom_call" | custom-call | flops 10000000000 | bytes 10000000 | tf_op jit(solution)/shard_map/scene/pallas_call | solution.py:474
  38.9 25.1 %all_to_all.10.received_ref = bf16[128,16,128]{2,1,0:T(8,128)(2,1)S(1)} all-to-all(bf16[128,16,128]{2,1,0:T(8,128)(2,1)S(1)} %get-tuple-element.9), channel_id=1, replica_groups=mesh['row'=8,'col'=16] {'row','col'}, dimensions={0} | all-to-all | bytes 1048576 | tf_op jit(solution)/shard_map/all_to_all | solution.py:596
  64.1 0.0 copy-start.1
  64.1 0.0 copy-start.2
  64.1 0.0 copy-start.3
  64.1 2.4 %attend.1 = bf16[128,8,128]{2,1,0:T(8,128)(2,1)} custom-call(bf16[128,16,128]{2,1,0:T(8,128)(2,1)S(1)} %all_to_all.10.received_ref), custom_call_target="tpu_custom_call" | custom-call | flops 10000000000 | bytes 1000000 | tf_op jit(solution)/shard_map/attend/pallas_call | solution.py:519
  66.5 4.5 %all-to-all-start.1 = ((bf16[128,8,128]{2,1,0:T(8,128)(2,1)}), bf16[128,8,128]{2,1,0:T(8,128)(2,1)S(1)}, u32[]{:S(2)}, u32[]{:S(2)}) async-start(bf16[128,8,128]{2,1,0:T(8,128)(2,1)} %attend.1), calls=%async_computation.1 | async-start | bytes 524288 | tf_op jit(solution)/shard_map/all_to_all | solution.py:597
  71.0 0.1 copy.22.live_ref
  71.1 11.0 %all-to-all-done.1.returned_ref = bf16[128,8,128]{2,1,0:T(8,128)(2,1)S(1)} async-done(((bf16[128,8,128]{2,1,0:T(8,128)(2,1)}), bf16[128,8,128]{2,1,0:T(8,128)(2,1)S(1)}, u32[]{:S(2)}, u32[]{:S(2)}) %all-to-all-start.1) | async-done | bytes 262176 | tf_op jit(solution)/shard_map/all_to_all | solution.py:597
  82.1 0.0 copy-done.1
  82.1 0.0 copy-done.2
  82.1 0.0 copy-done.3
  82.1 3.5 %agents.1 = bf16[32,512]{1,0:T(8,128)(2,1)} custom-call(bf16[128,8,128]{2,1,0:T(8,128)(2,1)S(1)} %all-to-all-done.1.returned_ref, f32[32,1]{1,0:T(8,128)S(1)} %copy.22.live_ref, f32[1,512]{1,0:T(1,128)S(1)} %bitcast.27, bf16[512,512]{1,0:T(8,128)(2,1)S(1)} %copy-done.2, bf16[512,2048]{1,0:T(8,128)(2,1)S(1)} %copy-done.1, bf16[2048,512]{1,0:T(8,128)(2,1)} %w_down_hbm.1), custom_call_target="tpu_custom_call" | custom-call | tf_op jit(solution)/shard_map/agents/pallas_call | solution.py:534
  (15 shorter events, 0.1 us)
Async XLA Ops:
  0.6 9.6 %copy-start = (bf16[128,64,128]{2,1,0:T(8,128)(2,1)S(1)}, bf16[128,64,128]{2,1,0:T(8,128)(2,1)}, u32[]{:S(2)}) copy-start(bf16[128,64,128]{2,1,0:T(8,128)(2,1)} %raster_ref.3) | copy-start | bytes 6291460
  0.6 14.0 %slice-start = ((bf16[128,64,128]{2,1,0:T(8,128)(2,1)}), bf16[128,16,128]{2,1,0:T(8,128)(2,1)S(1)}, s32[]{:S(2)}) async-start(bf16[128,64,128]{2,1,0:T(8,128)(2,1)} %raster_ref.3), calls=%async_computation.2 | async-start | bytes 1048576 | tf_op jit(solution)/shard_map/slice | solution.py:575
  0.6 17.7 %copy-start.10 = (s32[32]{0:T(128)S(1)}, s32[32]{0:T(128)}, u32[]{:S(2)}) copy-start(s32[32]{0:T(128)} %param.16) | copy-start | bytes 388
  2.5 19.1 %copy-start.6 = (bf16[3,3,128,128]{3,2,1,0:T(8,128)(2,1)S(1)}, bf16[3,3,128,128]{3,2,1,0:T(8,128)(2,1)}, u32[]{:S(2)}) copy-start(bf16[3,3,128,128]{3,2,1,0:T(8,128)(2,1)} %param.13) | copy-start | bytes 884740
  2.5 12.1 %collective-permute-start.1 = (bf16[17,64,128]{2,1,0:T(8,128)(2,1)}, bf16[17,64,128]{2,1,0:T(8,128)(2,1)S(1)}, u32[]{:S(2)}, u32[]{:S(2)}) collective-permute-start(bf16[17,64,128]{2,1,0:T(8,128)(2,1)} %get-tuple-element.7), channel_id=1, source_target_pairs={{16,0},{32,16},{48,32},{64,48},{80,64},{96,80},{112,96},{17,1},{33... | collective-permute-start | bytes 835592 | tf_op jit(solution)/shard_map/ppermute | solution.py:569
  3.9 7.6 %collective-permute-start = (bf16[2,64,128]{2,1,0:T(8,128)(2,1)}, bf16[2,64,128]{2,1,0:T(8,128)(2,1)S(1)}, u32[]{:S(2)}, u32[]{:S(2)}) collective-permute-start(bf16[2,64,128]{2,1,0:T(8,128)(2,1)} %get-tuple-element.6), channel_id=1, source_target_pairs={{0,16},{16,32},{32,48},{48,64},{64,80},{80,96},{96,112},{1,17},{17... | collective-permute-start | bytes 98312 | tf_op jit(solution)/shard_map/ppermute | solution.py:570
  14.8 12.9 %collective-permute-start.3 = (bf16[157,16,128]{2,1,0:T(8,128)(2,1)S(1)}, bf16[157,16,128]{2,1,0:T(8,128)(2,1)S(1)}, u32[]{:S(2)}, u32[]{:S(2)}) collective-permute-start(bf16[157,16,128]{2,1,0:T(8,128)(2,1)S(1)} %pad_maximum_fusion), channel_id=1, source_target_pairs={{1,0},{2,1},{3,2},{4,3},{5,4},{6,5},{7,6},{8,7},{9,8},{10,9},{11,1... | collective-permute-start | bytes 1929224 | tf_op jit(solution)/shard_map/ppermute | solution.py:576
  18.5 8.0 %collective-permute-start.2 = (bf16[2,147,128]{2,1,0:T(8,128)(2,1)S(1)}, bf16[2,147,128]{2,1,0:T(8,128)(2,1)S(1)}, u32[]{:S(2)}, u32[]{:S(2)}) collective-permute-start(bf16[2,147,128]{2,1,0:T(8,128)(2,1)S(1)} %pad_maximum_fusion.1), channel_id=1, source_target_pairs={{0,1},{1,2},{2,3},{3,4},{4,5},{5,6},{6,7},{7,8},{8,9},{9,10},{10,1... | collective-permute-start | bytes 225800 | tf_op jit(solution)/shard_map/ppermute | solution.py:577
  21.7 6.0 %copy-start.4 = (bf16[2048,512]{1,0:T(8,128)(2,1)S(1)}, bf16[2048,512]{1,0:T(8,128)(2,1)}, u32[]{:S(2)}) copy-start(bf16[2048,512]{1,0:T(8,128)(2,1)} %w_embed.1) | copy-start | bytes 6291460
  21.7 6.0 %copy-start.5 = (bf16[512,1536]{1,0:T(8,128)(2,1)S(1)}, bf16[512,1536]{1,0:T(8,128)(2,1)}, u32[]{:S(2)}) copy-start(bf16[512,1536]{1,0:T(8,128)(2,1)} %w_qkv.1) | copy-start | bytes 4718596
  21.7 6.0 %copy-start.7 = (bf16[3,3,128,128]{3,2,1,0:T(8,128)(2,1)S(1)}, bf16[3,3,128,128]{3,2,1,0:T(8,128)(2,1)}, u32[]{:S(2)}) copy-start(bf16[3,3,128,128]{3,2,1,0:T(8,128)(2,1)} %param.14) | copy-start | bytes 884740
  21.7 6.0 %copy-start.8 = (f32[512]{0:T(512)S(1)}, f32[512]{0:T(512)}, u32[]{:S(2)}) copy-start(f32[512]{0:T(512)} %param.18) | copy-start | bytes 6148
  21.7 6.0 %copy-start.9 = (s32[2,32]{1,0:T(2,128)S(1)}, s32[2,32]{1,0:T(2,128)}, u32[]{:S(2)}) copy-start(s32[2,32]{1,0:T(2,128)} %anchor_ref.1) | copy-start | bytes 772
  64.1 18.1 %copy-start.1 = (bf16[512,2048]{1,0:T(8,128)(2,1)S(1)}, bf16[512,2048]{1,0:T(8,128)(2,1)}, u32[]{:S(2)}) copy-start(bf16[512,2048]{1,0:T(8,128)(2,1)} %w_up.1) | copy-start | bytes 6291460
  64.1 18.1 %copy-start.2 = (bf16[512,512]{1,0:T(8,128)(2,1)S(1)}, bf16[512,512]{1,0:T(8,128)(2,1)}, u32[]{:S(2)}) copy-start(bf16[512,512]{1,0:T(8,128)(2,1)} %w_out.1) | copy-start | bytes 1572868
  64.1 18.1 %copy-start.3 = (f32[512]{0:T(512)S(1)}, f32[512]{0:T(512)}, u32[]{:S(2)}) copy-start(f32[512]{0:T(512)} %param.21) | copy-start | bytes 6148
  66.5 15.6 %all-to-all-start.1 = ((bf16[128,8,128]{2,1,0:T(8,128)(2,1)}), bf16[128,8,128]{2,1,0:T(8,128)(2,1)S(1)}, u32[]{:S(2)}, u32[]{:S(2)}) async-start(bf16[128,8,128]{2,1,0:T(8,128)(2,1)} %attend.1), calls=%async_computation.1 | async-start | bytes 524288 | tf_op jit(solution)/shard_map/all_to_all | solution.py:597

commit v6 on v5

--- a/solution.py
+++ b/solution.py
@@ -380,10 +380,10 @@
     returned_ref, live_ref, gain_ref, w_out, w_up, w_down_hbm, out_ref, w_down, w_sem
 ):
     quarter = w_down.shape[0] // 4
-    parts = [pl.ds(i * quarter, quarter) for i in range(4)]
+    quarters = [pl.ds(i * quarter, quarter) for i in range(4)]
     w_copies = [
         pltpu.make_async_copy(w_down_hbm.at[part], w_down.at[part], w_sem.at[i])
-        for i, part in enumerate(parts)
+        for i, part in enumerate(quarters)
     ]
     for w_copy in w_copies:
         w_copy.start()
@@ -419,9 +419,10 @@
     power = jnp.mean(after * after, axis=1, keepdims=True)
     normed = (after * lax.rsqrt(power + EPS) * gain_ref[...]).astype(BF16)
     activated = jax.nn.gelu(dot(normed, w_up[...])).astype(BF16)
-    for w_copy in w_copies:
+    for i, w_copy in enumerate(w_copies):
         w_copy.wait()
-    result = (after + dot(activated, w_down[...])).astype(BF16)
+        after = after + dot(activated[:, i * quarter : (i + 1) * quarter], w_down[quarters[i]])
+    result = after.astype(BF16)
     dh = lax.axis_index("col") // 4
     slot = iota((32, 32), 0)
     at = iota((32, 32), 1)

time: 86.1 us -> 85.9 us (level)
  no operation moved by 1% of the time
where the time goes in v6:
time: 85.9 us; the launch traced here: 85.6 us
  blocking collectives  25.1 us (29%)
  Pallas kernels  23.5 us (27%)
  starting transfers between devices  18.8 us (22%)
  waiting for transfers between devices  16.3 us (19%)
  between operations  1.09 us (1%)
    all_to_all x1, blocking collectives, per_device(): received = lax.all_to_all(payload, ('row', 'col'), 0, 0, tiled=True)  25.1 us
    pallas_call x1, Pallas kernels, scene(): pl.pallas_call(scene_kernel, out_shape=(jax.ShapeDtypeStruct((ROWS, COLS,...  11.2 us
    all_to_all x1, waiting for transfers between devices, per_device(): lax.all_to_all(attend(received), ('row', 'col'), 0, 0, tiled=True)  11 us
    ppermute x1, starting transfers between devices, per_device(): above = plain(lax.ppermute(bottom, 'row', forward(8)))  6.28 us
    pallas_call x1, Pallas kernels, first_layer(): pl.pallas_call(first_kernel, out_shape=jax.ShapeDtypeStruct((2 * PAIRS_1,...  4.77 us
    all_to_all x1, starting transfers between devices, per_device(): lax.all_to_all(attend(received), ('row', 'col'), 0, 0, tiled=True)  4.51 us
    ppermute x1, starting transfers between devices, per_device(): right = plain(lax.ppermute(plain(initial), 'col', backward(16)))  3.54 us
    pallas_call x1, Pallas kernels, finish(): pl.pallas_call(agent_kernel, out_shape=jax.ShapeDtypeStruct((32, 512), BF...  3.25 us
  transfers between devices with their start and end apart: 5, of which 4 were waited for; matrix products, arithmetic and copies ran while one was open for 0% of the time, Pallas kernels for 6%

profile of v6, /device:TPU:1, one launch (start us, length us, event | category | flops | bytes accessed | tf_op | source)
XLA Modules:
  0.0 85.6 jit_solution(9327767627644934148)
XLA Ops:
  0.6 0.0 copy-start
  0.6 0.0 slice-start
  0.6 0.0 copy-start.10
  0.7 1.8 %row_slices.1 = (bf16[17,64,128]{2,1,0:T(8,128)(2,1)}, bf16[2,64,128]{2,1,0:T(8,128)(2,1)}) custom-call(bf16[128,64,128]{2,1,0:T(8,128)(2,1)} %raster_ref.3), custom_call_target="tpu_custom_call" | custom-call | tf_op jit(solution)/shard_map/row_slices/pallas_call | solution.py:441
  2.5 0.0 copy-start.6
  2.5 1.4 %collective-permute-start.1 = (bf16[17,64,128]{2,1,0:T(8,128)(2,1)}, bf16[17,64,128]{2,1,0:T(8,128)(2,1)S(1)}, u32[]{:S(2)}, u32[]{:S(2)}) collective-permute-start(bf16[17,64,128]{2,1,0:T(8,128)(2,1)} %get-tuple-element.7), channel_id=1, source_target_pairs={{16,0},{32,16},{48,32},{64,48},{80,64},{96,80},{112,96},{17,1},{33... | collective-permute-start | bytes 835592 | tf_op jit(solution)/shard_map/ppermute | solution.py:570
  3.9 6.3 %collective-permute-start = (bf16[2,64,128]{2,1,0:T(8,128)(2,1)}, bf16[2,64,128]{2,1,0:T(8,128)(2,1)S(1)}, u32[]{:S(2)}, u32[]{:S(2)}) collective-permute-start(bf16[2,64,128]{2,1,0:T(8,128)(2,1)} %get-tuple-element.6), channel_id=1, source_target_pairs={{0,16},{16,32},{32,48},{48,64},{64,80},{80,96},{96,112},{1,17},{17... | collective-permute-start | bytes 98312 | tf_op jit(solution)/shard_map/ppermute | solution.py:571
  10.2 0.0 copy-done
  10.2 0.1 slice.34
  10.3 0.1 slice.28
  10.4 1.1 %collective-permute-done.above_ref = bf16[2,64,128]{2,1,0:T(8,128)(2,1)S(1)} collective-permute-done((bf16[2,64,128]{2,1,0:T(8,128)(2,1)}, bf16[2,64,128]{2,1,0:T(8,128)(2,1)S(1)}, u32[]{:S(2)}, u32[]{:S(2)}) %collective-permute-start) | collective-permute-done | bytes 32800 | tf_op jit(solution)/shard_map/ppermute | solution.py:571
  11.6 3.0 %collective-permute-done.1.below_ref = bf16[17,64,128]{2,1,0:T(8,128)(2,1)S(1)} collective-permute-done((bf16[17,64,128]{2,1,0:T(8,128)(2,1)}, bf16[17,64,128]{2,1,0:T(8,128)(2,1)S(1)}, u32[]{:S(2)}, u32[]{:S(2)}) %collective-permute-start.1) | collective-permute-done | bytes 278560 | tf_op jit(solution)/shard_map/ppermute | solution.py:570
  14.7 0.0 slice-done
  14.7 0.1 pad_maximum_fusion
  14.8 3.5 %collective-permute-start.3 = (bf16[157,16,128]{2,1,0:T(8,128)(2,1)S(1)}, bf16[157,16,128]{2,1,0:T(8,128)(2,1)S(1)}, u32[]{:S(2)}, u32[]{:S(2)}) collective-permute-start(bf16[157,16,128]{2,1,0:T(8,128)(2,1)S(1)} %pad_maximum_fusion), channel_id=1, source_target_pairs={{1,0},{2,1},{3,2},{4,3},{5,4},{6,5},{7,6},{8,7},{9,8},{10,9},{11,1... | collective-permute-start | bytes 1929224 | tf_op jit(solution)/shard_map/ppermute | solution.py:577
  18.4 0.0 copy-done.10
  18.4 0.1 pad.9.flags_ref
  18.5 3.1 %collective-permute-start.2 = (bf16[2,147,128]{2,1,0:T(8,128)(2,1)S(1)}, bf16[2,147,128]{2,1,0:T(8,128)(2,1)S(1)}, u32[]{:S(2)}, u32[]{:S(2)}) collective-permute-start(bf16[2,147,128]{2,1,0:T(8,128)(2,1)S(1)} %pad_maximum_fusion.1), channel_id=1, source_target_pairs={{0,1},{1,2},{2,3},{3,4},{4,5},{5,6},{6,7},{7,8},{8,9},{9,10},{10,1... | collective-permute-start | bytes 225800 | tf_op jit(solution)/shard_map/ppermute | solution.py:578
  21.6 0.0 copy-done.6
  21.7 0.0 copy-start.4
  21.7 0.0 copy-start.5
  21.7 0.0 copy-start.7
  21.7 0.0 copy-start.8
  21.7 0.0 copy-start.9
  21.7 4.8 %first_layer.1.inner_ref = bf16[152,64,128]{2,1,0:T(8,128)(2,1)S(1)} custom-call(bf16[128,64,128]{2,1,0:T(8,128)(2,1)S(1)} %copy-done, bf16[2,64,128]{2,1,0:T(8,128)(2,1)S(1)} %collective-permute-done.above_ref, bf16[17,64,128]{2,1,0:T(8,128)(2,1)S(1)} %collective-permute-done.1.below_ref, bf16[9,128,128]{2,1,0:T(8,128)(2,1)S(1)} %bitcast.28), custom_call_target="tpu_custom_call" | custom-call | flops 4000000000 | bytes 5000000 | tf_op jit(solution)/shard_map/first_layer/pallas_call | solution.py:455
  26.5 0.0 collective-permute-done.2.left_ref
  26.5 1.2 %collective-permute-done.3.right_ref = bf16[157,16,128]{2,1,0:T(8,128)(2,1)S(1)} collective-permute-done((bf16[157,16,128]{2,1,0:T(8,128)(2,1)S(1)}, bf16[157,16,128]{2,1,0:T(8,128)(2,1)S(1)}, u32[]{:S(2)}, u32[]{:S(2)}) %collective-permute-start.3) | collective-permute-done | bytes 643104 | tf_op jit(solution)/shard_map/ppermute | solution.py:577
  27.7 0.0 copy-done.4
  27.7 0.0 copy-done.5
  27.7 0.0 copy-done.7
  27.7 0.0 copy-done.8
  27.7 0.0 copy-done.9
  27.7 11.2 %scene.1 = (bf16[128,64,128]{2,1,0:T(8,128)(2,1)}, bf16[128,16,128]{2,1,0:T(8,128)(2,1)S(1)}) custom-call(s32[2,32]{1,0:T(2,128)S(1)} %copy-done.9, bf16[128,64,128]{2,1,0:T(8,128)(2,1)S(1)} %copy-done, bf16[2,64,128]{2,1,0:T(8,128)(2,1)S(1)} %collective-permute-done.above_ref, bf16[17,64,128]{2,1,0:T(8,128)(2,1)S(1)} %collective-permute-done.1.below_ref, ...), custom_call_target="tpu_custom_call" | custom-call | flops 10000000000 | bytes 10000000 | tf_op jit(solution)/shard_map/scene/pallas_call | solution.py:475
  38.9 25.1 %all_to_all.10.received_ref = bf16[128,16,128]{2,1,0:T(8,128)(2,1)S(1)} all-to-all(bf16[128,16,128]{2,1,0:T(8,128)(2,1)S(1)} %get-tuple-element.9), channel_id=1, replica_groups=mesh['row'=8,'col'=16] {'row','col'}, dimensions={0} | all-to-all | bytes 1048576 | tf_op jit(solution)/shard_map/all_to_all | solution.py:597
  64.1 0.0 copy-start.1
  64.1 0.0 copy-start.2
  64.1 0.0 copy-start.3
  64.1 2.4 %attend.1 = bf16[128,8,128]{2,1,0:T(8,128)(2,1)} custom-call(bf16[128,16,128]{2,1,0:T(8,128)(2,1)S(1)} %all_to_all.10.received_ref), custom_call_target="tpu_custom_call" | custom-call | flops 10000000000 | bytes 1000000 | tf_op jit(solution)/shard_map/attend/pallas_call | solution.py:520
  66.5 4.5 %all-to-all-start.1 = ((bf16[128,8,128]{2,1,0:T(8,128)(2,1)}), bf16[128,8,128]{2,1,0:T(8,128)(2,1)S(1)}, u32[]{:S(2)}, u32[]{:S(2)}) async-start(bf16[128,8,128]{2,1,0:T(8,128)(2,1)} %attend.1), calls=%async_computation.1 | async-start | bytes 524288 | tf_op jit(solution)/shard_map/all_to_all | solution.py:598
  71.0 0.1 copy.22.live_ref
  71.1 11.0 %all-to-all-done.1.returned_ref = bf16[128,8,128]{2,1,0:T(8,128)(2,1)S(1)} async-done(((bf16[128,8,128]{2,1,0:T(8,128)(2,1)}), bf16[128,8,128]{2,1,0:T(8,128)(2,1)S(1)}, u32[]{:S(2)}, u32[]{:S(2)}) %all-to-all-start.1) | async-done | bytes 262176 | tf_op jit(solution)/shard_map/all_to_all | solution.py:598
  82.1 0.0 copy-done.1
  82.1 0.0 copy-done.2
  82.1 0.0 copy-done.3
  82.1 3.3 %agents.1 = bf16[32,512]{1,0:T(8,128)(2,1)} custom-call(bf16[128,8,128]{2,1,0:T(8,128)(2,1)S(1)} %all-to-all-done.1.returned_ref, f32[32,1]{1,0:T(8,128)S(1)} %copy.22.live_ref, f32[1,512]{1,0:T(1,128)S(1)} %bitcast.27, bf16[512,512]{1,0:T(8,128)(2,1)S(1)} %copy-done.2, bf16[512,2048]{1,0:T(8,128)(2,1)S(1)} %copy-done.1, bf16[2048,512]{1,0:T(8,128)(2,1)} %w_down_hbm.1), custom_call_target="tpu_custom_call" | custom-call | tf_op jit(solution)/shard_map/agents/pallas_call | solution.py:535
  (15 shorter events, 0.1 us)
Async XLA Ops:
  0.6 9.6 %copy-start = (bf16[128,64,128]{2,1,0:T(8,128)(2,1)S(1)}, bf16[128,64,128]{2,1,0:T(8,128)(2,1)}, u32[]{:S(2)}) copy-start(bf16[128,64,128]{2,1,0:T(8,128)(2,1)} %raster_ref.3) | copy-start | bytes 6291460
  0.6 14.0 %slice-start = ((bf16[128,64,128]{2,1,0:T(8,128)(2,1)}), bf16[128,16,128]{2,1,0:T(8,128)(2,1)S(1)}, s32[]{:S(2)}) async-start(bf16[128,64,128]{2,1,0:T(8,128)(2,1)} %raster_ref.3), calls=%async_computation.2 | async-start | bytes 1048576 | tf_op jit(solution)/shard_map/slice | solution.py:576
  0.6 17.7 %copy-start.10 = (s32[32]{0:T(128)S(1)}, s32[32]{0:T(128)}, u32[]{:S(2)}) copy-start(s32[32]{0:T(128)} %param.16) | copy-start | bytes 388
  2.5 19.1 %copy-start.6 = (bf16[3,3,128,128]{3,2,1,0:T(8,128)(2,1)S(1)}, bf16[3,3,128,128]{3,2,1,0:T(8,128)(2,1)}, u32[]{:S(2)}) copy-start(bf16[3,3,128,128]{3,2,1,0:T(8,128)(2,1)} %param.13) | copy-start | bytes 884740
  2.5 12.1 %collective-permute-start.1 = (bf16[17,64,128]{2,1,0:T(8,128)(2,1)}, bf16[17,64,128]{2,1,0:T(8,128)(2,1)S(1)}, u32[]{:S(2)}, u32[]{:S(2)}) collective-permute-start(bf16[17,64,128]{2,1,0:T(8,128)(2,1)} %get-tuple-element.7), channel_id=1, source_target_pairs={{16,0},{32,16},{48,32},{64,48},{80,64},{96,80},{112,96},{17,1},{33... | collective-permute-start | bytes 835592 | tf_op jit(solution)/shard_map/ppermute | solution.py:570
  3.9 7.6 %collective-permute-start = (bf16[2,64,128]{2,1,0:T(8,128)(2,1)}, bf16[2,64,128]{2,1,0:T(8,128)(2,1)S(1)}, u32[]{:S(2)}, u32[]{:S(2)}) collective-permute-start(bf16[2,64,128]{2,1,0:T(8,128)(2,1)} %get-tuple-element.6), channel_id=1, source_target_pairs={{0,16},{16,32},{32,48},{48,64},{64,80},{80,96},{96,112},{1,17},{17... | collective-permute-start | bytes 98312 | tf_op jit(solution)/shard_map/ppermute | solution.py:571
  14.8 12.9 %collective-permute-start.3 = (bf16[157,16,128]{2,1,0:T(8,128)(2,1)S(1)}, bf16[157,16,128]{2,1,0:T(8,128)(2,1)S(1)}, u32[]{:S(2)}, u32[]{:S(2)}) collective-permute-start(bf16[157,16,128]{2,1,0:T(8,128)(2,1)S(1)} %pad_maximum_fusion), channel_id=1, source_target_pairs={{1,0},{2,1},{3,2},{4,3},{5,4},{6,5},{7,6},{8,7},{9,8},{10,9},{11,1... | collective-permute-start | bytes 1929224 | tf_op jit(solution)/shard_map/ppermute | solution.py:577
  18.5 8.0 %collective-permute-start.2 = (bf16[2,147,128]{2,1,0:T(8,128)(2,1)S(1)}, bf16[2,147,128]{2,1,0:T(8,128)(2,1)S(1)}, u32[]{:S(2)}, u32[]{:S(2)}) collective-permute-start(bf16[2,147,128]{2,1,0:T(8,128)(2,1)S(1)} %pad_maximum_fusion.1), channel_id=1, source_target_pairs={{0,1},{1,2},{2,3},{3,4},{4,5},{5,6},{6,7},{7,8},{8,9},{9,10},{10,1... | collective-permute-start | bytes 225800 | tf_op jit(solution)/shard_map/ppermute | solution.py:578
  21.7 6.0 %copy-start.4 = (bf16[2048,512]{1,0:T(8,128)(2,1)S(1)}, bf16[2048,512]{1,0:T(8,128)(2,1)}, u32[]{:S(2)}) copy-start(bf16[2048,512]{1,0:T(8,128)(2,1)} %w_embed.1) | copy-start | bytes 6291460
  21.7 6.0 %copy-start.5 = (bf16[512,1536]{1,0:T(8,128)(2,1)S(1)}, bf16[512,1536]{1,0:T(8,128)(2,1)}, u32[]{:S(2)}) copy-start(bf16[512,1536]{1,0:T(8,128)(2,1)} %w_qkv.1) | copy-start | bytes 4718596
  21.7 6.0 %copy-start.7 = (bf16[3,3,128,128]{3,2,1,0:T(8,128)(2,1)S(1)}, bf16[3,3,128,128]{3,2,1,0:T(8,128)(2,1)}, u32[]{:S(2)}) copy-start(bf16[3,3,128,128]{3,2,1,0:T(8,128)(2,1)} %param.14) | copy-start | bytes 884740
  21.7 6.0 %copy-start.8 = (f32[512]{0:T(512)S(1)}, f32[512]{0:T(512)}, u32[]{:S(2)}) copy-start(f32[512]{0:T(512)} %param.18) | copy-start | bytes 6148
  21.7 6.0 %copy-start.9 = (s32[2,32]{1,0:T(2,128)S(1)}, s32[2,32]{1,0:T(2,128)}, u32[]{:S(2)}) copy-start(s32[2,32]{1,0:T(2,128)} %anchor_ref.1) | copy-start | bytes 772
  64.1 18.1 %copy-start.1 = (bf16[512,2048]{1,0:T(8,128)(2,1)S(1)}, bf16[512,2048]{1,0:T(8,128)(2,1)}, u32[]{:S(2)}) copy-start(bf16[512,2048]{1,0:T(8,128)(2,1)} %w_up.1) | copy-start | bytes 6291460
  64.1 18.1 %copy-start.2 = (bf16[512,512]{1,0:T(8,128)(2,1)S(1)}, bf16[512,512]{1,0:T(8,128)(2,1)}, u32[]{:S(2)}) copy-start(bf16[512,512]{1,0:T(8,128)(2,1)} %w_out.1) | copy-start | bytes 1572868
  64.1 18.1 %copy-start.3 = (f32[512]{0:T(512)S(1)}, f32[512]{0:T(512)}, u32[]{:S(2)}) copy-start(f32[512]{0:T(512)} %param.21) | copy-start | bytes 6148
  66.5 15.6 %all-to-all-start.1 = ((bf16[128,8,128]{2,1,0:T(8,128)(2,1)}), bf16[128,8,128]{2,1,0:T(8,128)(2,1)S(1)}, u32[]{:S(2)}, u32[]{:S(2)}) async-start(bf16[128,8,128]{2,1,0:T(8,128)(2,1)} %attend.1), calls=%async_computation.1 | async-start | bytes 524288 | tf_op jit(solution)/shard_map/all_to_all | solution.py:598
